TPU v7x, 128 devices: a whole 4x4x4 slice. The times are simulated.
128 devices in a mesh: wide: 32 (over x, y_hi, z), narrow: 4 (over y_lo, core).
Axes of the slice: x: 4, y: 4 (y_hi: 2, y_lo: 2; y = y_hi * 2 + y_lo), z: 4, core: 2. Of those that a mesh axis runs over, the one named last changes fastest.
Arguments:
- target_ids: int32 [128, 256], P(('wide', 'narrow')), may hold values from 0 to 250111, as said below
- tgt_len: int32 [128], P(('wide', 'narrow')), may hold values from 64 to 256
- mem_len: int32 [128], P(('wide', 'narrow')), may hold values from 264 to 1056
- embed_table: bfloat16 [250112, 768], P(('wide', 'narrow')), may hold values from -6 to 6
- memory: bfloat16 [128, 1056, 768], P(('wide', 'narrow')), may hold values from -6 to 6
- self_qkv: bfloat16 [3, 768, 768], P(None, ('wide', 'narrow')), may hold values from -0.21875 to 0.21875
- self_out: bfloat16 [768, 768], P(('wide', 'narrow')), may hold values from -0.875 to 0.875
- gain_self: bfloat16 [768], P(('wide', 'narrow')), may hold values from 0.5 to 1.5
- cross_qkv: bfloat16 [3, 768, 768], P(None, ('wide', 'narrow')), may hold values from -0.21875 to 0.21875
- cross_out: bfloat16 [768, 768], P(('wide', 'narrow')), may hold values from -1.25 to 1.25
- gain_cross: bfloat16 [768], P(('wide', 'narrow')), may hold values from 0.5 to 1.5
- ffn_in: bfloat16 [2, 768, 2048], P(None, ('wide', 'narrow')), may hold values from -0.21875 to 0.21875
- ffn_out: bfloat16 [2048, 768], P(('wide', 'narrow')), may hold values from -0.125 to 0.125
- gain_ffn: bfloat16 [768], P(('wide', 'narrow')), may hold values from 0.5 to 1.5
- out_grad: bfloat16 [128, 256, 768], P(('wide', 'narrow')), may hold values from -6 to 6
Outputs:
- out: float32 [128, 256, 768], P(('wide', 'narrow'))
- memory_grad: float32 [128, 1056, 768], P(('wide', 'narrow'))
- embed_table_grad: float32 [250112, 768], P(('wide', 'narrow'))
- self_qkv_grad: float32 [3, 768, 768], P(None, ('wide', 'narrow'))
- self_out_grad: float32 [768, 768], P(('wide', 'narrow'))
- gain_self_grad: float32 [768], P(('wide', 'narrow'))
- cross_qkv_grad: float32 [3, 768, 768], P(None, ('wide', 'narrow'))
- cross_out_grad: float32 [768, 768], P(('wide', 'narrow'))
- gain_cross_grad: float32 [768], P(('wide', 'narrow'))
- ffn_in_grad: float32 [2, 768, 2048], P(None, ('wide', 'narrow'))
- ffn_out_grad: float32 [2048, 768], P(('wide', 'narrow'))
- gain_ffn_grad: float32 [768], P(('wide', 'narrow'))
Inputs may be any that keep to these rules, and one draw needn't show every extreme that they name: `target_ids`: the table rows held by one device are 1954 consecutive rows. Among the ids of one device's 1 sequence, at most 4 fall within the rows of any one device; in every draw each device's ids reach 4 for some device's rows, and one device's rows receive exactly 4 from every device's sequences.
All inputs are finite; a program needn't handle non-finite values.
Results may differ from a plain program's by a relative error of at most 0.034.
Values may be sent and summed in bfloat16 or wider, within the bound.
No kernel may reach another device: no remote copies, remote signals or barrier semaphores. Data moves between devices by JAX's collectives and lax.ppermute only.
A program may use at most 256 MiB of HBM per device.

v0:
```python
import functools

import jax
import jax.numpy as jnp
from jax import lax
from jax.experimental import pallas as pl
from jax.experimental.pallas import tpu as pltpu
from jax.sharding import Mesh, PartitionSpec as P

HEAD_SIZE = 64
D = 768
FF = 2048
TGT = 256
MEM = 1056
KEYS = 1152
PAIRS = 6
SELF_FORWARD, CROSS_FORWARD, CROSS_BACKWARD, SELF_BACKWARD = 6, 6, 2, 3


eps = 1e-06
masked_score = -1e30

AXES = ("x", "yh", "zh", "zl", "yl", "c")
SIZES = (4, 2, 2, 2, 2, 2)
RING_X, RING_Y, RING_Z = ("x",), ("yh", "yl"), ("zh", "zl")
RINGS = {"x": RING_X, "y": RING_Y, "z": RING_Z}
TORUS = RING_X + RING_Y + RING_Z + ("c",)
CHIPS = ("x", "yh", "zh", "zl", "yl")
EIGHT = ("zl", "yl", "c")
BLOCK = 48
SLOTS = 4
GAINS = 18

HBM = pl.BlockSpec(memory_space=pl.ANY)
SCALARS = pl.BlockSpec(memory_space=pltpu.SMEM)


def ring_pair(v, ring, first):
    perm = []
    for i in range(4):
        for c in range(2):
            perm.append((2 * i + c, 2 * (i ^ (1 if (c == 0) == first else 3)) + c))
    return lax.ppermute(v, ring + ("c",), perm)


def swap_cores(v):
    return lax.ppermute(v, "c", [(0, 1), (1, 0)])


def then(v, *tokens):
    return lax.optimization_barrier((v, *tokens))[0]


def add_low(*terms):
    return sum(t.astype(jnp.float32) for t in terms).astype(jnp.bfloat16)


def halve(low, high, ring):
    got = ring_pair(high, ring, False)
    back = ring_pair(add_low(low[1], got[1]), ring, True)
    return low[0], got[0], back


def ring_sum(mine, other, rings):
    got = swap_cores(other)
    low, high = add_low(mine[:2], got[:2]), add_low(mine[2:], got[2:])
    for ring in rings[:-1]:
        terms = halve(low, high, RINGS[ring])
        low, high = (add_low(*(t[at] for t in terms)) for at in (slice(0, 2), slice(2, 4)))
    return sum(t.astype(jnp.float32) for t in halve(low, high, RINGS[rings[-1]]))


def mm(a, b):
    return jnp.dot(a, b, preferred_element_type=jnp.float32)


def mm_nt(a, b):
    return lax.dot_general(a, b, (((1,), (1,)), ((), ())), preferred_element_type=jnp.float32)


def mm_tn(a, b):
    return lax.dot_general(a, b, (((0,), (0,)), ((), ())), preferred_element_type=jnp.float32)


def turned(v):
    return v.astype(jnp.float32).T.astype(v.dtype)


def first_half(shape):
    return lax.broadcasted_iota(jnp.int32, shape, 1) < HEAD_SIZE


def stacked_heads(pair):
    low = first_half(pair.shape)
    zero = jnp.zeros_like(pair)
    return jnp.concatenate([jnp.where(low, pair, zero), jnp.where(low, zero, pair)], axis=0)


def joined_heads(both):
    half = both.shape[0] // 2
    return jnp.where(first_half((half, both.shape[1])), both[:half], both[half:])


def rms_scale(hidden):
    return lax.rsqrt(jnp.mean(hidden * hidden, axis=-1, keepdims=True) + eps)


def rms_back(hidden, gain, grad):
    scale = rms_scale(hidden)
    u = grad * gain
    inner = jnp.mean(u * hidden, axis=-1, keepdims=True)
    grad_hidden = scale * u - hidden * (scale * scale * scale * inner)
    return grad_hidden, jnp.sum(grad * hidden * scale, axis=0, keepdims=True)


def my_place(pos_ref):
    return {"x": pos_ref[0], "y": pos_ref[1], "z": pos_ref[2]}


def group_member(at, core):
    group = at["x"] * 4 + (at["y"] >> 1) * 2 + (at["z"] >> 1)
    return group, (at["z"] & 1) * 4 + (at["y"] & 1) * 2 + core


def partners(core):
    return (0, 1 + 2 * core, 3 - 2 * core, 2)


def square_parts(width, group, member):
    row = pl.multiple_of(group * BLOCK, 16)
    column = pl.multiple_of(member * width, 128)
    return [((slice(None), slice(None)), 0, (pl.ds(row, BLOCK), pl.ds(column, width)))]


def torus():
    return [(x, y, z, c) for x in range(4) for y in range(4) for z in range(4) for c in range(2)]


def block_place(x, y, z, c):
    return x * 4 + (y // 2) * 2 + z // 2, (z % 2) * 4 + (y % 2) * 2 + c


def start_place(blocks, first, out, sem):
    for at in torus():
        group, member = block_place(*at)
        pltpu.make_async_copy(
            blocks.at[at + (slice(None), pl.ds(first, 384))],
            out.at[pl.ds(BLOCK * group, BLOCK), pl.ds(384 * member, 384)],
            sem,
        ).start()


def ffn_copies(j, whole_in, whole_out, block_of):
    found = []
    for at in torus():
        group, member = block_place(*at)
        block = block_of(at)
        if member % 4 == j:
            rows, columns = pl.ds(BLOCK * group, BLOCK), pl.ds(512 * member, 512)
            found.append((whole_in.at[rows, columns], block.at[:, pl.ds(768, 512)]))
        if at[0] == j:
            rows = pl.ds(16 * (8 * group + member), 16)
            for s in range(3):
                part = block.at[pl.ds(16 * s, 16), pl.ds(1280, 256)]
                found.append((whole_out.at[rows, pl.ds(256 * s, 256)], part))
    return found


def start_split(pos_ref, rings, parts, wholes, outs, sem):
    me = my_place(pos_ref)
    at = {}
    for source in range(2):
        core = pos_ref[3] ^ source
        flips = partners(core)
        for k3 in range(4):
            at[rings[0]] = me[rings[0]] ^ flips[k3]
            for k2 in range(4):
                at[rings[1]] = me[rings[1]] ^ flips[k2]
                for k1 in range(4):
                    at[rings[2]] = me[rings[2]] ^ flips[k1]
                    for dst, whole, src in parts(*group_member(at, core)):
                        pltpu.make_async_copy(
                            wholes[whole].at[src], outs[source].at[(k3, k2, k1) + dst], sem
                        ).start()


def start_split_whole(pos_ref, whole, outs, sem):
    for source in range(2):
        core = pos_ref[3] ^ source
        for group in range(16):
            for q in range(4):
                for dst, _, src in square_parts(384, group, 2 * q + core):
                    pltpu.make_async_copy(
                        whole.at[src], outs[source].at[(4 * group + q,) + dst], sem
                    ).start()


def wait_whole(refs, sem):
    for ref in refs:
        pltpu.make_async_copy(ref, ref, sem).wait()


def start_split(pos_ref, rings, parts, wholes, outs, sem):
    me = my_place(pos_ref)
    at = {}
    for source in range(2):
        core = pos_ref[3] ^ source
        flips = partners(core)
        for k3 in range(4):
            at[rings[0]] = me[rings[0]] ^ flips[k3]
            for k2 in range(4):
                at[rings[1]] = me[rings[1]] ^ flips[k2]
                for k1 in range(4):
                    at[rings[2]] = me[rings[2]] ^ flips[k1]
                    for dst, whole, src in parts(*group_member(at, core)):
                        pltpu.make_async_copy(
                            wholes[whole].at[src], outs[source].at[(k3, k2, k1) + dst], sem
                        ).start()


def start_split_whole(pos_ref, whole, outs, sem):
    for source in range(2):
        core = pos_ref[3] ^ source
        for group in range(16):
            for q in range(4):
                for dst, _, src in square_parts(384, group, 2 * q + core):
                    pltpu.make_async_copy(
                        whole.at[src], outs[source].at[(4 * group + q,) + dst], sem
                    ).start()


def softmax_low(scores, valid):
    scores = jnp.where(valid, scores, masked_score)
    expanded = jnp.exp(scores - jnp.max(scores, axis=-1, keepdims=True))
    total = jnp.sum(expanded, axis=-1, keepdims=True)
    return (expanded * (1.0 / total)).astype(jnp.bfloat16)


def softmax_back(weights, grads):
    weights = weights.astype(jnp.float32)
    inner = jnp.sum(weights * grads, axis=-1, keepdims=True)
    return (weights * (grads - inner)).astype(jnp.bfloat16)


def pair_columns(j, offset=0):
    return pl.ds(pl.multiple_of(offset + j * 128, 128), 128)


def pairs_here(together):
    j = pl.program_id(0)
    return [(s, j * together + s) for s in range(together)]


def self_forward_kernel(rows_ref, slot_ref, gain_ref, early_ref, blocks, *refs):
    emb_ref, qkv_ref, p_ref, mixed_ref, h1_ref, w_ref, sem = refs
    j = pl.program_id(0)

    @pl.when(j == 0)
    def _():
        start_place(blocks, 0, w_ref, sem)
        slots = rows_ref.shape[0]
        hits = slot_ref[...] == lax.broadcasted_iota(jnp.int32, (TGT, slots), 1)
        hidden = mm(hits.astype(jnp.bfloat16), rows_ref[...])
        emb_ref[...] = hidden.astype(jnp.bfloat16)
        normed = (hidden * rms_scale(hidden) * gain_ref[...]).astype(jnp.bfloat16)
        wait_whole([w_ref], sem)
        for k in range(3):
            at = pl.ds(768 * k, 768)
            qkv_ref[:, at] = mm(normed, w_ref[:, at]).astype(jnp.bfloat16)

    row = lax.broadcasted_iota(jnp.int32, (2 * TGT, TGT), 0) & (TGT - 1)
    causal = lax.broadcasted_iota(jnp.int32, (2 * TGT, TGT), 1) <= row
    for s, pair in pairs_here(SELF_FORWARD):
        queries = stacked_heads(qkv_ref[:, pair_columns(pair)]) * jnp.bfloat16(0.125)
        weights = softmax_low(mm_nt(queries, qkv_ref[:, pair_columns(pair, 768)]), causal)
        p_ref[s] = weights
        mixed = mm(weights, qkv_ref[:, pair_columns(pair, 1536)])
        mixed_ref[:, pair_columns(pair)] = joined_heads(mixed).astype(jnp.bfloat16)

    @pl.when(j == PAIRS // SELF_FORWARD - 1)
    def _():
        h1_ref[...] = emb_ref[...].astype(jnp.float32) + mm(mixed_ref[...], w_ref[:, 2304:])


def full(*shape):
    return pl.BlockSpec(shape, lambda j: (0,) * len(shape))


def shaped(dtype, *shape):
    return jax.ShapeDtypeStruct(shape, dtype)


def params(mib=56):
    return pltpu.CompilerParams(vmem_limit_bytes=mib * 2**20)


def cost(gflop, mbytes):
    return pl.CostEstimate(
        flops=int(gflop * 1e9), bytes_accessed=int(mbytes * 1e6), transcendentals=0
    )


def self_forward(rows, slot, gain, early, blocks):
    bf, f32 = jnp.bfloat16, jnp.float32
    return pl.pallas_call(
        self_forward_kernel,
        grid=(PAIRS // SELF_FORWARD,),
        in_specs=[full(512, D), full(TGT, 1), full(1, D), HBM, HBM],
        out_specs=[
            full(TGT, D),
            full(TGT, 3 * D),
            pl.BlockSpec((SELF_FORWARD, 512, TGT), lambda j: (j, 0, 0)),
            full(TGT, D),
            full(TGT, D),
            full(D, 4 * D),
        ],
        out_shape=[
            shaped(bf, TGT, D),
            shaped(bf, TGT, 3 * D),
            shaped(bf, PAIRS, 512, TGT),
            shaped(bf, TGT, D),
            shaped(f32, TGT, D),
            shaped(bf, D, 4 * D),
        ],
        scratch_shapes=[pltpu.SemaphoreType.DMA],
        compiler_params=params(),
        cost_estimate=cost(8, 12),
        name="self_forward",
    )(rows, slot, gain, early, blocks)


def cross_forward_kernel(len_ref, h1_ref, gain_ref, mem_ref, blocks, *refs):
    q_ref, k_ref, v_ref, p_ref, mixed_ref, h2_ref, w_ref, sem = refs
    j = pl.program_id(0)

    @pl.when(j == 0)
    def _():
        start_place(blocks, 384, w_ref, sem)
        hidden = h1_ref[...]
        normed = (hidden * rms_scale(hidden) * gain_ref[...]).astype(jnp.bfloat16)
        wait_whole([w_ref], sem)
        q_ref[...] = mm(normed, w_ref[:, :768]).astype(jnp.bfloat16)
        for out, offset in ((k_ref, 768), (v_ref, 1536)):
            for half in range(2):
                at = pl.ds(384 * half, 384)
                out[:MEM, at] = mm(mem_ref[...], w_ref[:, pl.ds(offset + 384 * half, 384)]).astype(
                    jnp.bfloat16
                )
            out[MEM:, :] = jnp.zeros((KEYS - MEM, D), jnp.bfloat16)

    reach = lax.broadcasted_iota(jnp.int32, (2 * TGT, KEYS), 1) < len_ref[0]
    for s, pair in pairs_here(CROSS_FORWARD):
        queries = stacked_heads(q_ref[:, pair_columns(pair)]) * jnp.bfloat16(0.125)
        weights = softmax_low(mm_nt(queries, k_ref[:, pair_columns(pair)]), reach)
        p_ref[s] = weights
        mixed = mm(weights, v_ref[:, pair_columns(pair)])
        mixed_ref[:, pair_columns(pair)] = joined_heads(mixed).astype(jnp.bfloat16)

    @pl.when(j == PAIRS // CROSS_FORWARD - 1)
    def _():
        h2_ref[...] = h1_ref[...] + mm(mixed_ref[...], w_ref[:, 2304:])


def cross_forward(mem_len, h1, gain, memory, blocks):
    bf, f32 = jnp.bfloat16, jnp.float32
    return pl.pallas_call(
        cross_forward_kernel,
        grid=(PAIRS // CROSS_FORWARD,),
        in_specs=[SCALARS, full(TGT, D), full(1, D), full(MEM, D), HBM],
        out_specs=[
            full(TGT, D),
            full(KEYS, D),
            full(KEYS, D),
            pl.BlockSpec((CROSS_FORWARD, 512, KEYS), lambda j: (j, 0, 0)),
            full(TGT, D),
            full(TGT, D),
            full(D, 4 * D),
        ],
        out_shape=[
            shaped(bf, TGT, D),
            shaped(bf, KEYS, D),
            shaped(bf, KEYS, D),
            shaped(bf, PAIRS, 512, KEYS),
            shaped(bf, TGT, D),
            shaped(f32, TGT, D),
            shaped(bf, D, 4 * D),
        ],
        scratch_shapes=[pltpu.SemaphoreType.DMA],
        compiler_params=params(),
        cost_estimate=cost(20, 20),
        name="cross_forward",
    )(mem_len, h1, gain, memory, blocks)


class piece_of:
    def __init__(self, ref):
        self.ref = ref

    @property
    def at(self):
        return self

    def __getitem__(self, place):
        rows, columns = place
        return self.ref.at[rows, pl.ds(columns.start - 768, columns.size)]


def ffn_kernel(len_ref, h2_ref, gain_ref, og_ref, blocks, *refs):
    out_ref, g2_ref, dgain_ref, pieces = refs[:4]
    w_in, w_out, g_in, g_out, normed, normed_t, low, gate, up, grad, inner, da, sems, sem = refs[4:]
    j = pl.program_id(0)
    bf, f32 = jnp.bfloat16, jnp.float32

    def kept():
        row = lax.broadcasted_iota(jnp.int32, (TGT, 1), 0)
        return row < len_ref[0]

    @pl.when(j == 0)
    def _():
        for quarter in range(FF // 512):
            for whole, block in ffn_copies(quarter, w_in, w_out, lambda at: blocks.at[at]):
                pltpu.make_async_copy(block, whole, sems.at[quarter]).start()
        hidden = h2_ref[...]
        a3 = (hidden * rms_scale(hidden) * gain_ref[...]).astype(bf)
        normed[...] = a3
        normed_t[...] = a3.astype(f32).T.astype(bf)
        low[...] = jnp.where(kept(), og_ref[...], jnp.zeros((), bf))

    width = 512
    gate_at = pl.ds(pl.multiple_of(j * width, width), width)
    up_at = pl.ds(pl.multiple_of(FF + j * width, width), width)
    wait_whole([w_in.at[:, gate_at], w_in.at[:, up_at], w_out.at[gate_at, :]], sems.at[j])
    gate[...] = mm(normed[...], w_in[:, gate_at])
    up[...] = mm(normed[...], w_in[:, up_at])
    grad[...] = mm_nt(low[...], w_out[gate_at, :])

    def unit(i, carry):
        at = pl.ds(pl.multiple_of(i * 32, 32), 32)
        g, u, d = gate[at, :], up[at, :], grad[at, :]
        square = g * g
        t = jnp.tanh(0.7978845608 * (g + 0.044715 * (g * square)))
        half = 0.5 * (1.0 + t)
        gelu = g * half
        slope = half + 0.5 * g * (1.0 - t * t) * (0.7978845608 * (1.0 + 3.0 * 0.044715 * square))
        inner[at, :] = (gelu * u).astype(bf)
        gate[at, :] = d * u * slope
        up[at, :] = d * gelu
        return carry

    lax.fori_loop(0, TGT // 32, unit, 0, unroll=True)
    c_gate, c_up = gate[...].astype(bf), up[...].astype(bf)
    part = mm(inner[...], w_out[gate_at, :])
    da_part = mm_nt(c_gate, w_in[:, gate_at]) + mm_nt(c_up, w_in[:, up_at])

    @pl.when(j == 0)
    def _():
        out_ref[...] = part
        da[...] = da_part

    @pl.when(j > 0)
    def _():
        out_ref[...] += part
        da[...] += da_part

    g_out[gate_at, :] = mm_tn(inner[...], low[...]).astype(bf)
    g_in[:, gate_at] = mm(normed_t[...], c_gate).astype(bf)
    g_in[:, up_at] = mm(normed_t[...], c_up).astype(bf)

    for quarter in range(FF // width):

        @pl.when(j == quarter)
        def _():
            for whole, block in ffn_copies(
                quarter, g_in, g_out, lambda at: piece_of(pieces.at[at[0], at[3], at[1], at[2]])
            ):
                pltpu.make_async_copy(whole, block, sem).start()

    @pl.when(j == FF // width - 1)
    def _():
        hidden = h2_ref[...]
        out_ref[...] = jnp.where(kept(), hidden + out_ref[...], 0.0)
        back, dgain = rms_back(hidden, gain_ref[...], da[...])
        g2_ref[...] = jnp.where(kept(), og_ref[...].astype(f32), 0.0) + back
        dgain_ref[...] = dgain
        wait_whole([g_in, g_out], sem)


def ffn_both(tgt_len, h2, gain, out_grad, blocks):
    bf, f32 = jnp.bfloat16, jnp.float32
    pieces = shaped(bf, 4, 2, 4, 4, BLOCK, 768)
    return pl.pallas_call(
        ffn_kernel,
        grid=(FF // 512,),
        in_specs=[SCALARS, full(TGT, D), full(1, D), full(TGT, D), HBM],
        out_specs=[full(TGT, D), full(TGT, D), full(1, D), HBM],
        out_shape=[shaped(f32, TGT, D), shaped(f32, TGT, D), shaped(f32, 1, D), pieces],
        scratch_shapes=[
            pltpu.VMEM((D, 2 * FF), bf),
            pltpu.VMEM((FF, D), bf),
            pltpu.VMEM((D, 2 * FF), bf),
            pltpu.VMEM((FF, D), bf),
            pltpu.VMEM((TGT, D), bf),
            pltpu.VMEM((D, TGT), bf),
            pltpu.VMEM((TGT, D), bf),
            pltpu.VMEM((TGT, 512), f32),
            pltpu.VMEM((TGT, 512), f32),
            pltpu.VMEM((TGT, 512), f32),
            pltpu.VMEM((TGT, 512), bf),
            pltpu.VMEM((TGT, D), f32),
            pltpu.SemaphoreType.DMA((FF // 512,)),
            pltpu.SemaphoreType.DMA,
        ],
        compiler_params=params(),
        cost_estimate=cost(15, 25),
        name="ffn_both",
    )(tgt_len, h2, gain, out_grad, blocks)


def cross_backward_kernel(h1_ref, gain_ref, g2_ref, w_ref, q_ref, k_ref, v_ref, p_ref, *refs):
    dq, dkv_ref, g1_ref, dgain_ref, grad_mixed = refs
    j = pl.program_id(0)
    bf = jnp.bfloat16

    @pl.when(j == 0)
    def _():
        grad_mixed[...] = mm_nt(g2_ref[...].astype(bf), w_ref[:, 2304:]).astype(bf)

    for s, pair in pairs_here(CROSS_BACKWARD):
        at = pair_columns(pair)
        d_pair = stacked_heads(grad_mixed[:, at])
        queries = stacked_heads(q_ref[:, at])
        weights = p_ref[s]
        grads = softmax_back(weights, mm_nt(d_pair, v_ref[:, at]))
        dq[:, at] = (joined_heads(mm(grads, k_ref[:, at])) * 0.125).astype(bf)
        dkv_ref[:, at] = (mm(turned(queries), grads) * 0.125).T.astype(bf)
        dkv_ref[:, pair_columns(pair, 768)] = mm(turned(d_pair), weights).T.astype(bf)

    @pl.when(j == PAIRS // CROSS_BACKWARD - 1)
    def _():
        back, dgain = rms_back(h1_ref[...], gain_ref[...], mm_nt(dq[...], w_ref[:, :768]))
        g1_ref[...] = g2_ref[...] + back
        dgain_ref[...] = dgain


def cross_backward(h1, gain, g2, w, q, k, v, p):
    bf, f32 = jnp.bfloat16, jnp.float32
    return pl.pallas_call(
        cross_backward_kernel,
        grid=(PAIRS // CROSS_BACKWARD,),
        in_specs=[
            full(TGT, D),
            full(1, D),
            full(TGT, D),
            full(D, 4 * D),
            full(TGT, D),
            full(KEYS, D),
            full(KEYS, D),
            pl.BlockSpec((CROSS_BACKWARD, 512, KEYS), lambda j: (j, 0, 0)),
        ],
        out_specs=[full(TGT, D), full(KEYS, 2 * D), full(TGT, D), full(1, D)],
        out_shape=[
            shaped(bf, TGT, D),
            shaped(bf, KEYS, 2 * D),
            shaped(f32, TGT, D),
            shaped(f32, 1, D),
        ],
        scratch_shapes=[pltpu.VMEM((TGT, D), bf)],
        compiler_params=params(),
        cost_estimate=cost(16, 20),
        name="cross_backward",
    )(h1, gain, g2, w, q, k, v, p)


def cross_grads_kernel(
    rings, pos_ref, h1_ref, gain_ref, g2_ref, mem_t_ref, mixed_ref, dq_ref, dkv_ref, *refs
):
    mine_ref, other_ref, whole, sem = refs
    bf = jnp.bfloat16
    hidden = h1_ref[...]
    normed = (hidden * rms_scale(hidden) * gain_ref[...]).astype(bf)
    whole[:, :768] = mm_tn(normed, dq_ref[...]).astype(bf)
    whole[:, 2304:] = mm_tn(mixed_ref[...], g2_ref[...].astype(bf)).astype(bf)
    for k in range(4):
        at = pl.ds(768 + 384 * k, 384)
        whole[:, at] = mm(mem_t_ref[...], dkv_ref[:, pl.ds(384 * k, 384)]).astype(bf)
    parts = functools.partial(square_parts, 384)
    start_split(pos_ref, rings, parts, [whole], [mine_ref, other_ref], sem)
    wait_whole([whole], sem)


def cross_grads(rings, pos, h1, gain, g2, mem_t, mixed, dq, dkv):
    bf = jnp.bfloat16
    pieces = shaped(bf, 4, 4, 4, BLOCK, 384)
    return pl.pallas_call(
        functools.partial(cross_grads_kernel, rings),
        in_specs=[SCALARS] + [pl.BlockSpec(memory_space=pltpu.VMEM)] * 7,
        out_specs=[HBM, HBM],
        out_shape=[pieces, pieces],
        scratch_shapes=[pltpu.VMEM((D, 4 * D), bf), pltpu.SemaphoreType.DMA],
        compiler_params=params(),
        cost_estimate=cost(6, 12),
        name="cross_grads",
    )(pos, h1, gain, g2, mem_t, mixed, dq, dkv)


def self_backward_kernel(slot_ref, emb_ref, gain_ref, g1_ref, w_ref, qkv_ref, p_ref, *refs):
    dg2_ref, dg3_ref, dqkv, out_ref, grad_mixed = refs
    j = pl.program_id(0)
    bf, f32 = jnp.bfloat16, jnp.float32

    @pl.when(j == 0)
    def _():
        grad_mixed[...] = mm_nt(g1_ref[...].astype(bf), w_ref[:, 2304:]).astype(bf)

    for s, pair in pairs_here(SELF_BACKWARD):
        at = pair_columns(pair)
        d_pair = stacked_heads(grad_mixed[:, at])
        queries = stacked_heads(qkv_ref[:, at])
        weights = p_ref[s]
        grads = softmax_back(weights, mm_nt(d_pair, qkv_ref[:, pair_columns(pair, 1536)]))
        dqkv[:, at] = (joined_heads(mm(grads, qkv_ref[:, pair_columns(pair, 768)])) * 0.125).astype(bf)
        dqkv[:, pair_columns(pair, 768)] = (mm_tn(grads, queries) * 0.125).astype(bf)
        dqkv[:, pair_columns(pair, 1536)] = mm_tn(weights, d_pair).astype(bf)

    @pl.when(j == PAIRS // SELF_BACKWARD - 1)
    def _():
        hidden = emb_ref[...].astype(f32)
        back, dgain = rms_back(hidden, gain_ref[...], mm_nt(dqkv[...], w_ref[:, :2304]))
        slots = out_ref.shape[0]
        hits = slot_ref[...] == lax.broadcasted_iota(jnp.int32, (TGT, slots), 1)
        out_ref[:, :D] = mm_tn(hits.astype(bf), (g1_ref[...] + back).astype(bf)).astype(bf)
        row = lax.broadcasted_iota(jnp.int32, (slots, D), 0)
        feature = lax.broadcasted_iota(jnp.int32, (slots, D), 1)
        first = (row // SLOTS) * 6
        owned = (row % SLOTS == 0) & (feature >= first) & (feature < first + 6)
        lane = lax.broadcasted_iota(jnp.int32, (D, 128), 1)
        place = lax.broadcasted_iota(jnp.int32, (D, 128), 0) % 6
        extra = jnp.zeros((slots, 128), f32)
        for k, grad in enumerate((dgain, dg2_ref[...], dg3_ref[...])):
            spread = jnp.where(owned, grad, 0.0).astype(bf)
            extra += mm(spread, (lane == place + 6 * k).astype(bf))
        out_ref[:, D:] = extra.astype(bf)


def self_backward(slot, emb, gain, g1, w, qkv, p, dg2, dg3):
    bf = jnp.bfloat16
    return pl.pallas_call(
        self_backward_kernel,
        grid=(PAIRS // SELF_BACKWARD,),
        in_specs=[
            full(TGT, 1),
            full(TGT, D),
            full(1, D),
            full(TGT, D),
            full(D, 4 * D),
            full(TGT, 3 * D),
            pl.BlockSpec((SELF_BACKWARD, 512, TGT), lambda j: (j, 0, 0)),
            full(1, D),
            full(1, D),
        ],
        out_specs=[full(TGT, 3 * D), full(512, D + 128)],
        out_shape=[shaped(bf, TGT, 3 * D), shaped(bf, 512, D + 128)],
        scratch_shapes=[pltpu.VMEM((TGT, D), bf)],
        compiler_params=params(),
        cost_estimate=cost(8, 10),
        name="self_backward",
    )(slot, emb, gain, g1, w, qkv, p, dg2, dg3)


def self_grads_kernel(pos_ref, emb_ref, gain_ref, g1_ref, mixed_ref, dqkv_ref, *refs):
    mine_ref, other_ref, whole, sem = refs
    bf, f32 = jnp.bfloat16, jnp.float32
    hidden = emb_ref[...].astype(f32)
    normed = turned((hidden * rms_scale(hidden) * gain_ref[...]).astype(bf))
    for k in range(3):
        at = pl.ds(768 * k, 768)
        whole[:, at] = mm(normed, dqkv_ref[:, at]).astype(bf)
    whole[:, 2304:] = mm_tn(mixed_ref[...], g1_ref[...].astype(bf)).astype(bf)
    start_split_whole(pos_ref, whole, [mine_ref, other_ref], sem)
    wait_whole([whole], sem)


def self_grads(pos, emb, gain, g1, mixed, dqkv):
    bf = jnp.bfloat16
    pieces = shaped(bf, 64, BLOCK, 384)
    return pl.pallas_call(
        self_grads_kernel,
        in_specs=[SCALARS] + [pl.BlockSpec(memory_space=pltpu.VMEM)] * 5,
        out_specs=[HBM, HBM],
        out_shape=[pieces, pieces],
        scratch_shapes=[pltpu.VMEM((D, 4 * D), bf), pltpu.SemaphoreType.DMA],
        compiler_params=params(),
        cost_estimate=cost(3, 8),
        name="self_grads",
    )(pos, emb, gain, g1, mixed, dqkv)


def after(v, token):
    return v + (token * 0).astype(v.dtype)


def column_blocks(self_qkv, self_out, cross_qkv, cross_out, ffn_in):
    def chunks(v):
        return v.reshape(6, 8, -1).swapaxes(0, 1)

    flat = [
        jnp.concatenate([jnp.swapaxes(qkv, 0, 1).reshape(6, -1), out], axis=1)
        for qkv, out in ((self_qkv, self_out), (cross_qkv, cross_out))
    ]
    flat.append(jnp.swapaxes(ffn_in, 0, 1).reshape(6, -1))
    whole = jnp.concatenate([chunks(v) for v in flat], axis=2)
    return lax.all_to_all(whole, EIGHT, 0, 0, tiled=True).reshape(BLOCK, -1)


def all_weights(whole, ffn_out):
    tail = ffn_out.reshape(16, 3, 256).swapaxes(0, 1).reshape(BLOCK, 256)
    piece = jnp.concatenate([whole, tail], axis=1)
    return lax.all_gather(piece, TORUS).reshape(4, 4, 4, 2, BLOCK, -1)


def body(
    target_ids,
    tgt_len,
    mem_len,
    embed_table,
    memory,
    self_qkv,
    self_out,
    gain_self,
    cross_qkv,
    cross_out,
    gain_cross,
    ffn_in,
    ffn_out,
    gain_ffn,
    out_grad,
):
    tgt_count = target_ids.shape[1]
    model_width = memory.shape[2]
    own_rows = embed_table.shape[0]
    owner_count = 128
    place_in = [lax.axis_index(ring) for ring in (RING_X, RING_Y, RING_Z, ("c",))]
    pos = jnp.stack(place_in).astype(jnp.int32)

    flat_ids = target_ids.reshape(tgt_count)
    owner_of = flat_ids // own_rows
    local_row = flat_ids - owner_of * own_rows
    owner_hits = (owner_of[:, None] == jnp.arange(owner_count)[None, :]).astype(jnp.int32)
    row_rank = jnp.sum(jnp.cumsum(owner_hits, axis=0) * owner_hits, axis=1) - 1
    slot_index = owner_of * SLOTS + row_rank
    slot_hits = slot_index[:, None] == jnp.arange(owner_count * SLOTS)[None, :]
    wanted = jnp.sum(jnp.where(slot_hits, local_row[:, None] + 1, 0), axis=0)
    gains = jnp.concatenate([gain_self, gain_cross, gain_ffn]).astype(jnp.float32)
    request = jnp.concatenate(
        [
            wanted.astype(jnp.float32).reshape(owner_count, SLOTS),
            jnp.broadcast_to(gains[None], (owner_count, GAINS)),
            jnp.zeros((owner_count, 32 - SLOTS - GAINS), jnp.float32),
        ],
        axis=1,
    )
    whole = column_blocks(self_qkv, self_out, cross_qkv, cross_out, ffn_in)
    arrived = lax.all_to_all(then(request, whole), AXES, split_axis=0, concat_axis=0, tiled=True)
    gain_self_all, gain_cross_all, gain_ffn_all = (
        arrived[:, SLOTS + 6 * k : SLOTS + 6 * k + 6].reshape(1, model_width) for k in range(3)
    )
    rows_wanted = arrived[:, :SLOTS].reshape(owner_count * SLOTS).astype(jnp.int32) - 1
    row_hits = (rows_wanted[:, None] == jnp.arange(own_rows)[None, :]).astype(jnp.bfloat16)
    fetched = jnp.dot(row_hits, embed_table, preferred_element_type=jnp.float32)
    fetched = fetched.astype(jnp.bfloat16).reshape(owner_count, SLOTS, model_width)
    returned = lax.all_to_all(fetched, AXES, split_axis=0, concat_axis=0, tiled=True)
    memory_rows = memory[0]
    memory_turned = jnp.pad(memory_rows.T, ((0, 0), (0, KEYS - MEM)))
    blocks = all_weights(whole, ffn_out)
    slot = slot_index.reshape(tgt_count, 1)

    embedded, self_proj, self_p, self_mixed, hidden_one, self_w = self_forward(
        returned.reshape(owner_count * SLOTS, model_width), slot, gain_self_all, memory_turned,
        blocks,
    )
    query, key, value, cross_p, cross_mixed, hidden_two, cross_w = cross_forward(
        mem_len, hidden_one, gain_cross_all, memory_rows, blocks
    )
    result, grad_two, gain_ffn_grad, pieces = ffn_both(
        tgt_len, hidden_two, gain_ffn_all, out_grad[0], blocks
    )
    ffn_sum = pieces.reshape(8, 4, 4, BLOCK, 768)
    for ring in (("x", "c"), RING_Y, RING_Z):
        ffn_sum = lax.psum_scatter(ffn_sum, ring)
    rings = ("z", "x", "y")
    grad_query, grad_kv, grad_one, gain_cross_grad = cross_backward(
        hidden_one, gain_cross_all, grad_two, cross_w, query, key, value, cross_p
    )
    mine, other = cross_grads(
        rings, pos, hidden_one, gain_cross_all, grad_two, memory_turned, cross_mixed,
        grad_query, grad_kv,
    )
    cross_sum = ring_sum(mine, other, rings)
    grad_proj, outgoing = self_backward(
        slot, embedded, gain_self_all, grad_one, self_w, self_proj, self_p,
        gain_cross_grad, gain_ffn_grad,
    )
    mine, other = self_grads(
        pos, embedded, gain_self_all, grad_one, self_mixed, grad_proj
    )
    self_sum = lax.all_to_all(add_low(mine, swap_cores(other)), CHIPS, 0, 0, tiled=True)
    self_sum = jnp.sum(self_sum.astype(jnp.float32), axis=0)
    memory_grad = jnp.einsum(
        "me,de->md", grad_kv[:MEM], cross_w[:, 768:2304], preferred_element_type=jnp.float32
    )[None]

    outgoing = outgoing.reshape(owner_count, SLOTS, model_width + 128)
    incoming = lax.all_to_all(outgoing, AXES, split_axis=0, concat_axis=0, tiled=True)
    incoming = incoming.reshape(owner_count * SLOTS, model_width + 128)
    gain_sums = jnp.sum(incoming[:, model_width : model_width + GAINS].astype(jnp.float32), axis=0)
    table_grad = jnp.einsum(
        "sr,sd->rd", row_hits, incoming[:, :model_width], preferred_element_type=jnp.float32
    )

    sums = jnp.concatenate([self_sum, cross_sum, ffn_sum[:, :512].astype(jnp.float32)], axis=1)
    sums = lax.all_to_all(sums.reshape(8, 6, -1), EIGHT, 0, 0, tiled=True)

    def rows_of(v):
        return jnp.swapaxes(v, 0, 1).reshape(6, -1)

    done = []
    for at in (0, 384):
        whole = rows_of(sums[:, :, at : at + 384])
        done.append(jnp.swapaxes(whole[:, :2304].reshape(6, 3, model_width), 0, 1))
        done.append(whole[:, 2304:])
    ffn_in_sum = jnp.swapaxes(rows_of(sums[:, :, 768:]).reshape(6, 2, 2048), 0, 1)
    ffn_out_sum = ffn_sum[:, 512:].astype(jnp.float32).reshape(3, 16, 256).swapaxes(0, 1).reshape(16, model_width)
    return (
        result[None],
        memory_grad,
        table_grad,
        done[0],
        done[1],
        gain_sums[:6],
        done[2],
        done[3],
        gain_sums[6:12],
        ffn_in_sum,
        ffn_out_sum,
        gain_sums[12:18],
    )


def solution(mesh):
    fine = Mesh(mesh.devices.reshape(SIZES), AXES)
    in_specs = (
        P(AXES, None),
        P(AXES),
        P(AXES),
        P(AXES, None),
        P(AXES, None, None),
        P(None, AXES, None),
        P(AXES, None),
        P(AXES),
        P(None, AXES, None),
        P(AXES, None),
        P(AXES),
        P(None, AXES, None),
        P(AXES, None),
        P(AXES),
        P(AXES, None, None),
    )
    out_specs = (
        P(AXES, None, None),
        P(AXES, None, None),
        P(AXES, None),
        P(None, AXES, None),
        P(AXES, None),
        P(AXES),
        P(None, AXES, None),
        P(AXES, None),
        P(AXES),
        P(None, AXES, None),
        P(AXES, None),
        P(AXES),
    )
    return jax.shard_map(body, mesh=fine, in_specs=in_specs, out_specs=out_specs, check_vma=False)
```

profile of v0, /device:TPU:0, one launch (start us, length us, event | category | flops | bytes accessed | tf_op | source)
XLA Modules:
  0.0 329.6 jit_solution(17829111435868095236)
XLA Ops:
  7.2 1.0 reshape_reshape.6
  8.2 0.8 pad_maximum_fusion.4
  9.0 0.8 pad_maximum_fusion.3
  9.8 0.7 pad_maximum_fusion.1
  10.5 4.3 %all-to-all-start = ((bf16[8,6,1280]{2,1,0:T(8,128)(2,1)}), bf16[8,6,1280]{2,1,0:T(8,128)(2,1)S(1)}, u32[]{:S(2)}, u32[]{:S(2)}) async-start(bf16[8,6,1280]{2,1,0:T(8,128)(2,1)} %pad_maximum_fusion.1), calls=%async_computation | async-start | bytes 327680 | tf_op jit(solution)/shard_map/all_to_all | solution.py:712
  14.9 0.8 reshape.304
  15.6 5.1 %all-to-all-done = bf16[8,6,1280]{2,1,0:T(8,128)(2,1)S(1)} async-done(((bf16[8,6,1280]{2,1,0:T(8,128)(2,1)}), bf16[8,6,1280]{2,1,0:T(8,128)(2,1)S(1)}, u32[]{:S(2)}, u32[]{:S(2)}) %all-to-all-start) | async-done | bytes 122912 | tf_op jit(solution)/shard_map/all_to_all | solution.py:712
  20.8 0.7 pad_maximum_fusion.2
  21.5 0.7 fusion.22
  22.2 0.7 broadcast_divide_fusion
  24.3 19.6 %all_to_all.37 = f32[128,1,32]{2,1,0:T(1,128)S(1)} all-to-all(f32[128,1,32]{2,1,0:T(1,128)S(1)} %bitcast.116), channel_id=1, replica_groups=mesh['x'=4,'yh'=2,'zh'=2,'zl'=2,'yl'=2,'c'=2] {'x','yh','zh','zl','yl','c'}, dimensions={0} | all-to-all | bytes 32768 | tf_op jit(solution)/shard_map/all_to_all | solution.py:763
  44.1 2.9 fusion.6
  46.9 2.4 reshape.301
  49.3 4.6 %all-to-all-start.2 = ((bf16[128,4,768]{2,1,0:T(4,128)(2,1)}), bf16[128,4,768]{2,1,0:T(4,128)(2,1)S(1)}, u32[]{:S(2)}, u32[]{:S(2)}) async-start(bf16[128,4,768]{2,1,0:T(4,128)(2,1)} %reshape.301), calls=%async_computation.2 | async-start | bytes 1572864 | tf_op jit(solution)/shard_map/all_to_all | solution.py:771
  54.4 3.2 copy.87
  58.9 1.4 pad.4.early_ref.mem_t_ref
  60.3 0.7 fusion.15.slot_ref
  61.1 0.7 reshape.303.gain_ref
  61.8 0.7 reshape.307.gain_ref
  62.6 0.7 reshape.308.gain_ref
  63.3 10.8 %all-to-all-done.2 = bf16[128,4,768]{2,1,0:T(4,128)(2,1)S(1)} async-done(((bf16[128,4,768]{2,1,0:T(4,128)(2,1)}), bf16[128,4,768]{2,1,0:T(4,128)(2,1)S(1)}, u32[]{:S(2)}, u32[]{:S(2)}) %all-to-all-start.2) | async-done | bytes 786464 | tf_op jit(solution)/shard_map/all_to_all | solution.py:771
  74.0 1.1 reshape.302.rows_ref
  75.1 37.9 %all-gather.3.cloned.1.call-done = bf16[6144,1536]{1,0:T(8,128)(2,1)} async-done(((bf16[48,1536]{1,0:T(8,128)(2,1)}), bf16[6144,1536]{1,0:T(8,128)(2,1)}) %all-gather.3.cloned.1.call-update) | async-done | bytes 18874384 | tf_op jit(solution)/shard_map/all_gather | solution.py:718
  113.0 7.8 %self_forward.1 = (bf16[256,768]{1,0:T(8,128)(2,1)}, bf16[256,2304]{1,0:T(8,128)(2,1)}, bf16[6,512,256]{2,1,0:T(8,128)(2,1)}, bf16[256,768]{1,0:T(8,128)(2,1)}, ...) custom-call(bf16[512,768]{1,0:T(8,128)(2,1)} %reshape.302.rows_ref, s32[256,1]{1,0:T(8,128)} %fusion.15.slot_ref, ...), custom_call_target="tpu_custom_call" | custom-call | flops 8000000000 | bytes 12000000 | tf_op jit(solution)/shard_map/self_forward/pallas_call | solution.py:305
  120.8 20.8 %cross_forward.1 = (bf16[256,768]{1,0:T(8,128)(2,1)}, bf16[1152,768]{1,0:T(8,128)(2,1)}, bf16[1152,768]{1,0:T(8,128)(2,1)}, bf16[6,512,1152]{2,1,0:T(8,128)(2,1)...) custom-call(s32[1]{0:T(128)S(6)} %copy.99.len_ref, ...), custom_call_target="tpu_custom_call" | custom-call | flops 20000000000 | bytes 20000000 | tf_op jit(solution)/shard_map/cross_forward/pallas_call | solution.py:366
  141.7 16.9 %ffn_both.1 = (f32[256,768]{1,0:T(8,128)}, f32[256,768]{1,0:T(8,128)}, f32[1,768]{1,0:T(1,128)}, bf16[4,2,4,4,48,768]{5,4,3,2,1,0:T(8,128)(2,1)}) custom-call(s32[1]{0:T(128)S(6)} %copy.98.len_ref, f32[256,768]{1,0:T(8,128)} %get-tuple-element.42.h2_ref, f32[1,768]{1,0:T(1,128)} %reshape.308.gain_ref, bf16[256,768]{1,0:T(8,128)(2,1)} %bitcast.139, ...), custom_call_target="tpu_custom_call" | custom-call | flops 15000000512 | bytes 25000000 | tf_op jit(solution)/shard_map/ffn_both/pallas_call | solution.py:491
  158.6 0.6 pad_add_fusion.pos_ref
  159.2 16.6 %cross_backward.1 = (bf16[256,768]{1,0:T(8,128)(2,1)}, bf16[1152,1536]{1,0:T(8,128)(2,1)}, f32[256,768]{1,0:T(8,128)}, f32[1,768]{1,0:T(1,128)}) custom-call(f32[256,768]{1,0:T(8,128)} %get-tuple-element.41.h1_ref, f32[1,768]{1,0:T(1,128)} %reshape.307.gain_ref, f32[256,768]{1,0:T(8,128)} %get-tuple-element.44.g2_ref, ...), custom_call_target="tpu_custom_call" | custom-call | flops 16000000000 | bytes 20000000 | tf_op jit(solution)/shard_map/cross_backward/pallas_call | solution.py:547
  175.8 10.7 %cross_grads.1 = (bf16[4,4,4,48,384]{4,3,2,1,0:T(8,128)(2,1)}, bf16[4,4,4,48,384]{4,3,2,1,0:T(8,128)(2,1)}) custom-call(s32[4]{0:T(128)} %pad_add_fusion.pos_ref, f32[256,768]{1,0:T(8,128)} %get-tuple-element.41.h1_ref, f32[1,768]{1,0:T(1,128)} %reshape.307.gain_ref, f32[256,768]{1,0:T(8,128)} %get-tuple-element.44.g2_ref, ...), custom_call_target="tpu_custom_call" | custom-call | flops 6000000000 | bytes 12000000 | tf_op jit(solution)/shard_map/cross_grads/pallas_call | solution.py:594
  186.5 0.4 collective-permute-start.1
  186.9 11.2 %self_backward.1 = (bf16[256,2304]{1,0:T(8,128)(2,1)}, bf16[512,896]{1,0:T(8,128)(2,1)}) custom-call(s32[256,1]{1,0:T(8,128)} %fusion.15.slot_ref, bf16[256,768]{1,0:T(8,128)(2,1)} %get-tuple-element.51.emb_ref, f32[1,768]{1,0:T(1,128)} %reshape.303.gain_ref, f32[256,768]{1,0:T(8,128)} %get-tuple-element.52.g1_ref, ...), custom_call_target="tpu_custom_call" | custom-call | flops 8000000000 | bytes 10000000 | tf_op jit(solution)/shard_map/self_backward/pallas_call | solution.py:647
  198.0 5.7 %self_grads.1 = (bf16[64,48,384]{2,1,0:T(8,128)(2,1)}, bf16[64,48,384]{2,1,0:T(8,128)(2,1)}) custom-call(s32[4]{0:T(128)} %pad_add_fusion.pos_ref, bf16[256,768]{1,0:T(8,128)(2,1)} %get-tuple-element.51.emb_ref, f32[1,768]{1,0:T(1,128)} %reshape.303.gain_ref, f32[256,768]{1,0:T(8,128)} %get-tuple-element.52.g1_ref, ...), custom_call_target="tpu_custom_call" | custom-call | flops 3000000000 | bytes 8000000 | tf_op jit(solution)/shard_map/self_grads/pallas_call | solution.py:686
  203.7 0.4 collective-permute-start
  204.1 1.7 add_convert_fusion.2
  205.8 2.4 collective-permute-start.2
  208.3 1.2 reshape.309
  209.5 7.6 %all-to-all-start.3 = ((bf16[128,4,896]{2,1,0:T(4,128)(2,1)}), bf16[128,4,896]{2,1,0:T(4,128)(2,1)S(1)}, u32[]{:S(2)}, u32[]{:S(2)}) async-start(bf16[128,4,896]{2,1,0:T(4,128)(2,1)} %reshape.309), calls=%async_computation.3 | async-start | bytes 1835008 | tf_op jit(solution)/shard_map/all_to_all | solution.py:813
  217.1 14.9 %collective-permute-done.2 = bf16[2,4,4,48,384]{4,3,2,1,0:T(8,128)(2,1)} collective-permute-done((bf16[2,4,4,48,384]{4,3,2,1,0:T(8,128)(2,1)}, bf16[2,4,4,48,384]{4,3,2,1,0:T(8,128)(2,1)}, u32[]{:S(2)}, u32[]{:S(2)}) %collective-permute-start.2) | collective-permute-done | bytes 1179680 | tf_op jit(solution)/shard_map/ppermute | solution.py:43
  231.9 1.2 fusion.8
  233.3 4.4 %add_convert_fusion = bf16[64,48,384]{2,1,0:T(8,128)(2,1)} fusion(bf16[64,48,384]{2,1,0:T(8,128)(2,1)} %collective-permute-done, bf16[64,48,384]{2,1,0:T(8,128)(2,1)} %get-tuple-element.61), kind=kLoop, calls=%fused_computation.1 | loop fusion | flops 4718592 | bytes 7077888 | tf_op jit(solution)/shard_map/convert_element_type | solution.py:55
  237.7 10.7 %all-to-all-start.4 = ((bf16[64,48,384]{2,1,0:T(8,128)(2,1)}), bf16[64,48,384]{2,1,0:T(8,128)(2,1)}, u32[]{:S(2)}, u32[]{:S(2)}) async-start(bf16[64,48,384]{2,1,0:T(8,128)(2,1)} %add_convert_fusion), calls=%async_computation.4 | async-start | bytes 4718592 | tf_op jit(solution)/shard_map/all_to_all | solution.py:806
  248.5 1.5 fusion.10
  250.0 3.0 collective-permute-start.4
  253.0 7.1 %convolution_bitcast_fusion = f32[1,1056,768]{2,1,0:T(8,128)} fusion(bf16[1152,1536]{1,0:T(8,128)(2,1)} %get-tuple-element.50.dkv_ref, bf16[768,3072]{1,0:T(8,128)(2,1)} %get-tuple-element.45.w_ref), kind=kOutput, calls=%fused_computation.5 | convolution fusion | flops 2491416576 | bytes 8847360 | tf_op jit(solution)/shard_map/me,de->md/dot_general | solution.py:808
  260.3 18.4 %collective-permute-done.4 = bf16[2,4,48,384]{3,2,1,0:T(8,128)(2,1)S(1)} collective-permute-done((bf16[2,4,48,384]{3,2,1,0:T(8,128)(2,1)S(1)}, bf16[2,4,48,384]{3,2,1,0:T(8,128)(2,1)S(1)}, u32[]{:S(2)}, u32[]{:S(2)}) %collective-permute-start.4) | collective-permute-done | bytes 294944 | tf_op jit(solution)/shard_map/ppermute | solution.py:43
  278.9 4.5 %fusion = f32[1954,768]{1,0:T(8,128)} fusion(s32[512]{0:T(512)S(1)} %sub.34, bf16[512,896]{1,0:T(8,128)(2,1)S(1)} %reshape.310), kind=kOutput, calls=%fused_computation.3 | convolution fusion | flops 1537688576 | bytes 6791168 | tf_op jit(solution)/shard_map/sr,sd->rd/dot_general | solution.py:816
  283.5 0.4 collective-permute-done.5
  284.0 2.8 collective-permute-start.6
  286.8 0.6 fusion.25
  287.4 2.2 collective-permute-done.6
  290.0 2.2 convert_reduce_fusion
  292.1 1.5 collective-permute-done.7
  293.7 12.3 %reduce-scatter.8.cloned.1.call-done = bf16[1,48,768]{2,1,0:T(8,128)(2,1)} async-done(((bf16[4,48,768]{2,1,0:T(8,128)(2,1)}), bf16[1,48,768]{2,1,0:T(8,128)(2,1)}) %reduce-scatter.8.cloned.1.call-update) | async-done | bytes 73744 | tf_op jit(solution)/shard_map/reduce_scatter | solution.py:789
  305.9 0.8 slice_convert_fusion.1
  306.7 0.7 slice.241
  307.5 0.8 reshape.312
  308.3 3.4 %all-to-all-start.5 = ((f32[8,6,1280]{2,1,0:T(8,128)}), f32[8,6,1280]{2,1,0:T(8,128)S(1)}, u32[]{:S(2)}, u32[]{:S(2)}) async-start(f32[8,6,1280]{2,1,0:T(8,128)} %reshape.312), calls=%async_computation.8 | async-start | bytes 655360 | tf_op jit(solution)/shard_map/all_to_all | solution.py:821
  311.7 0.6 copy.95
  312.3 6.9 %all-to-all-done.5 = f32[8,6,1280]{2,1,0:T(8,128)S(1)} async-done(((f32[8,6,1280]{2,1,0:T(8,128)}), f32[8,6,1280]{2,1,0:T(8,128)S(1)}, u32[]{:S(2)}, u32[]{:S(2)}) %all-to-all-start.5) | async-done | bytes 245792 | tf_op jit(solution)/shard_map/all_to_all | solution.py:821
  319.3 0.6 slice.234
  319.9 0.6 slice.235
  320.5 0.6 slice.238
  321.2 0.6 slice.239
  321.9 0.7 reshape_reshape.7
  (77 shorter events, 3.6 us)
Async XLA Ops:
  7.2 36.9 %copy-start = (bf16[1954,768]{1,0:T(8,128)(2,1)S(1)}, bf16[1954,768]{1,0:T(8,128)(2,1)}, u32[]{:S(2)}) copy-start(bf16[1954,768]{1,0:T(8,128)(2,1)} %param.18) | copy-start | bytes 9004036
  7.2 16.1 %copy-start.4 = (s32[1,256]{1,0:T(1,128)S(1)}, s32[1,256]{1,0:T(1,128)}, u32[]{:S(2)}) copy-start(s32[1,256]{1,0:T(1,128)} %param.15) | copy-start | bytes 3076
  7.2 16.7 %copy-start.7 = (bf16[6]{0:T(256)(128)(2,1)S(1)}, bf16[6]{0:T(256)(128)(2,1)}, u32[]{:S(2)}) copy-start(bf16[6]{0:T(256)(128)(2,1)} %param.22) | copy-start | bytes 40
  7.2 16.6 %copy-start.6 = (bf16[6]{0:T(256)(128)(2,1)S(1)}, bf16[6]{0:T(256)(128)(2,1)}, u32[]{:S(2)}) copy-start(bf16[6]{0:T(256)(128)(2,1)} %param.25) | copy-start | bytes 40
  7.2 16.6 %copy-start.5 = (bf16[6]{0:T(256)(128)(2,1)S(1)}, bf16[6]{0:T(256)(128)(2,1)}, u32[]{:S(2)}) copy-start(bf16[6]{0:T(256)(128)(2,1)} %param.28) | copy-start | bytes 40
  10.5 10.2 %all-to-all-start = ((bf16[8,6,1280]{2,1,0:T(8,128)(2,1)}), bf16[8,6,1280]{2,1,0:T(8,128)(2,1)S(1)}, u32[]{:S(2)}, u32[]{:S(2)}) async-start(bf16[8,6,1280]{2,1,0:T(8,128)(2,1)} %pad_maximum_fusion.1), calls=%async_computation | async-start | bytes 327680 | tf_op jit(solution)/shard_map/all_to_all | solution.py:712
  14.8 98.2 %all-gather.3.cloned.1.call-start = ((), (), s32[]{:S(2)}) async-start(), calls=%async_computation.12 | async-start | bytes 19021824 | tf_op jit(solution)/shard_map/all_gather | solution.py:718
  49.3 24.8 %all-to-all-start.2 = ((bf16[128,4,768]{2,1,0:T(4,128)(2,1)}), bf16[128,4,768]{2,1,0:T(4,128)(2,1)S(1)}, u32[]{:S(2)}, u32[]{:S(2)}) async-start(bf16[128,4,768]{2,1,0:T(4,128)(2,1)} %reshape.301), calls=%async_computation.2 | async-start | bytes 1572864 | tf_op jit(solution)/shard_map/all_to_all | solution.py:771
  53.9 179.4 %reduce-scatter.4.cloned.1.call-start = ((), (), s32[]{:S(2)}) async-start(), calls=%async_computation.9 | async-start | bytes 10616832 | tf_op jit(solution)/shard_map/reduce_scatter | solution.py:789
  186.5 17.6 %collective-permute-start.1 = (bf16[4,4,4,48,384]{4,3,2,1,0:T(8,128)(2,1)}, bf16[4,4,4,48,384]{4,3,2,1,0:T(8,128)(2,1)S(1)}, u32[]{:S(2)}, u32[]{:S(2)}) collective-permute-start(bf16[4,4,4,48,384]{4,3,2,1,0:T(8,128)(2,1)} %get-tuple-element.66), channel_id=1, source_target_pairs={{0,1},{1,0},{2,3},{3,2},{4,5},{5,4},{6,7},{7,6},{8,9},{9,8},{10,11... | collective-permute-start | bytes 7077896 | tf_op jit(solution)/shard_map/ppermute | solution.py:47
  198.0 6.1 %copy-start.2 = (bf16[4,4,4,48,384]{4,3,2,1,0:T(8,128)(2,1)S(1)}, bf16[4,4,4,48,384]{4,3,2,1,0:T(8,128)(2,1)}, u32[]{:S(2)}) copy-start(bf16[4,4,4,48,384]{4,3,2,1,0:T(8,128)(2,1)} %get-tuple-element.65) | copy-start | bytes 7077892
  203.7 29.6 %collective-permute-start = (bf16[64,48,384]{2,1,0:T(8,128)(2,1)}, bf16[64,48,384]{2,1,0:T(8,128)(2,1)}, u32[]{:S(2)}, u32[]{:S(2)}) collective-permute-start(bf16[64,48,384]{2,1,0:T(8,128)(2,1)} %get-tuple-element.62), channel_id=1, source_target_pairs={{0,1},{1,0},{2,3},{3,2},{4,5},{5,4},{6,7},{7,6},{8,9},{9,8},{10,11... | collective-permute-start | bytes 7077896 | tf_op jit(solution)/shard_map/ppermute | solution.py:47
  204.1 4.1 %copy-start.3 = (bf16[512,896]{1,0:T(8,128)(2,1)S(1)}, bf16[512,896]{1,0:T(8,128)(2,1)}, u32[]{:S(2)}) copy-start(bf16[512,896]{1,0:T(8,128)(2,1)} %get-tuple-element.58) | copy-start | bytes 2752516
  205.8 26.1 %collective-permute-start.2 = (bf16[2,4,4,48,384]{4,3,2,1,0:T(8,128)(2,1)}, bf16[2,4,4,48,384]{4,3,2,1,0:T(8,128)(2,1)}, u32[]{:S(2)}, u32[]{:S(2)}) collective-permute-start(bf16[2,4,4,48,384]{4,3,2,1,0:T(8,128)(2,1)} %get-tuple-element.73), channel_id=1, source_target_pairs={{0,12},{1,5},{4,8},{5,1},{8,4},{9,13},{12,0},{13,9},{2,14},{3,7},{... | collective-permute-start | bytes 3538952 | tf_op jit(solution)/shard_map/ppermute | solution.py:43
  209.5 28.3 %all-to-all-start.3 = ((bf16[128,4,896]{2,1,0:T(4,128)(2,1)}), bf16[128,4,896]{2,1,0:T(4,128)(2,1)S(1)}, u32[]{:S(2)}, u32[]{:S(2)}) async-start(bf16[128,4,896]{2,1,0:T(4,128)(2,1)} %reshape.309), calls=%async_computation.3 | async-start | bytes 1835008 | tf_op jit(solution)/shard_map/all_to_all | solution.py:813
  217.0 70.4 %reduce-scatter.6.cloned.1.call-start = ((), (), s32[]{:S(2)}) async-start(), calls=%async_computation.10 | async-start | bytes 1474560 | tf_op jit(solution)/shard_map/reduce_scatter | solution.py:789
  233.2 15.3 %collective-permute-start.3 = (bf16[4,4,48,384]{3,2,1,0:T(8,128)(2,1)S(1)}, bf16[4,4,48,384]{3,2,1,0:T(8,128)(2,1)}, u32[]{:S(2)}, u32[]{:S(2)}) collective-permute-start(bf16[4,4,48,384]{3,2,1,0:T(8,128)(2,1)S(1)} %fusion.8), channel_id=1, source_target_pairs={{0,4},{1,13},{4,0},{5,9},{8,12},{9,5},{12,8},{13,1},{2,6},{3,15},{... | collective-permute-start | bytes 1769480 | tf_op jit(solution)/shard_map/ppermute | solution.py:43
  237.7 52.2 %all-to-all-start.4 = ((bf16[64,48,384]{2,1,0:T(8,128)(2,1)}), bf16[64,48,384]{2,1,0:T(8,128)(2,1)}, u32[]{:S(2)}, u32[]{:S(2)}) async-start(bf16[64,48,384]{2,1,0:T(8,128)(2,1)} %add_convert_fusion), calls=%async_computation.4 | async-start | bytes 4718592 | tf_op jit(solution)/shard_map/all_to_all | solution.py:806
  248.5 57.5 %reduce-scatter.8.cloned.1.call-start = ((), (), s32[]{:S(2)}) async-start(), calls=%async_computation.11 | async-start | bytes 368640 | tf_op jit(solution)/shard_map/reduce_scatter | solution.py:789
  250.0 28.7 %collective-permute-start.4 = (bf16[2,4,48,384]{3,2,1,0:T(8,128)(2,1)S(1)}, bf16[2,4,48,384]{3,2,1,0:T(8,128)(2,1)S(1)}, u32[]{:S(2)}, u32[]{:S(2)}) collective-permute-start(bf16[2,4,48,384]{3,2,1,0:T(8,128)(2,1)S(1)} %get-tuple-element.75), channel_id=1, source_target_pairs={{0,96},{1,33},{32,64},{33,1},{64,32},{65,97},{96,0},{97,65},{2,98}... | collective-permute-start | bytes 884744 | tf_op jit(solution)/shard_map/ppermute | solution.py:43
  278.7 5.2 %collective-permute-start.5 = (bf16[4,48,384]{2,1,0:T(8,128)(2,1)S(1)}, bf16[4,48,384]{2,1,0:T(8,128)(2,1)S(1)}, u32[]{:S(2)}, u32[]{:S(2)}) collective-permute-start(bf16[4,48,384]{2,1,0:T(8,128)(2,1)S(1)} %fusion.11), channel_id=1, source_target_pairs={{0,32},{1,97},{32,0},{33,65},{64,96},{65,33},{96,64},{97,1},{2,34}... | collective-permute-start | bytes 442376 | tf_op jit(solution)/shard_map/ppermute | solution.py:43
  284.0 5.6 %collective-permute-start.6 = (bf16[2,48,384]{2,1,0:T(8,128)(2,1)S(1)}, bf16[2,48,384]{2,1,0:T(8,128)(2,1)S(1)}, u32[]{:S(2)}, u32[]{:S(2)}) collective-permute-start(bf16[2,48,384]{2,1,0:T(8,128)(2,1)S(1)} %get-tuple-element.77), channel_id=1, source_target_pairs={{0,18},{1,3},{2,16},{3,1},{16,2},{17,19},{18,0},{19,17},{4,22},{5,... | collective-permute-start | bytes 221192 | tf_op jit(solution)/shard_map/ppermute | solution.py:43
  289.6 4.0 %collective-permute-start.7 = (bf16[48,384]{1,0:T(8,128)(2,1)S(1)}, bf16[48,384]{1,0:T(8,128)(2,1)S(1)}, u32[]{:S(2)}, u32[]{:S(2)}) collective-permute-start(bf16[48,384]{1,0:T(8,128)(2,1)S(1)} %fusion.21), channel_id=1, source_target_pairs={{0,2},{1,19},{2,0},{3,17},{16,18},{17,3},{18,16},{19,1},{4,6},{5,2... | collective-permute-start | bytes 110600 | tf_op jit(solution)/shard_map/ppermute | solution.py:43
  290.0 32.6 %copy-start.1 = (bf16[1954,768]{1,0:T(8,128)(2,1)S(1)}, bf16[1954,768]{1,0:T(8,128)(2,1)}, u32[]{:S(2)}) copy-start(bf16[1954,768]{1,0:T(8,128)(2,1)} %param.18) | copy-start | bytes 9004036
  308.3 11.0 %all-to-all-start.5 = ((f32[8,6,1280]{2,1,0:T(8,128)}), f32[8,6,1280]{2,1,0:T(8,128)S(1)}, u32[]{:S(2)}, u32[]{:S(2)}) async-start(f32[8,6,1280]{2,1,0:T(8,128)} %reshape.312), calls=%async_computation.8 | async-start | bytes 655360 | tf_op jit(solution)/shard_map/all_to_all | solution.py:821
Sparse Core Ops, SparseCore 0:
  21.6 91.4 all-gather.2
  158.7 56.8 reduce-scatter.3
  233.4 48.5 reduce-scatter.5
  287.5 18.3 reduce-scatter.7
where the time goes:
time: 335 us; the launch traced here: 330 us
  waiting for transfers between devices  110 us (33%)
  Pallas kernels  89.6 us (27%)
  starting transfers between devices  40.5 us (12%)
  local copies, waits for them, and re-layouts  20.7 us (6%)
  blocking collectives  19.6 us (6%)
  other arithmetic  18.4 us (5%)
  between operations  15.9 us (5%)
  matrix products  14.4 us (4%)
    all_gather x1, waiting for transfers between devices, all_weights(): return lax.all_gather(piece, TORUS).reshape(4, 4, 4, 2, BLOCK, -1)  37.9 us
    ppermute x6, waiting for transfers between devices, ring_pair(): return lax.ppermute(v, ring + ('c',), perm)  37.4 us
    pallas_call x1, Pallas kernels, cross_forward(): pl.pallas_call(cross_forward_kernel, grid=(PAIRS // CROSS_FORWARD,), in_s...  20.8 us
    all_to_all x1, blocking collectives, body(): lax.all_to_all(then(request, whole), AXES, split_axis=0, concat_axis=0, t...  19.6 us
    pallas_call x1, Pallas kernels, ffn_both(): pl.pallas_call(ffn_kernel, grid=(FF // 512,), in_specs=[SCALARS, full(TGT...  16.9 us
    pallas_call x1, Pallas kernels, cross_backward(): pl.pallas_call(cross_backward_kernel, grid=(PAIRS // CROSS_BACKWARD,), in...  16.6 us
    reduce_scatter x3, waiting for transfers between devices, body(): ffn_sum = lax.psum_scatter(ffn_sum, ring)  12.3 us
    pallas_call x1, Pallas kernels, self_backward(): pl.pallas_call(self_backward_kernel, grid=(PAIRS // SELF_BACKWARD,), in_s...  11.2 us
  transfers between devices with their start and end apart: 17, of which 10 were waited for; matrix products, arithmetic and copies ran while one was open for 13% of the time, Pallas kernels for 13%

commit v1 on v0

--- a/solution.py
+++ b/solution.py
@@ -55,19 +55,25 @@
     return sum(t.astype(jnp.float32) for t in terms).astype(jnp.bfloat16)
 
 
-def halve(low, high, ring):
-    got = ring_pair(high, ring, False)
-    back = ring_pair(add_low(low[1], got[1]), ring, True)
-    return low[0], got[0], back
-
-
-def ring_sum(mine, other, rings):
-    got = swap_cores(other)
-    low, high = add_low(mine[:2], got[:2]), add_low(mine[2:], got[2:])
-    for ring in rings[:-1]:
-        terms = halve(low, high, RINGS[ring])
-        low, high = (add_low(*(t[at] for t in terms)) for at in (slice(0, 2), slice(2, 4)))
-    return sum(t.astype(jnp.float32) for t in halve(low, high, RINGS[rings[-1]]))
+def ring_sum_start(mine, got):
+    return add_low(mine[:2], got[:2]), add_low(mine[2:], got[2:])
+
+
+def ring_first(low, high, ring):
+    got = ring_pair(high, RINGS[ring], False)
+    return low[0], got[0], add_low(low[1], got[1])
+
+
+def ring_second(terms, ring):
+    return terms[0], terms[1], ring_pair(terms[2], RINGS[ring], True)
+
+
+def ring_halves(terms):
+    return tuple(add_low(*(t[at] for t in terms)) for at in (slice(0, 2), slice(2, 4)))
+
+
+def ring_total(low, high, ring):
+    return sum(t.astype(jnp.float32) for t in ring_second(ring_first(low, high, ring), ring))
 
 
 def mm(a, b):
@@ -184,17 +190,6 @@
                         ).start()
 
 
-def start_split_whole(pos_ref, whole, outs, sem):
-    for source in range(2):
-        core = pos_ref[3] ^ source
-        for group in range(16):
-            for q in range(4):
-                for dst, _, src in square_parts(384, group, 2 * q + core):
-                    pltpu.make_async_copy(
-                        whole.at[src], outs[source].at[(4 * group + q,) + dst], sem
-                    ).start()
-
-
 def wait_whole(refs, sem):
     for ref in refs:
         pltpu.make_async_copy(ref, ref, sem).wait()
@@ -252,7 +247,8 @@
 
 
 def self_forward_kernel(rows_ref, slot_ref, gain_ref, early_ref, blocks, *refs):
-    emb_ref, qkv_ref, p_ref, mixed_ref, h1_ref, w_ref, sem = refs
+    kept_ref, qkv_ref, p_ref, h1_ref, w_ref, sem = refs
+    emb_ref, mixed_ref = kept_ref.at[:, :D], kept_ref.at[:, D:]
     j = pl.program_id(0)
 
     @pl.when(j == 0)
@@ -307,18 +303,16 @@
         grid=(PAIRS // SELF_FORWARD,),
         in_specs=[full(512, D), full(TGT, 1), full(1, D), HBM, HBM],
         out_specs=[
-            full(TGT, D),
+            full(TGT, 2 * D),
             full(TGT, 3 * D),
             pl.BlockSpec((SELF_FORWARD, 512, TGT), lambda j: (j, 0, 0)),
-            full(TGT, D),
             full(TGT, D),
             full(D, 4 * D),
         ],
         out_shape=[
-            shaped(bf, TGT, D),
+            shaped(bf, TGT, 2 * D),
             shaped(bf, TGT, 3 * D),
             shaped(bf, PAIRS, 512, TGT),
-            shaped(bf, TGT, D),
             shaped(f32, TGT, D),
             shaped(bf, D, 4 * D),
         ],
@@ -603,8 +597,10 @@
     )(pos, h1, gain, g2, mem_t, mixed, dq, dkv)
 
 
-def self_backward_kernel(slot_ref, emb_ref, gain_ref, g1_ref, w_ref, qkv_ref, p_ref, *refs):
-    dg2_ref, dg3_ref, dqkv, out_ref, grad_mixed = refs
+def self_backward_kernel(
+    pos_ref, slot_ref, kept_ref, gain_ref, g1_ref, w_ref, qkv_ref, p_ref, *refs
+):
+    dg2_ref, dg3_ref, mine_ref, other_ref, out_ref, grad_mixed, dqkv = refs
     j = pl.program_id(0)
     bf, f32 = jnp.bfloat16, jnp.float32
 
@@ -624,7 +620,12 @@
 
     @pl.when(j == PAIRS // SELF_BACKWARD - 1)
     def _():
-        hidden = emb_ref[...].astype(f32)
+        for source, half_ref in enumerate((mine_ref, other_ref)):
+            first = pl.multiple_of((pos_ref[3] ^ source) * 384, 128)
+            for k in range(3):
+                half_ref[:, 384 * k : 384 * k + 384] = dqkv[:, pl.ds(768 * k + first, 384)]
+            half_ref[:, 1152:] = g1_ref[:, pl.ds(first, 384)].astype(bf)
+        hidden = kept_ref[:, :D].astype(f32)
         back, dgain = rms_back(hidden, gain_ref[...], mm_nt(dqkv[...], w_ref[:, :2304]))
         slots = out_ref.shape[0]
         hits = slot_ref[...] == lax.broadcasted_iota(jnp.int32, (TGT, slots), 1)
@@ -642,14 +643,15 @@
         out_ref[:, D:] = extra.astype(bf)
 
 
-def self_backward(slot, emb, gain, g1, w, qkv, p, dg2, dg3):
+def self_backward(pos, slot, kept, gain, g1, w, qkv, p, dg2, dg3):
     bf = jnp.bfloat16
     return pl.pallas_call(
         self_backward_kernel,
         grid=(PAIRS // SELF_BACKWARD,),
         in_specs=[
+            SCALARS,
             full(TGT, 1),
-            full(TGT, D),
+            full(TGT, 2 * D),
             full(1, D),
             full(TGT, D),
             full(D, 4 * D),
@@ -658,41 +660,62 @@
             full(1, D),
             full(1, D),
         ],
-        out_specs=[full(TGT, 3 * D), full(512, D + 128)],
-        out_shape=[shaped(bf, TGT, 3 * D), shaped(bf, 512, D + 128)],
-        scratch_shapes=[pltpu.VMEM((TGT, D), bf)],
+        out_specs=[full(TGT, 2 * D), full(TGT, 2 * D), full(512, D + 128)],
+        out_shape=[shaped(bf, TGT, 2 * D), shaped(bf, TGT, 2 * D), shaped(bf, 512, D + 128)],
+        scratch_shapes=[pltpu.VMEM((TGT, D), bf), pltpu.VMEM((TGT, 3 * D), bf)],
         compiler_params=params(),
         cost_estimate=cost(8, 10),
         name="self_backward",
-    )(slot, emb, gain, g1, w, qkv, p, dg2, dg3)
-
-
-def self_grads_kernel(pos_ref, emb_ref, gain_ref, g1_ref, mixed_ref, dqkv_ref, *refs):
-    mine_ref, other_ref, whole, sem = refs
+    )(pos, slot, kept, gain, g1, w, qkv, p, dg2, dg3)
+
+
+def self_grads_kernel(rings, pos_ref, gain_ref, kept_ref, kept_other_ref, half_ref, half_other_ref, *refs):
+    *outs, whole, sem = refs
     bf, f32 = jnp.bfloat16, jnp.float32
-    hidden = emb_ref[...].astype(f32)
-    normed = turned((hidden * rms_scale(hidden) * gain_ref[...]).astype(bf))
-    for k in range(3):
-        at = pl.ds(768 * k, 768)
-        whole[:, at] = mm(normed, dqkv_ref[:, at]).astype(bf)
-    whole[:, 2304:] = mm_tn(mixed_ref[...], g1_ref[...].astype(bf)).astype(bf)
-    start_split_whole(pos_ref, whole, [mine_ref, other_ref], sem)
+
+    def normed(kept):
+        hidden = kept[:, :D].astype(f32)
+        return turned((hidden * rms_scale(hidden) * gain_ref[...]).astype(bf))
+
+    whole[:, :1152] = (
+        mm(normed(kept_ref), half_ref[:, :1152])
+        + mm(normed(kept_other_ref), half_other_ref[:, :1152])
+    ).astype(bf)
+    whole[:, 1152:] = (
+        mm_tn(kept_ref[:, D:], half_ref[:, 1152:])
+        + mm_tn(kept_other_ref[:, D:], half_other_ref[:, 1152:])
+    ).astype(bf)
+    me, at = my_place(pos_ref), {}
+    flips = partners(pos_ref[3])
+    for k3 in range(4):
+        at[rings[0]] = me[rings[0]] ^ flips[k3]
+        for k2 in range(4):
+            at[rings[1]] = me[rings[1]] ^ flips[k2]
+            for k1 in range(4):
+                at[rings[2]] = me[rings[2]] ^ flips[k1]
+                group, member = group_member(at, 0)
+                row = pl.multiple_of(group * BLOCK, 16)
+                column = pl.multiple_of((member >> 1) * 384, 128)
+                pltpu.make_async_copy(
+                    whole.at[pl.ds(row, BLOCK), pl.ds(column, 384)],
+                    outs[k3 // 2].at[k3 % 2, k2, k1],
+                    sem,
+                ).start()
     wait_whole([whole], sem)
 
 
-def self_grads(pos, emb, gain, g1, mixed, dqkv):
+def self_grads(rings, pos, gain, kept, kept_other, half, half_other):
     bf = jnp.bfloat16
-    pieces = shaped(bf, 64, BLOCK, 384)
     return pl.pallas_call(
-        self_grads_kernel,
+        functools.partial(self_grads_kernel, rings),
         in_specs=[SCALARS] + [pl.BlockSpec(memory_space=pltpu.VMEM)] * 5,
         out_specs=[HBM, HBM],
-        out_shape=[pieces, pieces],
-        scratch_shapes=[pltpu.VMEM((D, 4 * D), bf), pltpu.SemaphoreType.DMA],
+        out_shape=[shaped(bf, 2, 4, 4, BLOCK, 384)] * 2,
+        scratch_shapes=[pltpu.VMEM((D, 2 * D), bf), pltpu.SemaphoreType.DMA],
         compiler_params=params(),
         cost_estimate=cost(3, 8),
         name="self_grads",
-    )(pos, emb, gain, g1, mixed, dqkv)
+    )(pos, gain, kept, kept_other, half, half_other)
 
 
 def after(v, token):
@@ -774,7 +797,7 @@
     blocks = all_weights(whole, ffn_out)
     slot = slot_index.reshape(tgt_count, 1)
 
-    embedded, self_proj, self_p, self_mixed, hidden_one, self_w = self_forward(
+    kept, self_proj, self_p, hidden_one, self_w = self_forward(
         returned.reshape(owner_count * SLOTS, model_width), slot, gain_self_all, memory_turned,
         blocks,
     )
@@ -784,38 +807,56 @@
     result, grad_two, gain_ffn_grad, pieces = ffn_both(
         tgt_len, hidden_two, gain_ffn_all, out_grad[0], blocks
     )
-    ffn_sum = pieces.reshape(8, 4, 4, BLOCK, 768)
-    for ring in (("x", "c"), RING_Y, RING_Z):
-        ffn_sum = lax.psum_scatter(ffn_sum, ring)
-    rings = ("z", "x", "y")
+    kept_other = swap_cores(kept)
+    ffn_x = lax.psum_scatter(pieces.reshape(8, 4, 4, BLOCK, 768), ("x", "c"))
+    ffn_y = lax.psum_scatter(ffn_x, RING_Y)
+    ffn_sum = lax.psum_scatter(ffn_y, RING_Z)
     grad_query, grad_kv, grad_one, gain_cross_grad = cross_backward(
         hidden_one, gain_cross_all, grad_two, cross_w, query, key, value, cross_p
     )
+    rings = ("z", "y", "x")
     mine, other = cross_grads(
         rings, pos, hidden_one, gain_cross_all, grad_two, memory_turned, cross_mixed,
         grad_query, grad_kv,
     )
-    cross_sum = ring_sum(mine, other, rings)
-    grad_proj, outgoing = self_backward(
-        slot, embedded, gain_self_all, grad_one, self_w, self_proj, self_p,
+    other = swap_cores(other)
+    half, half_other, outgoing = self_backward(
+        pos, slot, kept, gain_self_all, then(grad_one, mine), self_w, self_proj, self_p,
         gain_cross_grad, gain_ffn_grad,
     )
-    mine, other = self_grads(
-        pos, embedded, gain_self_all, grad_one, self_mixed, grad_proj
-    )
-    self_sum = lax.all_to_all(add_low(mine, swap_cores(other)), CHIPS, 0, 0, tiled=True)
-    self_sum = jnp.sum(self_sum.astype(jnp.float32), axis=0)
+    cross_start = ring_sum_start(then(mine, half), other)
+    outgoing = then(outgoing, cross_start).reshape(owner_count, SLOTS, model_width + 128)
+    incoming = lax.all_to_all(outgoing, AXES, split_axis=0, concat_axis=0, tiled=True)
+    self_rings = ("x", "z", "y")
+    self_low, self_high = self_grads(
+        self_rings, pos, then(gain_self_all, outgoing), kept, kept_other, half,
+        swap_cores(half_other),
+    )
+    cross_low, cross_high = cross_start
+    cross_terms = ring_first(then(cross_low, self_low), cross_high, rings[0])
     memory_grad = jnp.einsum(
-        "me,de->md", grad_kv[:MEM], cross_w[:, 768:2304], preferred_element_type=jnp.float32
+        "me,de->md", then(grad_kv, cross_terms[2], ffn_x)[:MEM], cross_w[:, 768:2304],
+        preferred_element_type=jnp.float32,
     )[None]
-
-    outgoing = outgoing.reshape(owner_count, SLOTS, model_width + 128)
-    incoming = lax.all_to_all(outgoing, AXES, split_axis=0, concat_axis=0, tiled=True)
-    incoming = incoming.reshape(owner_count * SLOTS, model_width + 128)
+    self_terms = ring_first(then(self_low, memory_grad, incoming), self_high, self_rings[0])
+    cross_terms = ring_second(cross_terms, rings[0])
+    cross_low, cross_high = ring_halves((then(cross_terms[0], self_terms[2]), *cross_terms[1:]))
+    self_terms = ring_second(self_terms, self_rings[0])
+    self_low, self_high = ring_halves((then(self_terms[0], cross_low), *self_terms[1:]))
+    cross_terms = ring_first(then(cross_low, self_low), cross_high, rings[1])
+    incoming = then(incoming, cross_terms[2]).reshape(
+        owner_count * SLOTS, model_width + 128
+    )
     gain_sums = jnp.sum(incoming[:, model_width : model_width + GAINS].astype(jnp.float32), axis=0)
     table_grad = jnp.einsum(
         "sr,sd->rd", row_hits, incoming[:, :model_width], preferred_element_type=jnp.float32
     )
+    cross_terms = ring_second(cross_terms, rings[1])
+    cross_low, cross_high = ring_halves((then(cross_terms[0], ffn_y), *cross_terms[1:]))
+    self_terms = ring_first(self_low, self_high, self_rings[1])
+    self_low, self_high = ring_halves(ring_second(self_terms, self_rings[1]))
+    cross_sum = ring_total(cross_low, cross_high, rings[2])
+    self_sum = ring_total(then(self_low, ffn_sum), self_high, self_rings[2])
 
     sums = jnp.concatenate([self_sum, cross_sum, ffn_sum[:, :512].astype(jnp.float32)], axis=1)
     sums = lax.all_to_all(sums.reshape(8, 6, -1), EIGHT, 0, 0, tiled=True)

time: 335 us -> 320 us (0.955)
  waiting for transfers between devices: 110 us -> 96.4 us
  starting transfers between devices: 40.5 us -> 33.5 us
    ppermute x6 -> x12, waiting for transfers between devices: 37.4 us -> 11.8 us  [ring_pair(): return lax.ppermute(v, ring + ('c',), perm)]
    all_to_all x1, waiting for transfers between devices: 0.01 us -> 12.7 us  [body(): lax.all_to_all(outgoing, AXES, split_axis=0, concat_axis=0, tiled=True)]
    all_to_all x1 -> x0, starting transfers between devices: 10.7 us -> none  [body(): lax.all_to_all(add_low(mine, swap_cores(other)), CHIPS, 0, 0, tiled=True)]
    ppermute x6 -> x12, starting transfers between devices: 8.9 us -> 14.3 us  [ring_pair(): return lax.ppermute(v, ring + ('c',), perm)]
    convert_element_type x7 -> x11, other arithmetic: 8.89 us -> 11.7 us  [add_low(): return sum((t.astype(jnp.float32) for t in terms)).astype(jnp.bfloat16)]
  transfers between devices with their start and end apart: 17 -> 23, of which waited for: 10 -> 11; matrix products, arithmetic and copies ran while one was open for 13% -> 15% of each run, Pallas kernels for 13% -> 14%
where the time goes in v1:
time: 320 us; the launch traced here: 314 us
  waiting for transfers between devices  96.4 us (30%)
  Pallas kernels  91.5 us (29%)
  starting transfers between devices  33.5 us (10%)
  local copies, waits for them, and re-layouts  22.8 us (7%)
  other arithmetic  19.9 us (6%)
  blocking collectives  19.6 us (6%)
  between operations  15.9 us (5%)
  matrix products  14.4 us (4%)
    all_gather x1, waiting for transfers between devices, all_weights(): return lax.all_gather(piece, TORUS).reshape(4, 4, 4, 2, BLOCK, -1)  37.9 us
    pallas_call x1, Pallas kernels, cross_forward(): pl.pallas_call(cross_forward_kernel, grid=(PAIRS // CROSS_FORWARD,), in_s...  20.8 us
    all_to_all x1, blocking collectives, body(): lax.all_to_all(then(request, whole), AXES, split_axis=0, concat_axis=0, t...  19.6 us
    pallas_call x1, Pallas kernels, ffn_both(): pl.pallas_call(ffn_kernel, grid=(FF // 512,), in_specs=[SCALARS, full(TGT...  16.9 us
    pallas_call x1, Pallas kernels, cross_backward(): pl.pallas_call(cross_backward_kernel, grid=(PAIRS // CROSS_BACKWARD,), in...  16.6 us
    ppermute x12, starting transfers between devices, ring_pair(): return lax.ppermute(v, ring + ('c',), perm)  14.3 us
    all_to_all x1, waiting for transfers between devices, body(): lax.all_to_all(outgoing, AXES, split_axis=0, concat_axis=0, tiled=True)  12.7 us
    ppermute x12, waiting for transfers between devices, ring_pair(): return lax.ppermute(v, ring + ('c',), perm)  11.8 us
  transfers between devices with their start and end apart: 23, of which 11 were waited for; matrix products, arithmetic and copies ran while one was open for 15% of the time, Pallas kernels for 14%

profile of v1, /device:TPU:0, one launch (start us, length us, event | category | flops | bytes accessed | tf_op | source)
XLA Modules:
  0.0 314.0 jit_solution(12784349877617403814)
XLA Ops:
  7.2 1.0 reshape_reshape.6
  8.2 0.8 pad_maximum_fusion.4
  9.0 0.8 pad_maximum_fusion.3
  9.8 0.7 pad_maximum_fusion.1
  10.5 4.3 %all-to-all-start = ((bf16[8,6,1280]{2,1,0:T(8,128)(2,1)}), bf16[8,6,1280]{2,1,0:T(8,128)(2,1)S(1)}, u32[]{:S(2)}, u32[]{:S(2)}) async-start(bf16[8,6,1280]{2,1,0:T(8,128)(2,1)} %pad_maximum_fusion.1), calls=%async_computation | async-start | bytes 327680 | tf_op jit(solution)/shard_map/all_to_all | solution.py:735
  14.9 0.8 reshape.327
  15.6 5.1 %all-to-all-done = bf16[8,6,1280]{2,1,0:T(8,128)(2,1)S(1)} async-done(((bf16[8,6,1280]{2,1,0:T(8,128)(2,1)}), bf16[8,6,1280]{2,1,0:T(8,128)(2,1)S(1)}, u32[]{:S(2)}, u32[]{:S(2)}) %all-to-all-start) | async-done | bytes 122912 | tf_op jit(solution)/shard_map/all_to_all | solution.py:735
  20.8 0.7 pad_maximum_fusion.2
  21.5 0.7 fusion.35
  22.2 0.7 broadcast_divide_fusion
  24.3 19.6 %all_to_all.32 = f32[128,1,32]{2,1,0:T(1,128)S(1)} all-to-all(f32[128,1,32]{2,1,0:T(1,128)S(1)} %bitcast.152), channel_id=1, replica_groups=mesh['x'=4,'yh'=2,'zh'=2,'zl'=2,'yl'=2,'c'=2] {'x','yh','zh','zl','yl','c'}, dimensions={0} | all-to-all | bytes 32768 | tf_op jit(solution)/shard_map/all_to_all | solution.py:786
  44.1 2.9 fusion.6
  46.9 2.4 reshape.324
  49.3 4.6 %all-to-all-start.2 = ((bf16[128,4,768]{2,1,0:T(4,128)(2,1)}), bf16[128,4,768]{2,1,0:T(4,128)(2,1)S(1)}, u32[]{:S(2)}, u32[]{:S(2)}) async-start(bf16[128,4,768]{2,1,0:T(4,128)(2,1)} %reshape.324), calls=%async_computation.2 | async-start | bytes 1572864 | tf_op jit(solution)/shard_map/all_to_all | solution.py:794
  54.4 3.2 %copy.87 = bf16[1,1056,768]{1,2,0:T(8,128)(2,1)S(1)} copy(bf16[1,1056,768]{2,1,0:T(8,128)(2,1)} %param.19) | data formatting | bytes 3244032 | tf_op args[4]
  58.9 1.4 pad.4.early_ref.mem_t_ref
  60.4 0.7 fusion.27.slot_ref
  61.1 0.7 reshape.326.gain_ref
  61.9 0.7 reshape.330.gain_ref
  62.6 0.7 reshape.331.gain_ref
  63.3 10.7 %all-to-all-done.2 = bf16[128,4,768]{2,1,0:T(4,128)(2,1)S(1)} async-done(((bf16[128,4,768]{2,1,0:T(4,128)(2,1)}), bf16[128,4,768]{2,1,0:T(4,128)(2,1)S(1)}, u32[]{:S(2)}, u32[]{:S(2)}) %all-to-all-start.2) | async-done | bytes 786464 | tf_op jit(solution)/shard_map/all_to_all | solution.py:794
  74.0 1.1 reshape.325.rows_ref
  75.1 37.9 %all-gather.3.cloned.1.call-done = bf16[6144,1536]{1,0:T(8,128)(2,1)} async-done(((bf16[48,1536]{1,0:T(8,128)(2,1)}), bf16[6144,1536]{1,0:T(8,128)(2,1)}) %all-gather.3.cloned.1.call-update) | async-done | bytes 18874384 | tf_op jit(solution)/shard_map/all_gather | solution.py:741
  113.0 9.5 %self_forward.1 = (bf16[256,1536]{1,0:T(8,128)(2,1)}, bf16[256,2304]{1,0:T(8,128)(2,1)}, bf16[6,512,256]{2,1,0:T(8,128)(2,1)}, f32[256,768]{1,0:T(8,128)}, bf16[768,3072]{1,0:T(8,128)(2,1)}) custom-call(bf16[512,768]{1,0:T(8,128)(2,1)} %reshape.325.rows_ref, s32[256,1]{1,0:T(8,128)} %fusion.27.slot_ref, f32[1,768]{1,0:T(1,128)} %reshape.326.gain_ref, ...), custom_call_target="tpu_custom_call" | custom-call | flops 8000000000 | bytes 12000000 | tf_op jit(solution)/shard_map/self_forward/pallas_call | solution.py:301
  122.5 20.8 %cross_forward.1 = (bf16[256,768]{1,0:T(8,128)(2,1)}, bf16[1152,768]{1,0:T(8,128)(2,1)}, bf16[1152,768]{1,0:T(8,128)(2,1)}, bf16[6,512,1152]{2,1,0:T(8,128)(2,1)...) custom-call(s32[1]{0:T(128)S(6)} %copy.99.len_ref, ...), custom_call_target="tpu_custom_call" | custom-call | flops 20000000000 | bytes 20000000 | tf_op jit(solution)/shard_map/cross_forward/pallas_call | solution.py:360
  143.3 16.9 %ffn_both.1 = (f32[256,768]{1,0:T(8,128)}, f32[256,768]{1,0:T(8,128)}, f32[1,768]{1,0:T(1,128)}, bf16[4,2,4,4,48,768]{5,4,3,2,1,0:T(8,128)(2,1)}) custom-call(s32[1]{0:T(128)S(6)} %copy.98.len_ref, f32[256,768]{1,0:T(8,128)} %get-tuple-element.55.h2_ref, f32[1,768]{1,0:T(1,128)} %reshape.331.gain_ref, bf16[256,768]{1,0:T(8,128)(2,1)} %bitcast.175, ...), custom_call_target="tpu_custom_call" | custom-call | flops 15000000512 | bytes 25000000 | tf_op jit(solution)/shard_map/ffn_both/pallas_call | solution.py:485
  160.8 16.6 %cross_backward.1 = (bf16[256,768]{1,0:T(8,128)(2,1)}, bf16[1152,1536]{1,0:T(8,128)(2,1)}, f32[256,768]{1,0:T(8,128)}, f32[1,768]{1,0:T(1,128)}) custom-call(f32[256,768]{1,0:T(8,128)} %get-tuple-element.54.h1_ref, f32[1,768]{1,0:T(1,128)} %reshape.330.gain_ref, f32[256,768]{1,0:T(8,128)} %get-tuple-element.57.g2_ref, ...), custom_call_target="tpu_custom_call" | custom-call | flops 16000000000 | bytes 20000000 | tf_op jit(solution)/shard_map/cross_backward/pallas_call | solution.py:541
  177.5 10.7 %cross_grads.1 = (bf16[4,4,4,48,384]{4,3,2,1,0:T(8,128)(2,1)}, bf16[4,4,4,48,384]{4,3,2,1,0:T(8,128)(2,1)}) custom-call(s32[4]{0:T(128)} %pad_add_fusion.pos_ref, f32[256,768]{1,0:T(8,128)} %get-tuple-element.54.h1_ref, f32[1,768]{1,0:T(1,128)} %reshape.330.gain_ref, f32[256,768]{1,0:T(8,128)} %get-tuple-element.57.g2_ref, ...), custom_call_target="tpu_custom_call" | custom-call | flops 6000000000 | bytes 12000000 | tf_op jit(solution)/shard_map/cross_grads/pallas_call | solution.py:588
  188.8 11.7 %self_backward.1 = (bf16[256,1536]{1,0:T(8,128)(2,1)}, bf16[256,1536]{1,0:T(8,128)(2,1)}, bf16[512,896]{1,0:T(8,128)(2,1)}) custom-call(s32[4]{0:T(128)} %pad_add_fusion.pos_ref, s32[256,1]{1,0:T(8,128)} %fusion.27.slot_ref, bf16[256,1536]{1,0:T(8,128)(2,1)} %get-tuple-element.67.kept_ref, f32[1,768]{1,0:T(1,128)} %reshape.326.gain_ref, ...), custom_call_target="tpu_custom_call" | custom-call | flops 8000000000 | bytes 10000000 | tf_op jit(solution)/shard_map/self_backward/pallas_call | solution.py:648
  200.9 1.7 add_convert_fusion.1
  202.6 2.6 collective-permute-start.3
  205.2 1.1 reshape.332
  206.4 5.2 %self_grads.1 = (bf16[2,4,4,48,384]{4,3,2,1,0:T(8,128)(2,1)}, bf16[2,4,4,48,384]{4,3,2,1,0:T(8,128)(2,1)}) custom-call(s32[4]{0:T(128)} %pad_add_fusion.pos_ref, f32[1,768]{1,0:T(1,128)} %reshape.326.gain_ref, bf16[256,1536]{1,0:T(8,128)(2,1)} %get-tuple-element.67.kept_ref, bf16[256,1536]{1,0:T(8,128)(2,1)} %collective-permute-done.1.kept_other_ref, ...), custom_call_target="tpu_custom_call" | custom-call | flops 3000000000 | bytes 8000000 | tf_op jit(solution)/shard_map/self_grads/pallas_call | solution.py:709
  211.6 2.5 collective-permute-start.4
  214.1 5.7 %all-to-all-start.3 = ((bf16[128,4,896]{2,1,0:T(4,128)(2,1)}), bf16[128,4,896]{2,1,0:T(4,128)(2,1)S(1)}, u32[]{:S(2)}, u32[]{:S(2)}) async-start(bf16[128,4,896]{2,1,0:T(4,128)(2,1)} %reshape.332), calls=%async_computation.4 | async-start | bytes 1835008 | tf_op jit(solution)/shard_map/all_to_all | solution.py:829
  220.5 2.0 fusion.8
  223.1 7.1 %convolution_bitcast_fusion = f32[1,1056,768]{2,1,0:T(8,128)} fusion(bf16[1152,1536]{1,0:T(8,128)(2,1)} %get-tuple-element.85.dkv_ref, bf16[768,3072]{1,0:T(8,128)(2,1)} %get-tuple-element.58.w_ref), kind=kOutput, calls=%fused_computation.3 | convolution fusion | flops 2491416576 | bytes 8847360 | tf_op jit(solution)/shard_map/me,de->md/dot_general | solution.py:837
  230.2 12.7 %all-to-all-done.3 = bf16[128,4,896]{2,1,0:T(4,128)(2,1)S(1)} async-done(((bf16[128,4,896]{2,1,0:T(4,128)(2,1)}), bf16[128,4,896]{2,1,0:T(4,128)(2,1)S(1)}, u32[]{:S(2)}, u32[]{:S(2)}) %all-to-all-start.3) | async-done | bytes 917536 | tf_op jit(solution)/shard_map/all_to_all | solution.py:829
  242.9 1.5 fusion.9
  245.0 1.5 fusion.17
  246.5 2.1 collective-permute-start.7
  248.7 5.7 %collective-permute-done.6 = bf16[4,4,48,384]{3,2,1,0:T(8,128)(2,1)S(1)} collective-permute-done((bf16[4,4,48,384]{3,2,1,0:T(8,128)(2,1)S(1)}, bf16[4,4,48,384]{3,2,1,0:T(8,128)(2,1)S(1)}, u32[]{:S(2)}, u32[]{:S(2)}) %collective-permute-start.6) | collective-permute-done | bytes 589856 | tf_op jit(solution)/shard_map/ppermute | solution.py:43
  254.4 1.3 fusion.11
  255.7 1.2 collective-permute-start.8
  257.5 0.7 collective-permute-start.12
  258.6 4.5 %fusion = f32[1954,768]{1,0:T(8,128)} fusion(s32[512]{0:T(512)S(1)} %sub.34, bf16[512,896]{1,0:T(8,128)(2,1)S(1)} %reshape.334), kind=kOutput, calls=%fused_computation.1 | convolution fusion | flops 1537688576 | bytes 6791168 | tf_op jit(solution)/shard_map/sr,sd->rd/dot_general | solution.py:851
  263.7 1.0 fusion.23
  264.6 1.0 collective-permute-start.13
  265.6 0.7 copy-done.5
  266.6 3.7 %collective-permute-done.13 = bf16[2,48,384]{2,1,0:T(8,128)(2,1)S(1)} collective-permute-done((bf16[2,48,384]{2,1,0:T(8,128)(2,1)S(1)}, bf16[2,48,384]{2,1,0:T(8,128)(2,1)S(1)}, u32[]{:S(2)}, u32[]{:S(2)}) %collective-permute-start.13) | collective-permute-done | bytes 73760 | tf_op jit(solution)/shard_map/ppermute | solution.py:43
  270.9 0.9 fusion.34
  272.0 1.7 fusion.25
  273.7 1.4 collective-permute-start.10
  275.0 0.8 collective-permute-done.14
  275.9 0.8 bitcast_add_fusion.2
  276.7 11.2 %reduce-scatter.8.cloned.1.call-done = bf16[1,48,768]{2,1,0:T(8,128)(2,1)} async-done(((bf16[4,48,768]{2,1,0:T(8,128)(2,1)}), bf16[1,48,768]{2,1,0:T(8,128)(2,1)}) %reduce-scatter.8.cloned.1.call-update) | async-done | bytes 73744 | tf_op jit(solution)/shard_map/reduce_scatter | solution.py:813
  287.9 1.6 collective-permute-start.11
  289.5 0.8 slice_convert_fusion.1
  290.3 0.7 slice.347
  291.0 0.9 collective-permute-done.11
  292.0 0.8 reshape.335
  292.7 3.4 %all-to-all-start.4 = ((f32[8,6,1280]{2,1,0:T(8,128)}), f32[8,6,1280]{2,1,0:T(8,128)S(1)}, u32[]{:S(2)}, u32[]{:S(2)}) async-start(f32[8,6,1280]{2,1,0:T(8,128)} %reshape.335), calls=%async_computation.7 | async-start | bytes 655360 | tf_op jit(solution)/shard_map/all_to_all | solution.py:862
  296.8 6.9 %all-to-all-done.4 = f32[8,6,1280]{2,1,0:T(8,128)S(1)} async-done(((f32[8,6,1280]{2,1,0:T(8,128)}), f32[8,6,1280]{2,1,0:T(8,128)S(1)}, u32[]{:S(2)}, u32[]{:S(2)}) %all-to-all-start.4) | async-done | bytes 245792 | tf_op jit(solution)/shard_map/all_to_all | solution.py:862
  306.3 0.7 reshape_reshape.7
  (108 shorter events, 11.5 us)
Async XLA Ops:
  7.2 36.9 %copy-start = (bf16[1954,768]{1,0:T(8,128)(2,1)S(1)}, bf16[1954,768]{1,0:T(8,128)(2,1)}, u32[]{:S(2)}) copy-start(bf16[1954,768]{1,0:T(8,128)(2,1)} %param.18) | copy-start | bytes 9004036
  7.2 16.1 %copy-start.9 = (s32[1,256]{1,0:T(1,128)S(1)}, s32[1,256]{1,0:T(1,128)}, u32[]{:S(2)}) copy-start(s32[1,256]{1,0:T(1,128)} %param.15) | copy-start | bytes 3076
  7.2 16.7 %copy-start.12 = (bf16[6]{0:T(256)(128)(2,1)S(1)}, bf16[6]{0:T(256)(128)(2,1)}, u32[]{:S(2)}) copy-start(bf16[6]{0:T(256)(128)(2,1)} %param.22) | copy-start | bytes 40
  7.2 16.6 %copy-start.11 = (bf16[6]{0:T(256)(128)(2,1)S(1)}, bf16[6]{0:T(256)(128)(2,1)}, u32[]{:S(2)}) copy-start(bf16[6]{0:T(256)(128)(2,1)} %param.25) | copy-start | bytes 40
  7.2 16.6 %copy-start.10 = (bf16[6]{0:T(256)(128)(2,1)S(1)}, bf16[6]{0:T(256)(128)(2,1)}, u32[]{:S(2)}) copy-start(bf16[6]{0:T(256)(128)(2,1)} %param.28) | copy-start | bytes 40
  10.5 10.2 %all-to-all-start = ((bf16[8,6,1280]{2,1,0:T(8,128)(2,1)}), bf16[8,6,1280]{2,1,0:T(8,128)(2,1)S(1)}, u32[]{:S(2)}, u32[]{:S(2)}) async-start(bf16[8,6,1280]{2,1,0:T(8,128)(2,1)} %pad_maximum_fusion.1), calls=%async_computation | async-start | bytes 327680 | tf_op jit(solution)/shard_map/all_to_all | solution.py:735
  14.8 98.2 %all-gather.3.cloned.1.call-start = ((), (), s32[]{:S(2)}) async-start(), calls=%async_computation.11 | async-start | bytes 19021824 | tf_op jit(solution)/shard_map/all_gather | solution.py:741
  49.3 24.8 %all-to-all-start.2 = ((bf16[128,4,768]{2,1,0:T(4,128)(2,1)}), bf16[128,4,768]{2,1,0:T(4,128)(2,1)S(1)}, u32[]{:S(2)}, u32[]{:S(2)}) async-start(bf16[128,4,768]{2,1,0:T(4,128)(2,1)} %reshape.324), calls=%async_computation.2 | async-start | bytes 1572864 | tf_op jit(solution)/shard_map/all_to_all | solution.py:794
  53.9 169.1 %reduce-scatter.4.cloned.1.call-start = ((), (), s32[]{:S(2)}) async-start(), calls=%async_computation.8 | async-start | bytes 10616832 | tf_op jit(solution)/shard_map/reduce_scatter | solution.py:811
  177.5 11.1 %copy-start.13 = (bf16[256,1536]{1,0:T(8,128)(2,1)S(1)}, bf16[256,1536]{1,0:T(8,128)(2,1)}, u32[]{:S(2)}) copy-start(bf16[256,1536]{1,0:T(8,128)(2,1)} %get-tuple-element.67.kept_ref) | copy-start | bytes 2359300
  188.2 12.6 %collective-permute-start = (bf16[4,4,4,48,384]{4,3,2,1,0:T(8,128)(2,1)}, bf16[4,4,4,48,384]{4,3,2,1,0:T(8,128)(2,1)S(1)}, u32[]{:S(2)}, u32[]{:S(2)}) collective-permute-start(bf16[4,4,4,48,384]{4,3,2,1,0:T(8,128)(2,1)} %get-tuple-element.77), channel_id=1, source_target_pairs={{0,1},{1,0},{2,3},{3,2},{4,5},{5,4},{6,7},{7,6},{8,9},{9,8},{10,11... | collective-permute-start | bytes 7077896 | tf_op jit(solution)/shard_map/ppermute | solution.py:47
  188.6 17.8 %collective-permute-start.1 = (bf16[256,1536]{1,0:T(8,128)(2,1)S(1)}, bf16[256,1536]{1,0:T(8,128)(2,1)}, u32[]{:S(2)}, u32[]{:S(2)}) collective-permute-start(bf16[256,1536]{1,0:T(8,128)(2,1)S(1)} %copy-done.13), channel_id=1, source_target_pairs={{0,1},{1,0},{2,3},{3,2},{4,5},{5,4},{6,7},{7,6},{8,9},{9,8},{10,11... | collective-permute-start | bytes 2359304 | tf_op jit(solution)/shard_map/ppermute | solution.py:47
  188.8 12.1 %copy-start.2 = (bf16[4,4,4,48,384]{4,3,2,1,0:T(8,128)(2,1)S(1)}, bf16[4,4,4,48,384]{4,3,2,1,0:T(8,128)(2,1)}, u32[]{:S(2)}) copy-start(bf16[4,4,4,48,384]{4,3,2,1,0:T(8,128)(2,1)} %get-tuple-element.76) | copy-start | bytes 7077892
  200.5 4.7 %copy-start.4 = (bf16[512,896]{1,0:T(8,128)(2,1)S(1)}, bf16[512,896]{1,0:T(8,128)(2,1)}, u32[]{:S(2)}) copy-start(bf16[512,896]{1,0:T(8,128)(2,1)} %get-tuple-element.79) | copy-start | bytes 2752516
  200.5 5.8 %collective-permute-start.2 = (bf16[256,1536]{1,0:T(8,128)(2,1)}, bf16[256,1536]{1,0:T(8,128)(2,1)}, u32[]{:S(2)}, u32[]{:S(2)}) collective-permute-start(bf16[256,1536]{1,0:T(8,128)(2,1)} %get-tuple-element.81), channel_id=1, source_target_pairs={{0,1},{1,0},{2,3},{3,2},{4,5},{5,4},{6,7},{7,6},{8,9},{9,8},{10,11... | collective-permute-start | bytes 2359304 | tf_op jit(solution)/shard_map/ppermute | solution.py:47
  202.6 18.0 %collective-permute-start.3 = (bf16[2,4,4,48,384]{4,3,2,1,0:T(8,128)(2,1)}, bf16[2,4,4,48,384]{4,3,2,1,0:T(8,128)(2,1)}, u32[]{:S(2)}, u32[]{:S(2)}) collective-permute-start(bf16[2,4,4,48,384]{4,3,2,1,0:T(8,128)(2,1)} %get-tuple-element.99), channel_id=1, source_target_pairs={{0,12},{1,5},{4,8},{5,1},{8,4},{9,13},{12,0},{13,9},{2,14},{3,7},{... | collective-permute-start | bytes 3538952 | tf_op jit(solution)/shard_map/ppermute | solution.py:43
  211.6 31.3 %collective-permute-start.4 = (bf16[2,4,4,48,384]{4,3,2,1,0:T(8,128)(2,1)}, bf16[2,4,4,48,384]{4,3,2,1,0:T(8,128)(2,1)}, u32[]{:S(2)}, u32[]{:S(2)}) collective-permute-start(bf16[2,4,4,48,384]{4,3,2,1,0:T(8,128)(2,1)} %get-tuple-element.87), channel_id=1, source_target_pairs={{0,96},{1,33},{32,64},{33,1},{64,32},{65,97},{96,0},{97,65},{2,98}... | collective-permute-start | bytes 3538952 | tf_op jit(solution)/shard_map/ppermute | solution.py:43
  214.1 28.8 %all-to-all-start.3 = ((bf16[128,4,896]{2,1,0:T(4,128)(2,1)}), bf16[128,4,896]{2,1,0:T(4,128)(2,1)S(1)}, u32[]{:S(2)}, u32[]{:S(2)}) async-start(bf16[128,4,896]{2,1,0:T(4,128)(2,1)} %reshape.332), calls=%async_computation.4 | async-start | bytes 1835008 | tf_op jit(solution)/shard_map/all_to_all | solution.py:829
  219.9 43.8 %reduce-scatter.6.cloned.1.call-start = ((), (), s32[]{:S(2)}) async-start(), calls=%async_computation.9 | async-start | bytes 1474560 | tf_op jit(solution)/shard_map/reduce_scatter | solution.py:812
  222.6 22.5 %collective-permute-start.5 = (bf16[4,4,48,384]{3,2,1,0:T(8,128)(2,1)}, bf16[4,4,48,384]{3,2,1,0:T(8,128)(2,1)}, u32[]{:S(2)}, u32[]{:S(2)}) collective-permute-start(bf16[4,4,48,384]{3,2,1,0:T(8,128)(2,1)} %fusion.8), channel_id=1, source_target_pairs={{0,4},{1,13},{4,0},{5,9},{8,12},{9,5},{12,8},{13,1},{2,6},{3,15},{... | collective-permute-start | bytes 1769480 | tf_op jit(solution)/shard_map/ppermute | solution.py:43
  223.1 64.8 %reduce-scatter.8.cloned.1.call-start = ((), (), s32[]{:S(2)}) async-start(), calls=%async_computation.10 | async-start | bytes 368640 | tf_op jit(solution)/shard_map/reduce_scatter | solution.py:813
  242.9 5.7 %copy-start.3 = (bf16[2,4,4,48,384]{4,3,2,1,0:T(8,128)(2,1)S(1)}, bf16[2,4,4,48,384]{4,3,2,1,0:T(8,128)(2,1)}, u32[]{:S(2)}) copy-start(bf16[2,4,4,48,384]{4,3,2,1,0:T(8,128)(2,1)} %get-tuple-element.86) | copy-start | bytes 3538948
  244.4 10.0 %collective-permute-start.6 = (bf16[4,4,48,384]{3,2,1,0:T(8,128)(2,1)S(1)}, bf16[4,4,48,384]{3,2,1,0:T(8,128)(2,1)S(1)}, u32[]{:S(2)}, u32[]{:S(2)}) collective-permute-start(bf16[4,4,48,384]{3,2,1,0:T(8,128)(2,1)S(1)} %fusion.9), channel_id=1, source_target_pairs={{0,32},{1,97},{32,0},{33,65},{64,96},{65,33},{96,64},{97,1},{2,34}... | collective-permute-start | bytes 1769480 | tf_op jit(solution)/shard_map/ppermute | solution.py:43
  246.5 10.3 %collective-permute-start.7 = (bf16[2,4,48,384]{3,2,1,0:T(8,128)(2,1)S(1)}, bf16[2,4,48,384]{3,2,1,0:T(8,128)(2,1)S(1)}, u32[]{:S(2)}, u32[]{:S(2)}) collective-permute-start(bf16[2,4,48,384]{3,2,1,0:T(8,128)(2,1)S(1)} %get-tuple-element.103), channel_id=1, source_target_pairs={{0,18},{1,3},{2,16},{3,1},{16,2},{17,19},{18,0},{19,17},{4,22},{5,... | collective-permute-start | bytes 884744 | tf_op jit(solution)/shard_map/ppermute | solution.py:43
  255.7 10.0 %collective-permute-start.8 = (bf16[2,4,48,384]{3,2,1,0:T(8,128)(2,1)S(1)}, bf16[2,4,48,384]{3,2,1,0:T(8,128)(2,1)S(1)}, u32[]{:S(2)}, u32[]{:S(2)}) collective-permute-start(bf16[2,4,48,384]{3,2,1,0:T(8,128)(2,1)S(1)} %get-tuple-element.100), channel_id=1, source_target_pairs={{0,12},{1,5},{4,8},{5,1},{8,4},{9,13},{12,0},{13,9},{2,14},{3,7},{... | collective-permute-start | bytes 884744 | tf_op jit(solution)/shard_map/ppermute | solution.py:43
  256.8 0.7 copy-start.6
  257.5 6.1 %collective-permute-start.12 = (bf16[4,48,384]{2,1,0:T(8,128)(2,1)S(1)}, bf16[4,48,384]{2,1,0:T(8,128)(2,1)}, u32[]{:S(2)}, u32[]{:S(2)}) collective-permute-start(bf16[4,48,384]{2,1,0:T(8,128)(2,1)S(1)} %fusion.18), channel_id=1, source_target_pairs={{0,2},{1,19},{2,0},{3,17},{16,18},{17,3},{18,16},{19,1},{4,6},{5,2... | collective-permute-start | bytes 442376 | tf_op jit(solution)/shard_map/ppermute | solution.py:43
  258.5 5.1 %copy-start.7 = (bf16[2,4,48,384]{3,2,1,0:T(8,128)(2,1)S(1)}, bf16[2,4,48,384]{3,2,1,0:T(8,128)(2,1)}, u32[]{:S(2)}) copy-start(bf16[2,4,48,384]{3,2,1,0:T(8,128)(2,1)} %copy-done.6) | copy-start | bytes 884740
  264.6 5.6 %collective-permute-start.13 = (bf16[2,48,384]{2,1,0:T(8,128)(2,1)S(1)}, bf16[2,48,384]{2,1,0:T(8,128)(2,1)S(1)}, u32[]{:S(2)}, u32[]{:S(2)}) collective-permute-start(bf16[2,48,384]{2,1,0:T(8,128)(2,1)S(1)} %get-tuple-element.107), channel_id=1, source_target_pairs={{0,96},{1,33},{32,64},{33,1},{64,32},{65,97},{96,0},{97,65},{2,98}... | collective-permute-start | bytes 221192 | tf_op jit(solution)/shard_map/ppermute | solution.py:43
  265.6 0.7 copy-start.5
  266.4 5.6 %collective-permute-start.9 = (bf16[4,48,384]{2,1,0:T(8,128)(2,1)S(1)}, bf16[4,48,384]{2,1,0:T(8,128)(2,1)}, u32[]{:S(2)}, u32[]{:S(2)}) collective-permute-start(bf16[4,48,384]{2,1,0:T(8,128)(2,1)S(1)} %fusion.19), channel_id=1, source_target_pairs={{0,4},{1,13},{4,0},{5,9},{8,12},{9,5},{12,8},{13,1},{2,6},{3,15},{... | collective-permute-start | bytes 442376 | tf_op jit(solution)/shard_map/ppermute | solution.py:43
  270.3 0.6 copy-start.8
  270.9 36.1 %copy-start.1 = (bf16[1954,768]{1,0:T(8,128)(2,1)S(1)}, bf16[1954,768]{1,0:T(8,128)(2,1)}, u32[]{:S(2)}) copy-start(bf16[1954,768]{1,0:T(8,128)(2,1)} %param.18) | copy-start | bytes 9004036
  271.9 4.0 %collective-permute-start.14 = (bf16[48,384]{1,0:T(8,128)(2,1)S(1)}, bf16[48,384]{1,0:T(8,128)(2,1)S(1)}, u32[]{:S(2)}, u32[]{:S(2)}) collective-permute-start(bf16[48,384]{1,0:T(8,128)(2,1)S(1)} %fusion.34), channel_id=1, source_target_pairs={{0,32},{1,97},{32,0},{33,65},{64,96},{65,33},{96,64},{97,1},{2,34}... | collective-permute-start | bytes 110600 | tf_op jit(solution)/shard_map/ppermute | solution.py:43
  273.7 14.2 %collective-permute-start.10 = (bf16[2,48,384]{2,1,0:T(8,128)(2,1)}, bf16[2,48,384]{2,1,0:T(8,128)(2,1)S(1)}, u32[]{:S(2)}, u32[]{:S(2)}) collective-permute-start(bf16[2,48,384]{2,1,0:T(8,128)(2,1)} %get-tuple-element.105), channel_id=1, source_target_pairs={{0,18},{1,3},{2,16},{3,1},{16,2},{17,19},{18,0},{19,17},{4,22},{5,... | collective-permute-start | bytes 221192 | tf_op jit(solution)/shard_map/ppermute | solution.py:43
  287.9 4.0 %collective-permute-start.11 = (bf16[48,384]{1,0:T(8,128)(2,1)S(1)}, bf16[48,384]{1,0:T(8,128)(2,1)S(1)}, u32[]{:S(2)}, u32[]{:S(2)}) collective-permute-start(bf16[48,384]{1,0:T(8,128)(2,1)S(1)} %fusion.33), channel_id=1, source_target_pairs={{0,2},{1,19},{2,0},{3,17},{16,18},{17,3},{18,16},{19,1},{4,6},{5,2... | collective-permute-start | bytes 110600 | tf_op jit(solution)/shard_map/ppermute | solution.py:43
  292.7 11.0 %all-to-all-start.4 = ((f32[8,6,1280]{2,1,0:T(8,128)}), f32[8,6,1280]{2,1,0:T(8,128)S(1)}, u32[]{:S(2)}, u32[]{:S(2)}) async-start(f32[8,6,1280]{2,1,0:T(8,128)} %reshape.335), calls=%async_computation.7 | async-start | bytes 655360 | tf_op jit(solution)/shard_map/all_to_all | solution.py:862
Sparse Core Ops, SparseCore 0:
  21.6 91.4 all-gather.2
  160.3 56.8 reduce-scatter.3
  223.2 28.6 reduce-scatter.5
  266.7 21.1 reduce-scatter.7

commit v2 on v1

--- a/solution.py
+++ b/solution.py
@@ -132,12 +132,6 @@
     return (0, 1 + 2 * core, 3 - 2 * core, 2)
 
 
-def square_parts(width, group, member):
-    row = pl.multiple_of(group * BLOCK, 16)
-    column = pl.multiple_of(member * width, 128)
-    return [((slice(None), slice(None)), 0, (pl.ds(row, BLOCK), pl.ds(column, width)))]
-
-
 def torus():
     return [(x, y, z, c) for x in range(4) for y in range(4) for z in range(4) for c in range(2)]
 
@@ -146,14 +140,20 @@
     return x * 4 + (y // 2) * 2 + z // 2, (z % 2) * 4 + (y % 2) * 2 + c
 
 
-def start_place(blocks, first, out, sem):
-    for at in torus():
-        group, member = block_place(*at)
-        pltpu.make_async_copy(
-            blocks.at[at + (slice(None), pl.ds(first, 384))],
-            out.at[pl.ds(BLOCK * group, BLOCK), pl.ds(384 * member, 384)],
-            sem,
-        ).start()
+def start_place(blocks, first, out, sems):
+    for matrix in range(4):
+        for at in torus():
+            group, member = block_place(*at)
+            if member // 2 == matrix:
+                pltpu.make_async_copy(
+                    blocks.at[at + (slice(None), pl.ds(first, 384))],
+                    out.at[pl.ds(BLOCK * group, BLOCK), pl.ds(384 * member, 384)],
+                    sems.at[matrix],
+                ).start()
+
+
+def wait_matrix(out, matrix, sems):
+    wait_whole([out.at[:, pl.ds(D * matrix, D)]], sems.at[matrix])
 
 
 def ffn_copies(j, whole_in, whole_out, block_of):
@@ -172,56 +172,30 @@
     return found
 
 
-def start_split(pos_ref, rings, parts, wholes, outs, sem):
+def ring_place(me, to, core):
+    distance = me ^ to
+    straight = distance ^ (distance >> 1)
+    turned_round = ((straight & 1) << 1) | (straight >> 1)
+    return jnp.where(core == 0, straight, turned_round)
+
+
+def start_split(pos_ref, rings, matrix, column_of, whole, out_of, core, sem):
     me = my_place(pos_ref)
-    at = {}
-    for source in range(2):
-        core = pos_ref[3] ^ source
-        flips = partners(core)
-        for k3 in range(4):
-            at[rings[0]] = me[rings[0]] ^ flips[k3]
-            for k2 in range(4):
-                at[rings[1]] = me[rings[1]] ^ flips[k2]
-                for k1 in range(4):
-                    at[rings[2]] = me[rings[2]] ^ flips[k1]
-                    for dst, whole, src in parts(*group_member(at, core)):
-                        pltpu.make_async_copy(
-                            wholes[whole].at[src], outs[source].at[(k3, k2, k1) + dst], sem
-                        ).start()
+    for x, y, z, c in torus():
+        group, member = block_place(x, y, z, 0)
+        if c == 0 and member // 2 == matrix:
+            to = {"x": x, "y": y, "z": z}
+            places = [ring_place(me[ring], to[ring], core) for ring in rings]
+            pltpu.make_async_copy(
+                whole.at[pl.ds(BLOCK * group, BLOCK), pl.ds(column_of(matrix), 384)],
+                out_of(*places),
+                sem,
+            ).start()
 
 
 def wait_whole(refs, sem):
     for ref in refs:
         pltpu.make_async_copy(ref, ref, sem).wait()
-
-
-def start_split(pos_ref, rings, parts, wholes, outs, sem):
-    me = my_place(pos_ref)
-    at = {}
-    for source in range(2):
-        core = pos_ref[3] ^ source
-        flips = partners(core)
-        for k3 in range(4):
-            at[rings[0]] = me[rings[0]] ^ flips[k3]
-            for k2 in range(4):
-                at[rings[1]] = me[rings[1]] ^ flips[k2]
-                for k1 in range(4):
-                    at[rings[2]] = me[rings[2]] ^ flips[k1]
-                    for dst, whole, src in parts(*group_member(at, core)):
-                        pltpu.make_async_copy(
-                            wholes[whole].at[src], outs[source].at[(k3, k2, k1) + dst], sem
-                        ).start()
-
-
-def start_split_whole(pos_ref, whole, outs, sem):
-    for source in range(2):
-        core = pos_ref[3] ^ source
-        for group in range(16):
-            for q in range(4):
-                for dst, _, src in square_parts(384, group, 2 * q + core):
-                    pltpu.make_async_copy(
-                        whole.at[src], outs[source].at[(4 * group + q,) + dst], sem
-                    ).start()
 
 
 def softmax_low(scores, valid):
@@ -247,7 +221,7 @@
 
 
 def self_forward_kernel(rows_ref, slot_ref, gain_ref, early_ref, blocks, *refs):
-    kept_ref, qkv_ref, p_ref, h1_ref, w_ref, sem = refs
+    kept_ref, qkv_ref, p_out, h1_ref, w_out, p_ref, w_ref, sem, sent = refs
     emb_ref, mixed_ref = kept_ref.at[:, :D], kept_ref.at[:, D:]
     j = pl.program_id(0)
 
@@ -259,10 +233,12 @@
         hidden = mm(hits.astype(jnp.bfloat16), rows_ref[...])
         emb_ref[...] = hidden.astype(jnp.bfloat16)
         normed = (hidden * rms_scale(hidden) * gain_ref[...]).astype(jnp.bfloat16)
-        wait_whole([w_ref], sem)
         for k in range(3):
             at = pl.ds(768 * k, 768)
+            wait_matrix(w_ref, k, sem)
             qkv_ref[:, at] = mm(normed, w_ref[:, at]).astype(jnp.bfloat16)
+        wait_matrix(w_ref, 3, sem)
+        pltpu.make_async_copy(w_ref, w_out, sent).start()
 
     row = lax.broadcasted_iota(jnp.int32, (2 * TGT, TGT), 0) & (TGT - 1)
     causal = lax.broadcasted_iota(jnp.int32, (2 * TGT, TGT), 1) <= row
@@ -270,12 +246,14 @@
         queries = stacked_heads(qkv_ref[:, pair_columns(pair)]) * jnp.bfloat16(0.125)
         weights = softmax_low(mm_nt(queries, qkv_ref[:, pair_columns(pair, 768)]), causal)
         p_ref[s] = weights
+        pltpu.make_async_copy(p_ref.at[s], p_out.at[s], sent).start()
         mixed = mm(weights, qkv_ref[:, pair_columns(pair, 1536)])
         mixed_ref[:, pair_columns(pair)] = joined_heads(mixed).astype(jnp.bfloat16)
 
     @pl.when(j == PAIRS // SELF_FORWARD - 1)
     def _():
         h1_ref[...] = emb_ref[...].astype(jnp.float32) + mm(mixed_ref[...], w_ref[:, 2304:])
+        wait_whole([w_ref, p_ref], sent)
 
 
 def full(*shape):
@@ -305,9 +283,9 @@
         out_specs=[
             full(TGT, 2 * D),
             full(TGT, 3 * D),
-            pl.BlockSpec((SELF_FORWARD, 512, TGT), lambda j: (j, 0, 0)),
+            HBM,
             full(TGT, D),
-            full(D, 4 * D),
+            HBM,
         ],
         out_shape=[
             shaped(bf, TGT, 2 * D),
@@ -316,7 +294,12 @@
             shaped(f32, TGT, D),
             shaped(bf, D, 4 * D),
         ],
-        scratch_shapes=[pltpu.SemaphoreType.DMA],
+        scratch_shapes=[
+            pltpu.VMEM((PAIRS, 512, TGT), bf),
+            pltpu.VMEM((D, 4 * D), bf),
+            pltpu.SemaphoreType.DMA((4,)),
+            pltpu.SemaphoreType.DMA,
+        ],
         compiler_params=params(),
         cost_estimate=cost(8, 12),
         name="self_forward",
@@ -324,7 +307,8 @@
 
 
 def cross_forward_kernel(len_ref, h1_ref, gain_ref, mem_ref, blocks, *refs):
-    q_ref, k_ref, v_ref, p_ref, mixed_ref, h2_ref, w_ref, sem = refs
+    q_ref, k_out, v_out, p_out, mixed_ref, h2_ref, w_out = refs[:7]
+    k_ref, v_ref, p_ref, w_ref, sem, sent = refs[7:]
     j = pl.program_id(0)
 
     @pl.when(j == 0)
@@ -332,27 +316,33 @@
         start_place(blocks, 384, w_ref, sem)
         hidden = h1_ref[...]
         normed = (hidden * rms_scale(hidden) * gain_ref[...]).astype(jnp.bfloat16)
-        wait_whole([w_ref], sem)
+        wait_matrix(w_ref, 0, sem)
         q_ref[...] = mm(normed, w_ref[:, :768]).astype(jnp.bfloat16)
-        for out, offset in ((k_ref, 768), (v_ref, 1536)):
+        for out, sent_to, offset in ((k_ref, k_out, 768), (v_ref, v_out, 1536)):
+            wait_matrix(w_ref, offset // D, sem)
             for half in range(2):
                 at = pl.ds(384 * half, 384)
                 out[:MEM, at] = mm(mem_ref[...], w_ref[:, pl.ds(offset + 384 * half, 384)]).astype(
                     jnp.bfloat16
                 )
             out[MEM:, :] = jnp.zeros((KEYS - MEM, D), jnp.bfloat16)
+            pltpu.make_async_copy(out, sent_to, sent).start()
+        wait_matrix(w_ref, 3, sem)
+        pltpu.make_async_copy(w_ref, w_out, sent).start()
 
     reach = lax.broadcasted_iota(jnp.int32, (2 * TGT, KEYS), 1) < len_ref[0]
     for s, pair in pairs_here(CROSS_FORWARD):
         queries = stacked_heads(q_ref[:, pair_columns(pair)]) * jnp.bfloat16(0.125)
         weights = softmax_low(mm_nt(queries, k_ref[:, pair_columns(pair)]), reach)
         p_ref[s] = weights
+        pltpu.make_async_copy(p_ref.at[s], p_out.at[s], sent).start()
         mixed = mm(weights, v_ref[:, pair_columns(pair)])
         mixed_ref[:, pair_columns(pair)] = joined_heads(mixed).astype(jnp.bfloat16)
 
     @pl.when(j == PAIRS // CROSS_FORWARD - 1)
     def _():
         h2_ref[...] = h1_ref[...] + mm(mixed_ref[...], w_ref[:, 2304:])
+        wait_whole([w_ref, k_ref, v_ref, p_ref], sent)
 
 
 def cross_forward(mem_len, h1, gain, memory, blocks):
@@ -363,12 +353,12 @@
         in_specs=[SCALARS, full(TGT, D), full(1, D), full(MEM, D), HBM],
         out_specs=[
             full(TGT, D),
-            full(KEYS, D),
-            full(KEYS, D),
-            pl.BlockSpec((CROSS_FORWARD, 512, KEYS), lambda j: (j, 0, 0)),
+            HBM,
+            HBM,
+            HBM,
             full(TGT, D),
             full(TGT, D),
-            full(D, 4 * D),
+            HBM,
         ],
         out_shape=[
             shaped(bf, TGT, D),
@@ -379,7 +369,14 @@
             shaped(f32, TGT, D),
             shaped(bf, D, 4 * D),
         ],
-        scratch_shapes=[pltpu.SemaphoreType.DMA],
+        scratch_shapes=[
+            pltpu.VMEM((KEYS, D), bf),
+            pltpu.VMEM((KEYS, D), bf),
+            pltpu.VMEM((PAIRS, 512, KEYS), bf),
+            pltpu.VMEM((D, 4 * D), bf),
+            pltpu.SemaphoreType.DMA((4,)),
+            pltpu.SemaphoreType.DMA,
+        ],
         compiler_params=params(),
         cost_estimate=cost(20, 20),
         name="cross_forward",
@@ -510,14 +507,14 @@
     )(tgt_len, h2, gain, out_grad, blocks)
 
 
-def cross_backward_kernel(h1_ref, gain_ref, g2_ref, w_ref, q_ref, k_ref, v_ref, p_ref, *refs):
+def cross_backward_kernel(h1_ref, gain_ref, g2_ref, wq_ref, wo_ref, q_ref, k_ref, v_ref, p_ref, *refs):
     dq, dkv_ref, g1_ref, dgain_ref, grad_mixed = refs
     j = pl.program_id(0)
     bf = jnp.bfloat16
 
     @pl.when(j == 0)
     def _():
-        grad_mixed[...] = mm_nt(g2_ref[...].astype(bf), w_ref[:, 2304:]).astype(bf)
+        grad_mixed[...] = mm_nt(g2_ref[...].astype(bf), wo_ref[...]).astype(bf)
 
     for s, pair in pairs_here(CROSS_BACKWARD):
         at = pair_columns(pair)
@@ -531,7 +528,7 @@
 
     @pl.when(j == PAIRS // CROSS_BACKWARD - 1)
     def _():
-        back, dgain = rms_back(h1_ref[...], gain_ref[...], mm_nt(dq[...], w_ref[:, :768]))
+        back, dgain = rms_back(h1_ref[...], gain_ref[...], mm_nt(dq[...], wq_ref[...]))
         g1_ref[...] = g2_ref[...] + back
         dgain_ref[...] = dgain
 
@@ -545,7 +542,8 @@
             full(TGT, D),
             full(1, D),
             full(TGT, D),
-            full(D, 4 * D),
+            pl.BlockSpec((D, D), lambda j: (0, 0)),
+            pl.BlockSpec((D, D), lambda j: (0, 3)),
             full(TGT, D),
             full(KEYS, D),
             full(KEYS, D),
@@ -562,7 +560,7 @@
         compiler_params=params(),
         cost_estimate=cost(16, 20),
         name="cross_backward",
-    )(h1, gain, g2, w, q, k, v, p)
+    )(h1, gain, g2, w, w, q, k, v, p)
 
 
 def cross_grads_kernel(
@@ -572,13 +570,30 @@
     bf = jnp.bfloat16
     hidden = h1_ref[...]
     normed = (hidden * rms_scale(hidden) * gain_ref[...]).astype(bf)
+
+    def send(matrix):
+        for source, out_ref in enumerate((mine_ref, other_ref)):
+            core = pos_ref[3] ^ source
+            start_split(
+                pos_ref,
+                rings,
+                matrix,
+                lambda m: pl.multiple_of(m * D + core * 384, 128),
+                whole,
+                lambda *places: out_ref.at[places],
+                core,
+                sem,
+            )
+
     whole[:, :768] = mm_tn(normed, dq_ref[...]).astype(bf)
+    send(0)
     whole[:, 2304:] = mm_tn(mixed_ref[...], g2_ref[...].astype(bf)).astype(bf)
+    send(3)
     for k in range(4):
         at = pl.ds(768 + 384 * k, 384)
         whole[:, at] = mm(mem_t_ref[...], dkv_ref[:, pl.ds(384 * k, 384)]).astype(bf)
-    parts = functools.partial(square_parts, 384)
-    start_split(pos_ref, rings, parts, [whole], [mine_ref, other_ref], sem)
+        if k % 2:
+            send(1 + k // 2)
     wait_whole([whole], sem)
 
 
@@ -718,10 +733,6 @@
     )(pos, gain, kept, kept_other, half, half_other)
 
 
-def after(v, token):
-    return v + (token * 0).astype(v.dtype)
-
-
 def column_blocks(self_qkv, self_out, cross_qkv, cross_out, ffn_in):
     def chunks(v):
         return v.reshape(6, 8, -1).swapaxes(0, 1)
@@ -838,11 +849,11 @@
         "me,de->md", then(grad_kv, cross_terms[2], ffn_x)[:MEM], cross_w[:, 768:2304],
         preferred_element_type=jnp.float32,
     )[None]
-    self_terms = ring_first(then(self_low, memory_grad, incoming), self_high, self_rings[0])
+    self_terms = ring_first(then(self_low, memory_grad), self_high, self_rings[0])
     cross_terms = ring_second(cross_terms, rings[0])
     cross_low, cross_high = ring_halves((then(cross_terms[0], self_terms[2]), *cross_terms[1:]))
     self_terms = ring_second(self_terms, self_rings[0])
-    self_low, self_high = ring_halves((then(self_terms[0], cross_low), *self_terms[1:]))
+    self_low, self_high = ring_halves((then(self_terms[0], cross_low, incoming), *self_terms[1:]))
     cross_terms = ring_first(then(cross_low, self_low), cross_high, rings[1])
     incoming = then(incoming, cross_terms[2]).reshape(
         owner_count * SLOTS, model_width + 128

time: 320 us -> 312 us (0.975)
  Pallas kernels: 91.5 us -> 85 us
  waiting for transfers between devices: 96.4 us -> 90.1 us
  starting transfers between devices: 33.5 us -> 38 us
    all_to_all x1, waiting for transfers between devices: 12.7 us -> 2.38 us  [body(): lax.all_to_all(outgoing, AXES, split_axis=0, concat_axis=0, tiled=True)]
    ppermute x12, starting transfers between devices: 14.3 us -> 18.9 us  [ring_pair(): return lax.ppermute(v, ring + ('c',), perm)]
    pallas_call x1, Pallas kernels: 20.8 us -> 17.3 us  [cross_forward(): pl.pallas_call(cross_forward_kernel, grid=(PAIRS // CROSS_FORWARD,), in_s...]
  transfers between devices with their start and end apart: 23 -> 23, of which waited for: 11 -> 13; matrix products, arithmetic and copies ran while one was open for 15% -> 16% of each run, Pallas kernels for 14% -> 14%
where the time goes in v2:
time: 312 us; the launch traced here: 307 us
  waiting for transfers between devices  90.1 us (29%)
  Pallas kernels  85 us (27%)
  starting transfers between devices  38 us (12%)
  local copies, waits for them, and re-layouts  22.1 us (7%)
  other arithmetic  21.5 us (7%)
  blocking collectives  19.6 us (6%)
  between operations  15.9 us (5%)
  matrix products  14.5 us (5%)
    all_gather x1, waiting for transfers between devices, all_weights(): return lax.all_gather(piece, TORUS).reshape(4, 4, 4, 2, BLOCK, -1)  37.9 us
    all_to_all x1, blocking collectives, body(): lax.all_to_all(then(request, whole), AXES, split_axis=0, concat_axis=0, t...  19.6 us
    ppermute x12, starting transfers between devices, ring_pair(): return lax.ppermute(v, ring + ('c',), perm)  18.9 us
    pallas_call x1, Pallas kernels, cross_forward(): pl.pallas_call(cross_forward_kernel, grid=(PAIRS // CROSS_FORWARD,), in_s...  17.3 us
    pallas_call x1, Pallas kernels, ffn_both(): pl.pallas_call(ffn_kernel, grid=(FF // 512,), in_specs=[SCALARS, full(TGT...  16.9 us
    pallas_call x1, Pallas kernels, cross_backward(): pl.pallas_call(cross_backward_kernel, grid=(PAIRS // CROSS_BACKWARD,), in...  16 us
    ppermute x12, waiting for transfers between devices, ring_pair(): return lax.ppermute(v, ring + ('c',), perm)  13.6 us
    reduce_scatter x1, waiting for transfers between devices, body(): ffn_sum = lax.psum_scatter(ffn_y, RING_Z)  13.4 us
  transfers between devices with their start and end apart: 23, of which 13 were waited for; matrix products, arithmetic and copies ran while one was open for 16% of the time, Pallas kernels for 14%

profile of v2, /device:TPU:0, one launch (start us, length us, event | category | flops | bytes accessed | tf_op | source)
XLA Modules:
  0.0 306.8 jit_solution(9425859179457153551)
XLA Ops:
  7.2 1.0 reshape_reshape.6
  8.2 0.8 pad_maximum_fusion.4
  9.0 0.8 pad_maximum_fusion.3
  9.8 0.7 pad_maximum_fusion.1
  10.5 4.3 %all-to-all-start = ((bf16[8,6,1280]{2,1,0:T(8,128)(2,1)}), bf16[8,6,1280]{2,1,0:T(8,128)(2,1)S(1)}, u32[]{:S(2)}, u32[]{:S(2)}) async-start(bf16[8,6,1280]{2,1,0:T(8,128)(2,1)} %pad_maximum_fusion.1), calls=%async_computation | async-start | bytes 327680 | tf_op jit(solution)/shard_map/all_to_all | solution.py:746
  14.9 0.8 reshape.327
  15.6 5.1 %all-to-all-done = bf16[8,6,1280]{2,1,0:T(8,128)(2,1)S(1)} async-done(((bf16[8,6,1280]{2,1,0:T(8,128)(2,1)}), bf16[8,6,1280]{2,1,0:T(8,128)(2,1)S(1)}, u32[]{:S(2)}, u32[]{:S(2)}) %all-to-all-start) | async-done | bytes 122912 | tf_op jit(solution)/shard_map/all_to_all | solution.py:746
  21.5 0.7 fusion.35
  22.2 0.7 broadcast_divide_fusion
  24.3 19.6 %all_to_all.32 = f32[128,1,32]{2,1,0:T(1,128)S(1)} all-to-all(f32[128,1,32]{2,1,0:T(1,128)S(1)} %bitcast.152), channel_id=1, replica_groups=mesh['x'=4,'yh'=2,'zh'=2,'zl'=2,'yl'=2,'c'=2] {'x','yh','zh','zl','yl','c'}, dimensions={0} | all-to-all | bytes 32768 | tf_op jit(solution)/shard_map/all_to_all | solution.py:797
  44.1 2.9 fusion.6
  46.9 2.4 reshape.324
  49.3 4.6 %all-to-all-start.2 = ((bf16[128,4,768]{2,1,0:T(4,128)(2,1)}), bf16[128,4,768]{2,1,0:T(4,128)(2,1)S(1)}, u32[]{:S(2)}, u32[]{:S(2)}) async-start(bf16[128,4,768]{2,1,0:T(4,128)(2,1)} %reshape.324), calls=%async_computation.2 | async-start | bytes 1572864 | tf_op jit(solution)/shard_map/all_to_all | solution.py:805
  54.4 3.2 %copy.87 = bf16[1,1056,768]{1,2,0:T(8,128)(2,1)S(1)} copy(bf16[1,1056,768]{2,1,0:T(8,128)(2,1)} %param.19) | data formatting | bytes 3244032 | tf_op args[4]
  58.9 1.4 pad.4.early_ref.mem_t_ref
  61.1 0.7 reshape.326.gain_ref
  61.9 0.7 reshape.330.gain_ref
  62.6 0.7 reshape.331.gain_ref
  63.3 10.7 %all-to-all-done.2 = bf16[128,4,768]{2,1,0:T(4,128)(2,1)S(1)} async-done(((bf16[128,4,768]{2,1,0:T(4,128)(2,1)}), bf16[128,4,768]{2,1,0:T(4,128)(2,1)S(1)}, u32[]{:S(2)}, u32[]{:S(2)}) %all-to-all-start.2) | async-done | bytes 786464 | tf_op jit(solution)/shard_map/all_to_all | solution.py:805
  74.0 1.1 reshape.325.rows_ref
  75.1 37.9 %all-gather.3.cloned.1.call-done = bf16[6144,1536]{1,0:T(8,128)(2,1)} async-done(((bf16[48,1536]{1,0:T(8,128)(2,1)}), bf16[6144,1536]{1,0:T(8,128)(2,1)}) %all-gather.3.cloned.1.call-update) | async-done | bytes 18874384 | tf_op jit(solution)/shard_map/all_gather | solution.py:752
  113.0 8.5 %self_forward.1 = (bf16[256,1536]{1,0:T(8,128)(2,1)}, bf16[256,2304]{1,0:T(8,128)(2,1)}, bf16[6,512,256]{2,1,0:T(8,128)(2,1)}, f32[256,768]{1,0:T(8,128)}, bf16[768,3072]{1,0:T(8,128)(2,1)}) custom-call(bf16[512,768]{1,0:T(8,128)(2,1)} %reshape.325.rows_ref, s32[256,1]{1,0:T(8,128)} %fusion.27.slot_ref, f32[1,768]{1,0:T(1,128)} %reshape.326.gain_ref, ...), custom_call_target="tpu_custom_call" | custom-call | flops 8000000000 | bytes 12000000 | tf_op jit(solution)/shard_map/self_forward/pallas_call | solution.py:279
  121.5 17.3 %cross_forward.1 = (bf16[256,768]{1,0:T(8,128)(2,1)}, bf16[1152,768]{1,0:T(8,128)(2,1)}, bf16[1152,768]{1,0:T(8,128)(2,1)}, bf16[6,512,1152]{2,1,0:T(8,128)(2,1)...) custom-call(s32[1]{0:T(128)S(6)} %copy.99.len_ref, ...), custom_call_target="tpu_custom_call" | custom-call | flops 20000000000 | bytes 20000000 | tf_op jit(solution)/shard_map/cross_forward/pallas_call | solution.py:350
  138.8 16.9 %ffn_both.1 = (f32[256,768]{1,0:T(8,128)}, f32[256,768]{1,0:T(8,128)}, f32[1,768]{1,0:T(1,128)}, bf16[4,2,4,4,48,768]{5,4,3,2,1,0:T(8,128)(2,1)}) custom-call(s32[1]{0:T(128)S(6)} %copy.98.len_ref, f32[256,768]{1,0:T(8,128)} %get-tuple-element.55.h2_ref, f32[1,768]{1,0:T(1,128)} %reshape.331.gain_ref, bf16[256,768]{1,0:T(8,128)(2,1)} %bitcast.175, ...), custom_call_target="tpu_custom_call" | custom-call | flops 15000000512 | bytes 25000000 | tf_op jit(solution)/shard_map/ffn_both/pallas_call | solution.py:482
  156.3 16.0 %cross_backward.1 = (bf16[256,768]{1,0:T(8,128)(2,1)}, bf16[1152,1536]{1,0:T(8,128)(2,1)}, f32[256,768]{1,0:T(8,128)}, f32[1,768]{1,0:T(1,128)}) custom-call(f32[256,768]{1,0:T(8,128)} %get-tuple-element.54.h1_ref, f32[1,768]{1,0:T(1,128)} %reshape.330.gain_ref, f32[256,768]{1,0:T(8,128)} %get-tuple-element.57.g2_ref, ...), custom_call_target="tpu_custom_call" | custom-call | flops 16000000000 | bytes 20000000 | tf_op jit(solution)/shard_map/cross_backward/pallas_call | solution.py:538
  172.4 9.4 %cross_grads.1 = (bf16[4,4,4,48,384]{4,3,2,1,0:T(8,128)(2,1)}, bf16[4,4,4,48,384]{4,3,2,1,0:T(8,128)(2,1)}) custom-call(s32[4]{0:T(128)} %pad_add_fusion.pos_ref, f32[256,768]{1,0:T(8,128)} %get-tuple-element.54.h1_ref, f32[1,768]{1,0:T(1,128)} %reshape.330.gain_ref, f32[256,768]{1,0:T(8,128)} %get-tuple-element.57.g2_ref, ...), custom_call_target="tpu_custom_call" | custom-call | flops 6000000000 | bytes 12000000 | tf_op jit(solution)/shard_map/cross_grads/pallas_call | solution.py:603
  182.4 11.7 %self_backward.1 = (bf16[256,1536]{1,0:T(8,128)(2,1)}, bf16[256,1536]{1,0:T(8,128)(2,1)}, bf16[512,896]{1,0:T(8,128)(2,1)}) custom-call(s32[4]{0:T(128)} %pad_add_fusion.pos_ref, s32[256,1]{1,0:T(8,128)} %fusion.27.slot_ref, bf16[256,1536]{1,0:T(8,128)(2,1)} %get-tuple-element.67.kept_ref, f32[1,768]{1,0:T(1,128)} %reshape.326.gain_ref, ...), custom_call_target="tpu_custom_call" | custom-call | flops 8000000000 | bytes 10000000 | tf_op jit(solution)/shard_map/self_backward/pallas_call | solution.py:663
  194.4 1.7 add_convert_fusion.1
  196.1 2.6 collective-permute-start.3
  198.7 1.1 reshape.332
  199.9 5.2 %self_grads.1 = (bf16[2,4,4,48,384]{4,3,2,1,0:T(8,128)(2,1)}, bf16[2,4,4,48,384]{4,3,2,1,0:T(8,128)(2,1)}) custom-call(s32[4]{0:T(128)} %pad_add_fusion.pos_ref, f32[1,768]{1,0:T(1,128)} %reshape.326.gain_ref, bf16[256,1536]{1,0:T(8,128)(2,1)} %get-tuple-element.67.kept_ref, bf16[256,1536]{1,0:T(8,128)(2,1)} %collective-permute-done.1.kept_other_ref, ...), custom_call_target="tpu_custom_call" | custom-call | flops 3000000000 | bytes 8000000 | tf_op jit(solution)/shard_map/self_grads/pallas_call | solution.py:724
  205.1 2.6 collective-permute-start.4
  207.7 5.7 %all-to-all-start.3 = ((bf16[128,4,896]{2,1,0:T(4,128)(2,1)}), bf16[128,4,896]{2,1,0:T(4,128)(2,1)S(1)}, u32[]{:S(2)}, u32[]{:S(2)}) async-start(bf16[128,4,896]{2,1,0:T(4,128)(2,1)} %reshape.332), calls=%async_computation.4 | async-start | bytes 1835008 | tf_op jit(solution)/shard_map/all_to_all | solution.py:840
  214.1 2.0 fusion.8
  216.7 7.2 %convolution_bitcast_fusion = f32[1,1056,768]{2,1,0:T(8,128)} fusion(bf16[1152,1536]{1,0:T(8,128)(2,1)} %get-tuple-element.85.dkv_ref, bf16[768,3072]{1,0:T(8,128)(2,1)} %get-tuple-element.58.wq_ref.wo_ref), kind=kOutput, calls=%fused_computation.3 | convolution fusion | flops 2491416576 | bytes 8847360 | tf_op jit(solution)/shard_map/me,de->md/dot_general | solution.py:848
  223.8 5.1 %collective-permute-done.4 = bf16[2,4,4,48,384]{4,3,2,1,0:T(8,128)(2,1)} collective-permute-done((bf16[2,4,4,48,384]{4,3,2,1,0:T(8,128)(2,1)}, bf16[2,4,4,48,384]{4,3,2,1,0:T(8,128)(2,1)}, u32[]{:S(2)}, u32[]{:S(2)}) %collective-permute-start.4) | collective-permute-done | bytes 1179680 | tf_op jit(solution)/shard_map/ppermute | solution.py:43
  228.9 2.0 fusion.9
  231.7 1.5 fusion.17
  233.1 2.8 collective-permute-start.7
  236.0 2.4 all-to-all-done.3
  238.4 2.8 collective-permute-done.6
  241.2 1.5 fusion.11
  242.6 3.0 collective-permute-start.8
  245.7 1.7 collective-permute-done.7
  247.3 1.0 fusion.18
  249.1 4.5 %fusion = f32[1954,768]{1,0:T(8,128)} fusion(s32[512]{0:T(512)S(1)} %sub.34, bf16[512,896]{1,0:T(8,128)(2,1)S(1)} %reshape.334), kind=kOutput, calls=%fused_computation.1 | convolution fusion | flops 1537688576 | bytes 6791168 | tf_op jit(solution)/shard_map/sr,sd->rd/dot_general | solution.py:862
  254.2 1.0 fusion.23
  255.2 0.9 collective-permute-start.13
  256.1 0.7 copy-done.5
  256.9 1.6 collective-permute-start.9
  258.5 2.3 collective-permute-done.13
  261.5 0.9 fusion.34
  262.5 1.7 fusion.25
  264.2 2.1 collective-permute-start.10
  266.5 0.8 bitcast_add_fusion.2
  267.2 13.4 %reduce-scatter.8.cloned.1.call-done = bf16[1,48,768]{2,1,0:T(8,128)(2,1)} async-done(((bf16[4,48,768]{2,1,0:T(8,128)(2,1)}), bf16[1,48,768]{2,1,0:T(8,128)(2,1)}) %reduce-scatter.8.cloned.1.call-update) | async-done | bytes 73744 | tf_op jit(solution)/shard_map/reduce_scatter | solution.py:824
  280.7 1.6 collective-permute-start.11
  282.3 0.8 slice_convert_fusion.1
  283.1 0.7 slice.347
  283.8 0.9 collective-permute-done.11
  284.8 0.8 reshape.335
  285.5 3.4 %all-to-all-start.4 = ((f32[8,6,1280]{2,1,0:T(8,128)}), f32[8,6,1280]{2,1,0:T(8,128)S(1)}, u32[]{:S(2)}, u32[]{:S(2)}) async-start(f32[8,6,1280]{2,1,0:T(8,128)} %reshape.335), calls=%async_computation.7 | async-start | bytes 655360 | tf_op jit(solution)/shard_map/all_to_all | solution.py:873
  289.6 6.9 %all-to-all-done.4 = f32[8,6,1280]{2,1,0:T(8,128)S(1)} async-done(((f32[8,6,1280]{2,1,0:T(8,128)}), f32[8,6,1280]{2,1,0:T(8,128)S(1)}, u32[]{:S(2)}, u32[]{:S(2)}) %all-to-all-start.4) | async-done | bytes 245792 | tf_op jit(solution)/shard_map/all_to_all | solution.py:873
  299.1 0.7 reshape_reshape.7
  (104 shorter events, 12.7 us)
Async XLA Ops:
  7.2 36.9 %copy-start = (bf16[1954,768]{1,0:T(8,128)(2,1)S(1)}, bf16[1954,768]{1,0:T(8,128)(2,1)}, u32[]{:S(2)}) copy-start(bf16[1954,768]{1,0:T(8,128)(2,1)} %param.18) | copy-start | bytes 9004036
  7.2 16.1 %copy-start.7 = (s32[1,256]{1,0:T(1,128)S(1)}, s32[1,256]{1,0:T(1,128)}, u32[]{:S(2)}) copy-start(s32[1,256]{1,0:T(1,128)} %param.15) | copy-start | bytes 3076
  7.2 16.7 %copy-start.10 = (bf16[6]{0:T(256)(128)(2,1)S(1)}, bf16[6]{0:T(256)(128)(2,1)}, u32[]{:S(2)}) copy-start(bf16[6]{0:T(256)(128)(2,1)} %param.22) | copy-start | bytes 40
  7.2 16.6 %copy-start.9 = (bf16[6]{0:T(256)(128)(2,1)S(1)}, bf16[6]{0:T(256)(128)(2,1)}, u32[]{:S(2)}) copy-start(bf16[6]{0:T(256)(128)(2,1)} %param.25) | copy-start | bytes 40
  7.2 16.6 %copy-start.8 = (bf16[6]{0:T(256)(128)(2,1)S(1)}, bf16[6]{0:T(256)(128)(2,1)}, u32[]{:S(2)}) copy-start(bf16[6]{0:T(256)(128)(2,1)} %param.28) | copy-start | bytes 40
  10.5 10.2 %all-to-all-start = ((bf16[8,6,1280]{2,1,0:T(8,128)(2,1)}), bf16[8,6,1280]{2,1,0:T(8,128)(2,1)S(1)}, u32[]{:S(2)}, u32[]{:S(2)}) async-start(bf16[8,6,1280]{2,1,0:T(8,128)(2,1)} %pad_maximum_fusion.1), calls=%async_computation | async-start | bytes 327680 | tf_op jit(solution)/shard_map/all_to_all | solution.py:746
  14.8 98.2 %all-gather.3.cloned.1.call-start = ((), (), s32[]{:S(2)}) async-start(), calls=%async_computation.11 | async-start | bytes 19021824 | tf_op jit(solution)/shard_map/all_gather | solution.py:752
  49.3 24.8 %all-to-all-start.2 = ((bf16[128,4,768]{2,1,0:T(4,128)(2,1)}), bf16[128,4,768]{2,1,0:T(4,128)(2,1)S(1)}, u32[]{:S(2)}, u32[]{:S(2)}) async-start(bf16[128,4,768]{2,1,0:T(4,128)(2,1)} %reshape.324), calls=%async_computation.2 | async-start | bytes 1572864 | tf_op jit(solution)/shard_map/all_to_all | solution.py:805
  53.9 162.7 %reduce-scatter.4.cloned.1.call-start = ((), (), s32[]{:S(2)}) async-start(), calls=%async_computation.8 | async-start | bytes 10616832 | tf_op jit(solution)/shard_map/reduce_scatter | solution.py:822
  172.3 9.8 %copy-start.11 = (bf16[256,1536]{1,0:T(8,128)(2,1)S(1)}, bf16[256,1536]{1,0:T(8,128)(2,1)}, u32[]{:S(2)}) copy-start(bf16[256,1536]{1,0:T(8,128)(2,1)} %get-tuple-element.67.kept_ref) | copy-start | bytes 2359300
  181.8 12.6 %collective-permute-start = (bf16[4,4,4,48,384]{4,3,2,1,0:T(8,128)(2,1)}, bf16[4,4,4,48,384]{4,3,2,1,0:T(8,128)(2,1)S(1)}, u32[]{:S(2)}, u32[]{:S(2)}) collective-permute-start(bf16[4,4,4,48,384]{4,3,2,1,0:T(8,128)(2,1)} %get-tuple-element.77), channel_id=1, source_target_pairs={{0,1},{1,0},{2,3},{3,2},{4,5},{5,4},{6,7},{7,6},{8,9},{9,8},{10,11... | collective-permute-start | bytes 7077896 | tf_op jit(solution)/shard_map/ppermute | solution.py:47
  182.1 17.8 %collective-permute-start.1 = (bf16[256,1536]{1,0:T(8,128)(2,1)S(1)}, bf16[256,1536]{1,0:T(8,128)(2,1)}, u32[]{:S(2)}, u32[]{:S(2)}) collective-permute-start(bf16[256,1536]{1,0:T(8,128)(2,1)S(1)} %copy-done.11), channel_id=1, source_target_pairs={{0,1},{1,0},{2,3},{3,2},{4,5},{5,4},{6,7},{7,6},{8,9},{9,8},{10,11... | collective-permute-start | bytes 2359304 | tf_op jit(solution)/shard_map/ppermute | solution.py:47
  182.4 12.0 %copy-start.2 = (bf16[4,4,4,48,384]{4,3,2,1,0:T(8,128)(2,1)S(1)}, bf16[4,4,4,48,384]{4,3,2,1,0:T(8,128)(2,1)}, u32[]{:S(2)}) copy-start(bf16[4,4,4,48,384]{4,3,2,1,0:T(8,128)(2,1)} %get-tuple-element.76) | copy-start | bytes 7077892
  194.1 4.6 %copy-start.4 = (bf16[512,896]{1,0:T(8,128)(2,1)S(1)}, bf16[512,896]{1,0:T(8,128)(2,1)}, u32[]{:S(2)}) copy-start(bf16[512,896]{1,0:T(8,128)(2,1)} %get-tuple-element.79) | copy-start | bytes 2752516
  194.1 5.8 %collective-permute-start.2 = (bf16[256,1536]{1,0:T(8,128)(2,1)}, bf16[256,1536]{1,0:T(8,128)(2,1)}, u32[]{:S(2)}, u32[]{:S(2)}) collective-permute-start(bf16[256,1536]{1,0:T(8,128)(2,1)} %get-tuple-element.81), channel_id=1, source_target_pairs={{0,1},{1,0},{2,3},{3,2},{4,5},{5,4},{6,7},{7,6},{8,9},{9,8},{10,11... | collective-permute-start | bytes 2359304 | tf_op jit(solution)/shard_map/ppermute | solution.py:47
  196.1 18.0 %collective-permute-start.3 = (bf16[2,4,4,48,384]{4,3,2,1,0:T(8,128)(2,1)}, bf16[2,4,4,48,384]{4,3,2,1,0:T(8,128)(2,1)}, u32[]{:S(2)}, u32[]{:S(2)}) collective-permute-start(bf16[2,4,4,48,384]{4,3,2,1,0:T(8,128)(2,1)} %get-tuple-element.99), channel_id=1, source_target_pairs={{0,12},{1,5},{4,8},{5,1},{8,4},{9,13},{12,0},{13,9},{2,14},{3,7},{... | collective-permute-start | bytes 3538952 | tf_op jit(solution)/shard_map/ppermute | solution.py:43
  205.1 23.8 %collective-permute-start.4 = (bf16[2,4,4,48,384]{4,3,2,1,0:T(8,128)(2,1)}, bf16[2,4,4,48,384]{4,3,2,1,0:T(8,128)(2,1)}, u32[]{:S(2)}, u32[]{:S(2)}) collective-permute-start(bf16[2,4,4,48,384]{4,3,2,1,0:T(8,128)(2,1)} %get-tuple-element.87), channel_id=1, source_target_pairs={{0,96},{1,33},{32,64},{33,1},{64,32},{65,97},{96,0},{97,65},{2,98}... | collective-permute-start | bytes 3538952 | tf_op jit(solution)/shard_map/ppermute | solution.py:43
  207.7 30.7 %all-to-all-start.3 = ((bf16[128,4,896]{2,1,0:T(4,128)(2,1)}), bf16[128,4,896]{2,1,0:T(4,128)(2,1)S(1)}, u32[]{:S(2)}, u32[]{:S(2)}) async-start(bf16[128,4,896]{2,1,0:T(4,128)(2,1)} %reshape.332), calls=%async_computation.4 | async-start | bytes 1835008 | tf_op jit(solution)/shard_map/all_to_all | solution.py:840
  213.4 40.8 %reduce-scatter.6.cloned.1.call-start = ((), (), s32[]{:S(2)}) async-start(), calls=%async_computation.9 | async-start | bytes 1474560 | tf_op jit(solution)/shard_map/reduce_scatter | solution.py:823
  216.1 15.6 %collective-permute-start.5 = (bf16[4,4,48,384]{3,2,1,0:T(8,128)(2,1)}, bf16[4,4,48,384]{3,2,1,0:T(8,128)(2,1)}, u32[]{:S(2)}, u32[]{:S(2)}) collective-permute-start(bf16[4,4,48,384]{3,2,1,0:T(8,128)(2,1)} %fusion.8), channel_id=1, source_target_pairs={{0,4},{1,13},{4,0},{5,9},{8,12},{9,5},{12,8},{13,1},{2,6},{3,15},{... | collective-permute-start | bytes 1769480 | tf_op jit(solution)/shard_map/ppermute | solution.py:43
  216.6 64.1 %reduce-scatter.8.cloned.1.call-start = ((), (), s32[]{:S(2)}) async-start(), calls=%async_computation.10 | async-start | bytes 368640 | tf_op jit(solution)/shard_map/reduce_scatter | solution.py:824
  216.6 12.3 %copy-start.3 = (bf16[2,4,4,48,384]{4,3,2,1,0:T(8,128)(2,1)S(1)}, bf16[2,4,4,48,384]{4,3,2,1,0:T(8,128)(2,1)}, u32[]{:S(2)}) copy-start(bf16[2,4,4,48,384]{4,3,2,1,0:T(8,128)(2,1)} %get-tuple-element.86) | copy-start | bytes 3538948
  231.0 10.2 %collective-permute-start.6 = (bf16[4,4,48,384]{3,2,1,0:T(8,128)(2,1)}, bf16[4,4,48,384]{3,2,1,0:T(8,128)(2,1)}, u32[]{:S(2)}, u32[]{:S(2)}) collective-permute-start(bf16[4,4,48,384]{3,2,1,0:T(8,128)(2,1)} %fusion.9), channel_id=1, source_target_pairs={{0,32},{1,97},{32,0},{33,65},{64,96},{65,33},{96,64},{97,1},{2,34}... | collective-permute-start | bytes 1769480 | tf_op jit(solution)/shard_map/ppermute | solution.py:43
  233.1 14.2 %collective-permute-start.7 = (bf16[2,4,48,384]{3,2,1,0:T(8,128)(2,1)S(1)}, bf16[2,4,48,384]{3,2,1,0:T(8,128)(2,1)}, u32[]{:S(2)}, u32[]{:S(2)}) collective-permute-start(bf16[2,4,48,384]{3,2,1,0:T(8,128)(2,1)S(1)} %get-tuple-element.103), channel_id=1, source_target_pairs={{0,18},{1,3},{2,16},{3,1},{16,2},{17,19},{18,0},{19,17},{4,22},{5,... | collective-permute-start | bytes 884744 | tf_op jit(solution)/shard_map/ppermute | solution.py:43
  242.6 13.5 %collective-permute-start.8 = (bf16[2,4,48,384]{3,2,1,0:T(8,128)(2,1)S(1)}, bf16[2,4,48,384]{3,2,1,0:T(8,128)(2,1)S(1)}, u32[]{:S(2)}, u32[]{:S(2)}) collective-permute-start(bf16[2,4,48,384]{3,2,1,0:T(8,128)(2,1)S(1)} %get-tuple-element.100), channel_id=1, source_target_pairs={{0,12},{1,5},{4,8},{5,1},{8,4},{9,13},{12,0},{13,9},{2,14},{3,7},{... | collective-permute-start | bytes 884744 | tf_op jit(solution)/shard_map/ppermute | solution.py:43
  248.3 5.9 %collective-permute-start.12 = (bf16[4,48,384]{2,1,0:T(8,128)(2,1)S(1)}, bf16[4,48,384]{2,1,0:T(8,128)(2,1)S(1)}, u32[]{:S(2)}, u32[]{:S(2)}) collective-permute-start(bf16[4,48,384]{2,1,0:T(8,128)(2,1)S(1)} %fusion.18), channel_id=1, source_target_pairs={{0,2},{1,19},{2,0},{3,17},{16,18},{17,3},{18,16},{19,1},{4,6},{5,2... | collective-permute-start | bytes 442376 | tf_op jit(solution)/shard_map/ppermute | solution.py:43
  255.2 5.6 %collective-permute-start.13 = (bf16[2,48,384]{2,1,0:T(8,128)(2,1)S(1)}, bf16[2,48,384]{2,1,0:T(8,128)(2,1)S(1)}, u32[]{:S(2)}, u32[]{:S(2)}) collective-permute-start(bf16[2,48,384]{2,1,0:T(8,128)(2,1)S(1)} %get-tuple-element.107), channel_id=1, source_target_pairs={{0,96},{1,33},{32,64},{33,1},{64,32},{65,97},{96,0},{97,65},{2,98}... | collective-permute-start | bytes 221192 | tf_op jit(solution)/shard_map/ppermute | solution.py:43
  256.1 0.7 copy-start.5
  256.9 5.7 %collective-permute-start.9 = (bf16[4,48,384]{2,1,0:T(8,128)(2,1)S(1)}, bf16[4,48,384]{2,1,0:T(8,128)(2,1)}, u32[]{:S(2)}, u32[]{:S(2)}) collective-permute-start(bf16[4,48,384]{2,1,0:T(8,128)(2,1)S(1)} %fusion.19), channel_id=1, source_target_pairs={{0,4},{1,13},{4,0},{5,9},{8,12},{9,5},{12,8},{13,1},{2,6},{3,15},{... | collective-permute-start | bytes 442376 | tf_op jit(solution)/shard_map/ppermute | solution.py:43
  260.9 0.6 copy-start.6
  261.5 38.4 %copy-start.1 = (bf16[1954,768]{1,0:T(8,128)(2,1)S(1)}, bf16[1954,768]{1,0:T(8,128)(2,1)}, u32[]{:S(2)}) copy-start(bf16[1954,768]{1,0:T(8,128)(2,1)} %param.18) | copy-start | bytes 9004036
  262.4 4.0 %collective-permute-start.14 = (bf16[48,384]{1,0:T(8,128)(2,1)S(1)}, bf16[48,384]{1,0:T(8,128)(2,1)S(1)}, u32[]{:S(2)}, u32[]{:S(2)}) collective-permute-start(bf16[48,384]{1,0:T(8,128)(2,1)S(1)} %fusion.34), channel_id=1, source_target_pairs={{0,32},{1,97},{32,0},{33,65},{64,96},{65,33},{96,64},{97,1},{2,34}... | collective-permute-start | bytes 110600 | tf_op jit(solution)/shard_map/ppermute | solution.py:43
  264.2 16.4 %collective-permute-start.10 = (bf16[2,48,384]{2,1,0:T(8,128)(2,1)}, bf16[2,48,384]{2,1,0:T(8,128)(2,1)S(1)}, u32[]{:S(2)}, u32[]{:S(2)}) collective-permute-start(bf16[2,48,384]{2,1,0:T(8,128)(2,1)} %get-tuple-element.105), channel_id=1, source_target_pairs={{0,18},{1,3},{2,16},{3,1},{16,2},{17,19},{18,0},{19,17},{4,22},{5,... | collective-permute-start | bytes 221192 | tf_op jit(solution)/shard_map/ppermute | solution.py:43
  280.7 4.0 %collective-permute-start.11 = (bf16[48,384]{1,0:T(8,128)(2,1)S(1)}, bf16[48,384]{1,0:T(8,128)(2,1)S(1)}, u32[]{:S(2)}, u32[]{:S(2)}) collective-permute-start(bf16[48,384]{1,0:T(8,128)(2,1)S(1)} %fusion.33), channel_id=1, source_target_pairs={{0,2},{1,19},{2,0},{3,17},{16,18},{17,3},{18,16},{19,1},{4,6},{5,2... | collective-permute-start | bytes 110600 | tf_op jit(solution)/shard_map/ppermute | solution.py:43
  285.5 11.0 %all-to-all-start.4 = ((f32[8,6,1280]{2,1,0:T(8,128)}), f32[8,6,1280]{2,1,0:T(8,128)S(1)}, u32[]{:S(2)}, u32[]{:S(2)}) async-start(f32[8,6,1280]{2,1,0:T(8,128)} %reshape.335), calls=%async_computation.7 | async-start | bytes 655360 | tf_op jit(solution)/shard_map/all_to_all | solution.py:873
Sparse Core Ops, SparseCore 0:
  21.6 91.4 all-gather.2
  155.8 57.8 reduce-scatter.3
  216.7 31.9 reduce-scatter.5
  258.6 21.9 reduce-scatter.7

commit v3 on v2

--- a/solution.py
+++ b/solution.py
@@ -854,7 +854,7 @@
     cross_low, cross_high = ring_halves((then(cross_terms[0], self_terms[2]), *cross_terms[1:]))
     self_terms = ring_second(self_terms, self_rings[0])
     self_low, self_high = ring_halves((then(self_terms[0], cross_low, incoming), *self_terms[1:]))
-    cross_terms = ring_first(then(cross_low, self_low), cross_high, rings[1])
+    cross_terms = ring_first(then(cross_low, self_low, ffn_y), cross_high, rings[1])
     incoming = then(incoming, cross_terms[2]).reshape(
         owner_count * SLOTS, model_width + 128
     )
@@ -863,7 +863,7 @@
         "sr,sd->rd", row_hits, incoming[:, :model_width], preferred_element_type=jnp.float32
     )
     cross_terms = ring_second(cross_terms, rings[1])
-    cross_low, cross_high = ring_halves((then(cross_terms[0], ffn_y), *cross_terms[1:]))
+    cross_low, cross_high = ring_halves(cross_terms)
     self_terms = ring_first(self_low, self_high, self_rings[1])
     self_low, self_high = ring_halves(ring_second(self_terms, self_rings[1]))
     cross_sum = ring_total(cross_low, cross_high, rings[2])

time: 312 us -> 313 us (level)
  the two profiles are of different devices: /device:TPU:0 before, /device:TPU:80 now
where the time goes in v3:
time: 313 us; the launch traced here: 307 us
  waiting for transfers between devices  95.2 us (30%)
  Pallas kernels  85.1 us (27%)
  starting transfers between devices  37.2 us (12%)
  local copies, waits for them, and re-layouts  22.4 us (7%)
  other arithmetic  20.3 us (6%)
  between operations  15.9 us (5%)
  matrix products  15.8 us (5%)
  blocking collectives  15.3 us (5%)
    all_gather x1, waiting for transfers between devices, all_weights(): return lax.all_gather(piece, TORUS).reshape(4, 4, 4, 2, BLOCK, -1)  42 us
    ppermute x12, waiting for transfers between devices, ring_pair(): return lax.ppermute(v, ring + ('c',), perm)  33.9 us
    pallas_call x1, Pallas kernels, cross_forward(): pl.pallas_call(cross_forward_kernel, grid=(PAIRS // CROSS_FORWARD,), in_s...  17.3 us
    pallas_call x1, Pallas kernels, ffn_both(): pl.pallas_call(ffn_kernel, grid=(FF // 512,), in_specs=[SCALARS, full(TGT...  16.9 us
    pallas_call x1, Pallas kernels, cross_backward(): pl.pallas_call(cross_backward_kernel, grid=(PAIRS // CROSS_BACKWARD,), in...  16 us
    all_to_all x1, blocking collectives, body(): lax.all_to_all(then(request, whole), AXES, split_axis=0, concat_axis=0, t...  15.3 us
    ppermute x12, starting transfers between devices, ring_pair(): return lax.ppermute(v, ring + ('c',), perm)  11.9 us
    pallas_call x1, Pallas kernels, self_backward(): pl.pallas_call(self_backward_kernel, grid=(PAIRS // SELF_BACKWARD,), in_s...  11.7 us
  transfers between devices with their start and end apart: 23, of which 13 were waited for; matrix products, arithmetic and copies ran while one was open for 16% of the time, Pallas kernels for 14%

profile of v3, /device:TPU:80, one launch (start us, length us, event | category | flops | bytes accessed | tf_op | source)
XLA Modules:
  0.0 307.2 jit_solution(1664104717101503370)
XLA Ops:
  7.2 1.0 reshape_reshape.6
  8.2 0.8 pad_maximum_fusion.4
  9.0 0.8 pad_maximum_fusion.3
  9.8 0.7 pad_maximum_fusion.1
  10.5 3.6 %all-to-all-start = ((bf16[8,6,1280]{2,1,0:T(8,128)(2,1)}), bf16[8,6,1280]{2,1,0:T(8,128)(2,1)S(1)}, u32[]{:S(2)}, u32[]{:S(2)}) async-start(bf16[8,6,1280]{2,1,0:T(8,128)(2,1)} %pad_maximum_fusion.1), calls=%async_computation | async-start | bytes 327680 | tf_op jit(solution)/shard_map/all_to_all | solution.py:746
  14.2 0.8 reshape.331
  15.0 5.1 %all-to-all-done = bf16[8,6,1280]{2,1,0:T(8,128)(2,1)S(1)} async-done(((bf16[8,6,1280]{2,1,0:T(8,128)(2,1)}), bf16[8,6,1280]{2,1,0:T(8,128)(2,1)S(1)}, u32[]{:S(2)}, u32[]{:S(2)}) %all-to-all-start) | async-done | bytes 122912 | tf_op jit(solution)/shard_map/all_to_all | solution.py:746
  20.8 0.7 fusion.33
  21.5 0.7 broadcast_divide_fusion
  23.6 15.3 %all_to_all.32 = f32[128,1,32]{2,1,0:T(1,128)S(1)} all-to-all(f32[128,1,32]{2,1,0:T(1,128)S(1)} %bitcast.148), channel_id=1, replica_groups=mesh['x'=4,'yh'=2,'zh'=2,'zl'=2,'yl'=2,'c'=2] {'x','yh','zh','zl','yl','c'}, dimensions={0} | all-to-all | bytes 32768 | tf_op jit(solution)/shard_map/all_to_all | solution.py:797
  39.1 2.9 fusion.6
  41.9 2.4 reshape.328
  44.3 8.4 %all-to-all-start.2 = ((bf16[128,4,768]{2,1,0:T(4,128)(2,1)}), bf16[128,4,768]{2,1,0:T(4,128)(2,1)S(1)}, u32[]{:S(2)}, u32[]{:S(2)}) async-start(bf16[128,4,768]{2,1,0:T(4,128)(2,1)} %reshape.328), calls=%async_computation.2 | async-start | bytes 1572864 | tf_op jit(solution)/shard_map/all_to_all | solution.py:805
  53.2 3.2 %copy.87 = bf16[1,1056,768]{1,2,0:T(8,128)(2,1)S(1)} copy(bf16[1,1056,768]{2,1,0:T(8,128)(2,1)} %param.19) | data formatting | bytes 3244032 | tf_op args[4]
  57.7 1.4 pad.4.early_ref.mem_t_ref
  59.9 0.7 reshape.330.gain_ref
  60.7 0.7 reshape.334.gain_ref
  61.4 0.7 reshape.335.gain_ref
  62.1 6.3 %all-to-all-done.2 = bf16[128,4,768]{2,1,0:T(4,128)(2,1)S(1)} async-done(((bf16[128,4,768]{2,1,0:T(4,128)(2,1)}), bf16[128,4,768]{2,1,0:T(4,128)(2,1)S(1)}, u32[]{:S(2)}, u32[]{:S(2)}) %all-to-all-start.2) | async-done | bytes 786464 | tf_op jit(solution)/shard_map/all_to_all | solution.py:805
  68.4 1.1 reshape.329.rows_ref
  69.5 42.0 %all-gather.3.cloned.1.call-done = bf16[6144,1536]{1,0:T(8,128)(2,1)} async-done(((bf16[48,1536]{1,0:T(8,128)(2,1)}), bf16[6144,1536]{1,0:T(8,128)(2,1)}) %all-gather.3.cloned.1.call-update) | async-done | bytes 18874384 | tf_op jit(solution)/shard_map/all_gather | solution.py:752
  111.5 8.5 %self_forward.1 = (bf16[256,1536]{1,0:T(8,128)(2,1)}, bf16[256,2304]{1,0:T(8,128)(2,1)}, bf16[6,512,256]{2,1,0:T(8,128)(2,1)}, f32[256,768]{1,0:T(8,128)}, bf16[768,3072]{1,0:T(8,128)(2,1)}) custom-call(bf16[512,768]{1,0:T(8,128)(2,1)} %reshape.329.rows_ref, s32[256,1]{1,0:T(8,128)} %fusion.25.slot_ref, f32[1,768]{1,0:T(1,128)} %reshape.330.gain_ref, ...), custom_call_target="tpu_custom_call" | custom-call | flops 8000000000 | bytes 12000000 | tf_op jit(solution)/shard_map/self_forward/pallas_call | solution.py:279
  120.0 17.3 %cross_forward.1 = (bf16[256,768]{1,0:T(8,128)(2,1)}, bf16[1152,768]{1,0:T(8,128)(2,1)}, bf16[1152,768]{1,0:T(8,128)(2,1)}, bf16[6,512,1152]{2,1,0:T(8,128)(2,1)...) custom-call(s32[1]{0:T(128)S(6)} %copy.99.len_ref, ...), custom_call_target="tpu_custom_call" | custom-call | flops 20000000000 | bytes 20000000 | tf_op jit(solution)/shard_map/cross_forward/pallas_call | solution.py:350
  137.3 16.9 %ffn_both.1 = (f32[256,768]{1,0:T(8,128)}, f32[256,768]{1,0:T(8,128)}, f32[1,768]{1,0:T(1,128)}, bf16[4,2,4,4,48,768]{5,4,3,2,1,0:T(8,128)(2,1)}) custom-call(s32[1]{0:T(128)S(6)} %copy.98.len_ref, f32[256,768]{1,0:T(8,128)} %get-tuple-element.54.h2_ref, f32[1,768]{1,0:T(1,128)} %reshape.335.gain_ref, bf16[256,768]{1,0:T(8,128)(2,1)} %bitcast.171, ...), custom_call_target="tpu_custom_call" | custom-call | flops 15000000512 | bytes 25000000 | tf_op jit(solution)/shard_map/ffn_both/pallas_call | solution.py:482
  154.8 16.0 %cross_backward.1 = (bf16[256,768]{1,0:T(8,128)(2,1)}, bf16[1152,1536]{1,0:T(8,128)(2,1)}, f32[256,768]{1,0:T(8,128)}, f32[1,768]{1,0:T(1,128)}) custom-call(f32[256,768]{1,0:T(8,128)} %get-tuple-element.53.h1_ref, f32[1,768]{1,0:T(1,128)} %reshape.334.gain_ref, f32[256,768]{1,0:T(8,128)} %get-tuple-element.56.g2_ref, ...), custom_call_target="tpu_custom_call" | custom-call | flops 16000000000 | bytes 20000000 | tf_op jit(solution)/shard_map/cross_backward/pallas_call | solution.py:538
  170.8 9.4 %cross_grads.1 = (bf16[4,4,4,48,384]{4,3,2,1,0:T(8,128)(2,1)}, bf16[4,4,4,48,384]{4,3,2,1,0:T(8,128)(2,1)}) custom-call(s32[4]{0:T(128)} %pad_add_fusion.pos_ref, f32[256,768]{1,0:T(8,128)} %get-tuple-element.53.h1_ref, f32[1,768]{1,0:T(1,128)} %reshape.334.gain_ref, f32[256,768]{1,0:T(8,128)} %get-tuple-element.56.g2_ref, ...), custom_call_target="tpu_custom_call" | custom-call | flops 6000000000 | bytes 12000000 | tf_op jit(solution)/shard_map/cross_grads/pallas_call | solution.py:603
  180.9 11.7 %self_backward.1 = (bf16[256,1536]{1,0:T(8,128)(2,1)}, bf16[256,1536]{1,0:T(8,128)(2,1)}, bf16[512,896]{1,0:T(8,128)(2,1)}) custom-call(s32[4]{0:T(128)} %pad_add_fusion.pos_ref, s32[256,1]{1,0:T(8,128)} %fusion.25.slot_ref, bf16[256,1536]{1,0:T(8,128)(2,1)} %get-tuple-element.66.kept_ref, f32[1,768]{1,0:T(1,128)} %reshape.330.gain_ref, ...), custom_call_target="tpu_custom_call" | custom-call | flops 8000000000 | bytes 10000000 | tf_op jit(solution)/shard_map/self_backward/pallas_call | solution.py:663
  192.8 1.7 add_convert_fusion.1
  195.2 1.1 reshape.336
  196.4 5.3 %self_grads.1 = (bf16[2,4,4,48,384]{4,3,2,1,0:T(8,128)(2,1)}, bf16[2,4,4,48,384]{4,3,2,1,0:T(8,128)(2,1)}) custom-call(s32[4]{0:T(128)} %pad_add_fusion.pos_ref, f32[1,768]{1,0:T(1,128)} %reshape.330.gain_ref, bf16[256,1536]{1,0:T(8,128)(2,1)} %get-tuple-element.66.kept_ref, bf16[256,1536]{1,0:T(8,128)(2,1)} %collective-permute-done.1.kept_other_ref, ...), custom_call_target="tpu_custom_call" | custom-call | flops 3000000000 | bytes 8000000 | tf_op jit(solution)/shard_map/self_grads/pallas_call | solution.py:724
  201.7 1.7 collective-permute-start.4
  203.4 8.8 %all-to-all-start.3 = ((bf16[128,4,896]{2,1,0:T(4,128)(2,1)}), bf16[128,4,896]{2,1,0:T(4,128)(2,1)S(1)}, u32[]{:S(2)}, u32[]{:S(2)}) async-start(bf16[128,4,896]{2,1,0:T(4,128)(2,1)} %reshape.336), calls=%async_computation.4 | async-start | bytes 1835008 | tf_op jit(solution)/shard_map/all_to_all | solution.py:840
  212.2 2.0 fusion.8
  214.3 1.5 collective-permute-start.5
  215.9 7.2 %convolution_bitcast_fusion = f32[1,1056,768]{2,1,0:T(8,128)} fusion(bf16[1152,1536]{1,0:T(8,128)(2,1)} %get-tuple-element.84.dkv_ref, bf16[768,3072]{1,0:T(8,128)(2,1)} %get-tuple-element.57.wq_ref.wo_ref), kind=kOutput, calls=%fused_computation.3 | convolution fusion | flops 2491416576 | bytes 8847360 | tf_op jit(solution)/shard_map/me,de->md/dot_general | solution.py:848
  223.0 4.9 %collective-permute-done.4 = bf16[2,4,4,48,384]{4,3,2,1,0:T(8,128)(2,1)} collective-permute-done((bf16[2,4,4,48,384]{4,3,2,1,0:T(8,128)(2,1)}, bf16[2,4,4,48,384]{4,3,2,1,0:T(8,128)(2,1)}, u32[]{:S(2)}, u32[]{:S(2)}) %collective-permute-start.4) | collective-permute-done | bytes 1179680 | tf_op jit(solution)/shard_map/ppermute | solution.py:43
  227.9 2.1 fusion.9
  230.8 1.5 fusion.17
  232.2 0.9 all-to-all-done.3
  233.1 7.1 %collective-permute-done.6 = bf16[4,4,48,384]{3,2,1,0:T(8,128)(2,1)} collective-permute-done((bf16[4,4,48,384]{3,2,1,0:T(8,128)(2,1)}, bf16[4,4,48,384]{3,2,1,0:T(8,128)(2,1)}, u32[]{:S(2)}, u32[]{:S(2)}) %collective-permute-start.6) | collective-permute-done | bytes 589856 | tf_op jit(solution)/shard_map/ppermute | solution.py:43
  240.2 1.5 fusion.11
  242.2 6.3 %collective-permute-done.8 = bf16[2,4,48,384]{3,2,1,0:T(8,128)(2,1)S(1)} collective-permute-done((bf16[2,4,48,384]{3,2,1,0:T(8,128)(2,1)S(1)}, bf16[2,4,48,384]{3,2,1,0:T(8,128)(2,1)S(1)}, u32[]{:S(2)}, u32[]{:S(2)}) %collective-permute-start.8) | collective-permute-done | bytes 294944 | tf_op jit(solution)/shard_map/ppermute | solution.py:43
  248.5 2.5 collective-permute-start.9
  251.6 2.6 collective-permute-done.9
  254.2 0.7 fusion.23
  255.4 3.5 %collective-permute-done.7 = bf16[2,4,48,384]{3,2,1,0:T(8,128)(2,1)S(1)} collective-permute-done((bf16[2,4,48,384]{3,2,1,0:T(8,128)(2,1)S(1)}, bf16[2,4,48,384]{3,2,1,0:T(8,128)(2,1)S(1)}, u32[]{:S(2)}, u32[]{:S(2)}) %collective-permute-start.7) | collective-permute-done | bytes 294944 | tf_op jit(solution)/shard_map/ppermute | solution.py:43
  258.9 0.7 copy-done.5
  259.6 2.2 collective-permute-start.12
  261.9 1.1 reshape.338
  263.0 5.8 %fusion = f32[1954,768]{1,0:T(8,128)} fusion(s32[512]{0:T(512)S(1)} %sub.34, bf16[512,896]{1,0:T(8,128)(2,1)} %reshape.338), kind=kOutput, calls=%fused_computation.1 | convolution fusion | flops 1537688576 | bytes 6791168 | tf_op jit(solution)/shard_map/sr,sd->rd/dot_general | solution.py:862
  268.8 1.0 fusion.21
  269.8 0.8 collective-permute-start.13
  270.6 1.0 convert_reduce_fusion
  271.5 3.9 %collective-permute-done.13 = bf16[2,48,384]{2,1,0:T(8,128)(2,1)S(1)} collective-permute-done((bf16[2,48,384]{2,1,0:T(8,128)(2,1)S(1)}, bf16[2,48,384]{2,1,0:T(8,128)(2,1)S(1)}, u32[]{:S(2)}, u32[]{:S(2)}) %collective-permute-start.13) | collective-permute-done | bytes 73760 | tf_op jit(solution)/shard_map/ppermute | solution.py:43
  276.1 3.4 %collective-permute-done.14 = bf16[48,384]{1,0:T(8,128)(2,1)S(1)} collective-permute-done((bf16[48,384]{1,0:T(8,128)(2,1)S(1)}, bf16[48,384]{1,0:T(8,128)(2,1)S(1)}, u32[]{:S(2)}, u32[]{:S(2)}) %collective-permute-start.14) | collective-permute-done | bytes 36896 | tf_op jit(solution)/shard_map/ppermute | solution.py:43
  279.5 0.8 fusion.31
  280.4 0.8 slice_convert_fusion.1
  281.2 0.7 slice.348
  282.0 2.4 collective-permute-done.11
  284.4 0.8 bitcast_add_fusion.5
  285.2 0.8 reshape.339
  285.9 3.4 %all-to-all-start.4 = ((f32[8,6,1280]{2,1,0:T(8,128)}), f32[8,6,1280]{2,1,0:T(8,128)S(1)}, u32[]{:S(2)}, u32[]{:S(2)}) async-start(f32[8,6,1280]{2,1,0:T(8,128)} %reshape.339), calls=%async_computation.7 | async-start | bytes 655360 | tf_op jit(solution)/shard_map/all_to_all | solution.py:873
  290.0 6.9 %all-to-all-done.4 = f32[8,6,1280]{2,1,0:T(8,128)S(1)} async-done(((f32[8,6,1280]{2,1,0:T(8,128)}), f32[8,6,1280]{2,1,0:T(8,128)S(1)}, u32[]{:S(2)}, u32[]{:S(2)}) %all-to-all-start.4) | async-done | bytes 245792 | tf_op jit(solution)/shard_map/all_to_all | solution.py:873
  299.5 0.7 reshape_reshape.7
  (103 shorter events, 12.4 us)
Async XLA Ops:
  7.2 31.9 %copy-start = (bf16[1954,768]{1,0:T(8,128)(2,1)S(1)}, bf16[1954,768]{1,0:T(8,128)(2,1)}, u32[]{:S(2)}) copy-start(bf16[1954,768]{1,0:T(8,128)(2,1)} %param.18) | copy-start | bytes 9004036
  7.2 15.4 %copy-start.7 = (s32[1,256]{1,0:T(1,128)S(1)}, s32[1,256]{1,0:T(1,128)}, u32[]{:S(2)}) copy-start(s32[1,256]{1,0:T(1,128)} %param.15) | copy-start | bytes 3076
  7.2 16.0 %copy-start.10 = (bf16[6]{0:T(256)(128)(2,1)S(1)}, bf16[6]{0:T(256)(128)(2,1)}, u32[]{:S(2)}) copy-start(bf16[6]{0:T(256)(128)(2,1)} %param.22) | copy-start | bytes 40
  7.2 16.0 %copy-start.9 = (bf16[6]{0:T(256)(128)(2,1)S(1)}, bf16[6]{0:T(256)(128)(2,1)}, u32[]{:S(2)}) copy-start(bf16[6]{0:T(256)(128)(2,1)} %param.25) | copy-start | bytes 40
  7.2 16.0 %copy-start.8 = (bf16[6]{0:T(256)(128)(2,1)S(1)}, bf16[6]{0:T(256)(128)(2,1)}, u32[]{:S(2)}) copy-start(bf16[6]{0:T(256)(128)(2,1)} %param.28) | copy-start | bytes 40
  10.5 9.5 %all-to-all-start = ((bf16[8,6,1280]{2,1,0:T(8,128)(2,1)}), bf16[8,6,1280]{2,1,0:T(8,128)(2,1)S(1)}, u32[]{:S(2)}, u32[]{:S(2)}) async-start(bf16[8,6,1280]{2,1,0:T(8,128)(2,1)} %pad_maximum_fusion.1), calls=%async_computation | async-start | bytes 327680 | tf_op jit(solution)/shard_map/all_to_all | solution.py:746
  14.2 97.4 %all-gather.3.cloned.1.call-start = ((), (), s32[]{:S(2)}) async-start(), calls=%async_computation.11 | async-start | bytes 19021824 | tf_op jit(solution)/shard_map/all_gather | solution.py:752
  44.3 24.2 %all-to-all-start.2 = ((bf16[128,4,768]{2,1,0:T(4,128)(2,1)}), bf16[128,4,768]{2,1,0:T(4,128)(2,1)S(1)}, u32[]{:S(2)}, u32[]{:S(2)}) async-start(bf16[128,4,768]{2,1,0:T(4,128)(2,1)} %reshape.328), calls=%async_computation.2 | async-start | bytes 1572864 | tf_op jit(solution)/shard_map/all_to_all | solution.py:805
  52.7 163.1 %reduce-scatter.4.cloned.1.call-start = ((), (), s32[]{:S(2)}) async-start(), calls=%async_computation.8 | async-start | bytes 10616832 | tf_op jit(solution)/shard_map/reduce_scatter | solution.py:822
  170.8 9.8 %copy-start.11 = (bf16[256,1536]{1,0:T(8,128)(2,1)S(1)}, bf16[256,1536]{1,0:T(8,128)(2,1)}, u32[]{:S(2)}) copy-start(bf16[256,1536]{1,0:T(8,128)(2,1)} %get-tuple-element.66.kept_ref) | copy-start | bytes 2359300
  180.3 12.6 %collective-permute-start = (bf16[4,4,4,48,384]{4,3,2,1,0:T(8,128)(2,1)}, bf16[4,4,4,48,384]{4,3,2,1,0:T(8,128)(2,1)S(1)}, u32[]{:S(2)}, u32[]{:S(2)}) collective-permute-start(bf16[4,4,4,48,384]{4,3,2,1,0:T(8,128)(2,1)} %get-tuple-element.76), channel_id=1, source_target_pairs={{0,1},{1,0},{2,3},{3,2},{4,5},{5,4},{6,7},{7,6},{8,9},{9,8},{10,11... | collective-permute-start | bytes 7077896 | tf_op jit(solution)/shard_map/ppermute | solution.py:47
  180.6 15.8 %collective-permute-start.1 = (bf16[256,1536]{1,0:T(8,128)(2,1)S(1)}, bf16[256,1536]{1,0:T(8,128)(2,1)}, u32[]{:S(2)}, u32[]{:S(2)}) collective-permute-start(bf16[256,1536]{1,0:T(8,128)(2,1)S(1)} %copy-done.11), channel_id=1, source_target_pairs={{0,1},{1,0},{2,3},{3,2},{4,5},{5,4},{6,7},{7,6},{8,9},{9,8},{10,11... | collective-permute-start | bytes 2359304 | tf_op jit(solution)/shard_map/ppermute | solution.py:47
  180.8 12.0 %copy-start.2 = (bf16[4,4,4,48,384]{4,3,2,1,0:T(8,128)(2,1)S(1)}, bf16[4,4,4,48,384]{4,3,2,1,0:T(8,128)(2,1)}, u32[]{:S(2)}) copy-start(bf16[4,4,4,48,384]{4,3,2,1,0:T(8,128)(2,1)} %get-tuple-element.75) | copy-start | bytes 7077892
  192.6 2.7 copy-start.4
  192.6 3.8 %collective-permute-start.2 = (bf16[256,1536]{1,0:T(8,128)(2,1)}, bf16[256,1536]{1,0:T(8,128)(2,1)}, u32[]{:S(2)}, u32[]{:S(2)}) collective-permute-start(bf16[256,1536]{1,0:T(8,128)(2,1)} %get-tuple-element.80), channel_id=1, source_target_pairs={{0,1},{1,0},{2,3},{3,2},{4,5},{5,4},{6,7},{7,6},{8,9},{9,8},{10,11... | collective-permute-start | bytes 2359304 | tf_op jit(solution)/shard_map/ppermute | solution.py:47
  194.6 17.7 %collective-permute-start.3 = (bf16[2,4,4,48,384]{4,3,2,1,0:T(8,128)(2,1)}, bf16[2,4,4,48,384]{4,3,2,1,0:T(8,128)(2,1)}, u32[]{:S(2)}, u32[]{:S(2)}) collective-permute-start(bf16[2,4,4,48,384]{4,3,2,1,0:T(8,128)(2,1)} %get-tuple-element.97), channel_id=1, source_target_pairs={{0,12},{1,5},{4,8},{5,1},{8,4},{9,13},{12,0},{13,9},{2,14},{3,7},{... | collective-permute-start | bytes 3538952 | tf_op jit(solution)/shard_map/ppermute | solution.py:43
  201.7 26.3 %collective-permute-start.4 = (bf16[2,4,4,48,384]{4,3,2,1,0:T(8,128)(2,1)}, bf16[2,4,4,48,384]{4,3,2,1,0:T(8,128)(2,1)}, u32[]{:S(2)}, u32[]{:S(2)}) collective-permute-start(bf16[2,4,4,48,384]{4,3,2,1,0:T(8,128)(2,1)} %get-tuple-element.86), channel_id=1, source_target_pairs={{0,96},{1,33},{32,64},{33,1},{64,32},{65,97},{96,0},{97,65},{2,98}... | collective-permute-start | bytes 3538952 | tf_op jit(solution)/shard_map/ppermute | solution.py:43
  203.4 29.7 %all-to-all-start.3 = ((bf16[128,4,896]{2,1,0:T(4,128)(2,1)}), bf16[128,4,896]{2,1,0:T(4,128)(2,1)S(1)}, u32[]{:S(2)}, u32[]{:S(2)}) async-start(bf16[128,4,896]{2,1,0:T(4,128)(2,1)} %reshape.336), calls=%async_computation.4 | async-start | bytes 1835008 | tf_op jit(solution)/shard_map/all_to_all | solution.py:840
  212.2 43.2 %reduce-scatter.6.cloned.1.call-start = ((), (), s32[]{:S(2)}) async-start(), calls=%async_computation.9 | async-start | bytes 1474560 | tf_op jit(solution)/shard_map/reduce_scatter | solution.py:823
  214.3 16.5 %collective-permute-start.5 = (bf16[4,4,48,384]{3,2,1,0:T(8,128)(2,1)}, bf16[4,4,48,384]{3,2,1,0:T(8,128)(2,1)}, u32[]{:S(2)}, u32[]{:S(2)}) collective-permute-start(bf16[4,4,48,384]{3,2,1,0:T(8,128)(2,1)} %fusion.8), channel_id=1, source_target_pairs={{0,4},{1,13},{4,0},{5,9},{8,12},{9,5},{12,8},{13,1},{2,6},{3,15},{... | collective-permute-start | bytes 1769480 | tf_op jit(solution)/shard_map/ppermute | solution.py:43
  215.8 63.7 %reduce-scatter.8.cloned.1.call-start = ((), (), s32[]{:S(2)}) async-start(), calls=%async_computation.10 | async-start | bytes 368640 | tf_op jit(solution)/shard_map/reduce_scatter | solution.py:824
  215.9 12.1 %copy-start.3 = (bf16[2,4,4,48,384]{4,3,2,1,0:T(8,128)(2,1)S(1)}, bf16[2,4,4,48,384]{4,3,2,1,0:T(8,128)(2,1)}, u32[]{:S(2)}) copy-start(bf16[2,4,4,48,384]{4,3,2,1,0:T(8,128)(2,1)} %get-tuple-element.85) | copy-start | bytes 3538948
  230.0 10.2 %collective-permute-start.6 = (bf16[4,4,48,384]{3,2,1,0:T(8,128)(2,1)}, bf16[4,4,48,384]{3,2,1,0:T(8,128)(2,1)}, u32[]{:S(2)}, u32[]{:S(2)}) collective-permute-start(bf16[4,4,48,384]{3,2,1,0:T(8,128)(2,1)} %fusion.9), channel_id=1, source_target_pairs={{0,32},{1,97},{32,0},{33,65},{64,96},{65,33},{96,64},{97,1},{2,34}... | collective-permute-start | bytes 1769480 | tf_op jit(solution)/shard_map/ppermute | solution.py:43
  241.6 6.8 %collective-permute-start.8 = (bf16[2,4,48,384]{3,2,1,0:T(8,128)(2,1)S(1)}, bf16[2,4,48,384]{3,2,1,0:T(8,128)(2,1)S(1)}, u32[]{:S(2)}, u32[]{:S(2)}) collective-permute-start(bf16[2,4,48,384]{3,2,1,0:T(8,128)(2,1)S(1)} %get-tuple-element.98), channel_id=1, source_target_pairs={{0,12},{1,5},{4,8},{5,1},{8,4},{9,13},{12,0},{13,9},{2,14},{3,7},{... | collective-permute-start | bytes 884744 | tf_op jit(solution)/shard_map/ppermute | solution.py:43
  248.5 5.7 %collective-permute-start.9 = (bf16[4,48,384]{2,1,0:T(8,128)(2,1)S(1)}, bf16[4,48,384]{2,1,0:T(8,128)(2,1)S(1)}, u32[]{:S(2)}, u32[]{:S(2)}) collective-permute-start(bf16[4,48,384]{2,1,0:T(8,128)(2,1)S(1)} %fusion.19), channel_id=1, source_target_pairs={{0,4},{1,13},{4,0},{5,9},{8,12},{9,5},{12,8},{13,1},{2,6},{3,15},{... | collective-permute-start | bytes 442376 | tf_op jit(solution)/shard_map/ppermute | solution.py:43
  251.0 7.9 %collective-permute-start.7 = (bf16[2,4,48,384]{3,2,1,0:T(8,128)(2,1)S(1)}, bf16[2,4,48,384]{3,2,1,0:T(8,128)(2,1)S(1)}, u32[]{:S(2)}, u32[]{:S(2)}) collective-permute-start(bf16[2,4,48,384]{3,2,1,0:T(8,128)(2,1)S(1)} %get-tuple-element.101), channel_id=1, source_target_pairs={{0,18},{1,3},{2,16},{3,1},{16,2},{17,19},{18,0},{19,17},{4,22},{5,... | collective-permute-start | bytes 884744 | tf_op jit(solution)/shard_map/ppermute | solution.py:43
  254.8 24.7 %collective-permute-start.10 = (bf16[2,48,384]{2,1,0:T(8,128)(2,1)}, bf16[2,48,384]{2,1,0:T(8,128)(2,1)}, u32[]{:S(2)}, u32[]{:S(2)}) collective-permute-start(bf16[2,48,384]{2,1,0:T(8,128)(2,1)} %get-tuple-element.103), channel_id=1, source_target_pairs={{0,18},{1,3},{2,16},{3,1},{16,2},{17,19},{18,0},{19,17},{4,22},{5,... | collective-permute-start | bytes 221192 | tf_op jit(solution)/shard_map/ppermute | solution.py:43
  258.9 0.7 copy-start.5
  259.6 9.1 %collective-permute-start.12 = (bf16[4,48,384]{2,1,0:T(8,128)(2,1)S(1)}, bf16[4,48,384]{2,1,0:T(8,128)(2,1)}, u32[]{:S(2)}, u32[]{:S(2)}) collective-permute-start(bf16[4,48,384]{2,1,0:T(8,128)(2,1)S(1)} %fusion.18), channel_id=1, source_target_pairs={{0,2},{1,19},{2,0},{3,17},{16,18},{17,3},{18,16},{19,1},{4,6},{5,2... | collective-permute-start | bytes 442376 | tf_op jit(solution)/shard_map/ppermute | solution.py:43
  263.0 5.8 %copy-start.6 = (bf16[2,4,48,384]{3,2,1,0:T(8,128)(2,1)S(1)}, bf16[2,4,48,384]{3,2,1,0:T(8,128)(2,1)}, u32[]{:S(2)}) copy-start(bf16[2,4,48,384]{3,2,1,0:T(8,128)(2,1)} %copy-done.5) | copy-start | bytes 884740
  263.0 37.2 %copy-start.1 = (bf16[1954,768]{1,0:T(8,128)(2,1)S(1)}, bf16[1954,768]{1,0:T(8,128)(2,1)}, u32[]{:S(2)}) copy-start(bf16[1954,768]{1,0:T(8,128)(2,1)} %param.18) | copy-start | bytes 9004036
  269.8 5.6 %collective-permute-start.13 = (bf16[2,48,384]{2,1,0:T(8,128)(2,1)S(1)}, bf16[2,48,384]{2,1,0:T(8,128)(2,1)S(1)}, u32[]{:S(2)}, u32[]{:S(2)}) collective-permute-start(bf16[2,48,384]{2,1,0:T(8,128)(2,1)S(1)} %get-tuple-element.105), channel_id=1, source_target_pairs={{0,96},{1,33},{32,64},{33,1},{64,32},{65,97},{96,0},{97,65},{2,98}... | collective-permute-start | bytes 221192 | tf_op jit(solution)/shard_map/ppermute | solution.py:43
  275.4 4.0 %collective-permute-start.14 = (bf16[48,384]{1,0:T(8,128)(2,1)S(1)}, bf16[48,384]{1,0:T(8,128)(2,1)S(1)}, u32[]{:S(2)}, u32[]{:S(2)}) collective-permute-start(bf16[48,384]{1,0:T(8,128)(2,1)S(1)} %fusion.32), channel_id=1, source_target_pairs={{0,32},{1,97},{32,0},{33,65},{64,96},{65,33},{96,64},{97,1},{2,34}... | collective-permute-start | bytes 110600 | tf_op jit(solution)/shard_map/ppermute | solution.py:43
  280.3 4.0 %collective-permute-start.11 = (bf16[48,384]{1,0:T(8,128)(2,1)S(1)}, bf16[48,384]{1,0:T(8,128)(2,1)S(1)}, u32[]{:S(2)}, u32[]{:S(2)}) collective-permute-start(bf16[48,384]{1,0:T(8,128)(2,1)S(1)} %fusion.31), channel_id=1, source_target_pairs={{0,2},{1,19},{2,0},{3,17},{16,18},{17,3},{18,16},{19,1},{4,6},{5,2... | collective-permute-start | bytes 110600 | tf_op jit(solution)/shard_map/ppermute | solution.py:43
  285.9 11.0 %all-to-all-start.4 = ((f32[8,6,1280]{2,1,0:T(8,128)}), f32[8,6,1280]{2,1,0:T(8,128)S(1)}, u32[]{:S(2)}, u32[]{:S(2)}) async-start(f32[8,6,1280]{2,1,0:T(8,128)} %reshape.339), calls=%async_computation.7 | async-start | bytes 655360 | tf_op jit(solution)/shard_map/all_to_all | solution.py:873
Sparse Core Ops, SparseCore 0:
  20.9 90.5 all-gather.2
  154.3 60.7 reduce-scatter.3
  217.6 26.7 reduce-scatter.5
  255.5 19.2 reduce-scatter.7
